TPU v7x, 256 devices: a whole 4x4x8 slice. The times are simulated.
256 devices in a mesh: dp: 64 (over z_lo, y, x), mp: 4 (over z_hi, core).
Axes of the slice: x: 4, y: 4, z: 8 (z_hi: 2, z_lo: 4; z = z_hi * 4 + z_lo), core: 2. Of those that a mesh axis runs over, the one named last changes fastest.
Arguments:
- tokens: bfloat16 [16384, 8192], P('dp', 'mp'), may hold values from -8 to 8
- attn_gain: bfloat16 [8192], replicated, may hold values from 0.5 to 1.5
- w_query: bfloat16 [8192, 4096], P('dp', 'mp'), may hold values from -2 to 2
- key_projection_weight: bfloat16 [8192, 512], P('dp', 'mp'), may hold values from -2 to 2
- value_projection_weight: bfloat16 [8192, 512], P('dp', 'mp'), may hold values from -0.0625 to 0.0625
- w_out: bfloat16 [4096, 8192], P('mp', 'dp'), may hold values from -0.09375 to 0.09375
- final_gain: bfloat16 [8192], P('mp'), may hold values from 0.5 to 1.5
- unembed: bfloat16 [64128, 8192], P('dp', 'mp'), may hold values from -0.29882812 to 0.29882812
- clean_ids: int32 [64], replicated, may hold values from 0 to 64127, as said below
- corrupt_ids: int32 [64], replicated, may hold values from 0 to 64127
Outputs:
- head_out: bfloat16 [16384, 4096], P('dp', 'mp')
- scores: float32 [64, 32], P('dp', 'mp')
- metric: float32 [64], P('dp')
Inputs may be any that keep to these rules, and one draw needn't show every extreme that they name: `clean_ids`: split the ids into 64 aligned blocks of equal size and number the groups of 1 sequence alike; the block of a clean answer, minus the number of its sequence's group, taken modulo the number of blocks, is drawn so that every such offset occurs for some sequence.
All inputs are finite; a program needn't handle non-finite values.
Results may differ from a plain program's by a relative error of at most 0.015.
Values may be sent and summed in bfloat16 or wider, within the bound.
No kernel may reach another device: no remote copies, remote signals or barrier semaphores. Data moves between devices by JAX's collectives and lax.ppermute only.
A program may use at most 128 MiB of HBM per device.

v0:
```python
import functools
import math

import jax
import jax.numpy as jnp
from jax import lax
from jax.experimental import pallas as pl
from jax.experimental.pallas import tpu as pltpu
from jax.sharding import Mesh, PartitionSpec as P

MODEL_WIDTH = 8192
HEAD_SIZE = 128
LENGTH = 256
TOKENS = 16384
DP = ("zl", "y", "x")
MP = ("zh", "c")
F32 = jnp.float32
BF16 = jnp.bfloat16


def from_everyone(value, axis):
    count = lax.axis_size(axis)
    return lax.all_to_all(
        jnp.broadcast_to(value[None], (count, *value.shape)), axis, 0, 0, tiled=True
    )


def send(value, route):
    pairs = []
    for z in range(4):
        for c in range(2):
            to = route(z, c)
            pairs.append((z * 2 + c, (to[0] % 4) * 2 + to[1]))
    return lax.ppermute(value, ("zl", "c"), pairs)


def along(value, step):
    place = lambda z: (z % 4) * 2 + z // 4
    pairs = [(place(z), place((z + step) % 8)) for z in range(8)]
    return lax.ppermute(value, ("zl", "zh"), pairs)


def to_column_owners(value, zl, m):
    got = []
    for i in range(4):
        pairs = [(a * 4 + b, b * 4 + (a + i) % 4) for a in range(4) for b in range(4)]
        got.append(lax.ppermute(value, ("zl", *MP), pairs))
    got = jnp.stack(got)
    return jnp.stack([lax.dynamic_index_in_dim(got, (m - a) % 4, 0, keepdims=False) for a in range(4)])


def sum_over_mp(value):
    others = [
        lax.ppermute(value, MP, [(i, i ^ step) for i in range(4)]).astype(F32) for step in (1, 2, 3)
    ]
    return value.astype(F32) + others[0] + (others[1] + others[2])


def swap_cores(value):
    return lax.ppermute(value, "c", [(0, 1), (1, 0)])


def rotary_tables():
    half = HEAD_SIZE // 2
    positions = jnp.arange(LENGTH, dtype=F32)
    inv_freq = jnp.exp(
        jnp.arange(half, dtype=F32) * (-2.0 * math.log(500000.0) / HEAD_SIZE)
    )
    angles = positions[:, None] * inv_freq[None, :]
    cos, sin = jnp.cos(angles), jnp.sin(angles)
    return jnp.concatenate([cos, cos], axis=1), jnp.concatenate([-sin, sin], axis=1)


def attention_kernel(heads, kept, came, squares, cos_ref, sin_ref, out, total):
    scale = lax.rsqrt(squares[...] * (1.0 / MODEL_WIDTH) + 1e-05)
    cos, sin = cos_ref[...], sin_ref[...]

    def column(i):
        at = slice(i * HEAD_SIZE, (i + 1) * HEAD_SIZE)
        return (kept[:, at] + came[:, at]) * scale

    def rotated(i):
        t = column(i)
        return (t * cos + pltpu.roll(t, HEAD_SIZE // 2, 1) * sin).astype(BF16)

    key, value = rotated(heads), column(heads + 1).astype(BF16)
    row = lax.broadcasted_iota(jnp.int32, (LENGTH, LENGTH), 0)
    causal = row >= lax.broadcasted_iota(jnp.int32, (LENGTH, LENGTH), 1)
    for h in range(heads):
        logits = lax.dot_general(
            rotated(h), key, (((1,), (1,)), ((), ())), preferred_element_type=F32
        )
        logits = jnp.where(causal, logits * (1.0 / math.sqrt(HEAD_SIZE)), -1e30)
        e = jnp.exp(logits - jnp.max(logits, axis=1, keepdims=True))
        probs = (e / jnp.sum(e, axis=1, keepdims=True)).astype(BF16)
        mixed = jnp.dot(probs, value, preferred_element_type=F32).astype(BF16)
        at = slice(h * HEAD_SIZE, (h + 1) * HEAD_SIZE)
        out[:, at] = mixed
        total[:, at] = jnp.sum(mixed.astype(F32), axis=0, keepdims=True)


def attention(heads, kept, came, squares, tables):
    return pl.pallas_call(
        functools.partial(attention_kernel, heads),
        out_shape=(
            jax.ShapeDtypeStruct((LENGTH, heads * HEAD_SIZE), BF16),
            jax.ShapeDtypeStruct((1, heads * HEAD_SIZE), F32),
        ),
        compiler_params=pltpu.CompilerParams(vmem_limit_bytes=24 * 1024 * 1024),
        cost_estimate=pl.CostEstimate(
            flops=4 * heads * LENGTH * LENGTH * HEAD_SIZE,
            bytes_accessed=2 * 4 * LENGTH * 768,
            transcendentals=heads * LENGTH * LENGTH,
        ),
    )(kept, came, squares, *tables)


def ring_share(block):
    got = {0: block}
    for r in (1, 2, 3):
        for sign in (1, -1):
            got[-sign * r] = along(got[-sign * (r - 1)], sign)
    cut = block.shape[0] // 2
    got[4] = (along(got[-3][:cut], 1), along(got[3][cut:], -1))
    return got


def per_device(tokens, gain, w_query, w_key, w_value, w_out, final_gain, unembed, clean, corrupt):
    zh, zl, core = lax.axis_index("zh"), lax.axis_index("zl"), lax.axis_index("c")
    yx = lax.axis_index(("y", "x"))
    first = core == 0

    def back(cols):
        return lax.dot_general(
            cols.astype(BF16), w_out, (((1,), (1,)), ((), ())), preferred_element_type=F32
        )

    even = zl % 2 == 0
    width = w_query.shape[1] // 2

    with jax.named_scope("tokens"):
        blocks = ring_share(tokens)

    with jax.named_scope("weights"):
        wkv = jnp.concatenate([w_key, w_value], axis=1)
        upper = zl // 2
        pieces = [
            jnp.concatenate(
                [lax.dynamic_slice_in_dim(w_query, h * width, width, 1), wkv], axis=1
            )
            for h in (upper, 1 - upper)
        ]
        pa = send(pieces[0], lambda z, c: (2 * c + z // 2, z % 2))
        pb = send(pieces[1], lambda z, c: (2 * c + 1 - z // 2, z % 2))
        rows = jnp.concatenate([jnp.where(even, pa, pb), jnp.where(even, pb, pa)], axis=1)

    with jax.named_scope("direction"):
        vocab_rows = unembed.shape[0]
        ids = lax.axis_index(DP) * vocab_rows + jnp.arange(vocab_rows, dtype=jnp.int32)
        one_hot = (clean[:, None] == ids[None, :]).astype(F32) - (
            corrupt[:, None] == ids[None, :]
        ).astype(F32)
        found = jnp.dot(one_hot.astype(BF16), unembed, preferred_element_type=F32)
        found = found.reshape(4, 16, 16, 128).swapaxes(1, 2).astype(BF16)
        here = (jnp.arange(4) == zl)[:, None, None, None]
        own_last = jnp.where(here, tokens[LENGTH - 1].reshape(1, 16, 1, 128), 0).astype(BF16)
        packed = jnp.concatenate([found, own_last], axis=2).reshape(64, 17, 128)
        packed = lax.all_to_all(packed, DP, 0, 0, tiled=True)
        rows, packed, *_ = lax.optimization_barrier((rows, packed, blocks[1], blocks[-1]))
        weights = lax.all_gather(rows, ("y", "x"), axis=0, tiled=True)
        packed = packed.astype(F32)
        packed = jnp.sum(packed.reshape(4, 16, 17, 128), axis=0)
        gain_cols = lax.dynamic_slice_in_dim(final_gain, yx * 128, 128, 0).astype(F32)
        weighted = gain_cols * jnp.sum(packed[:, :16], axis=0)
        both = jnp.stack([weighted, packed[:, 16]])
        both = to_column_owners(both, zl, 2 * zh + core)
        weighted_cols = both[:, 0].reshape(64, 128)
        token_cols = both[:, 1].reshape(64, 128)
        back_w = back(weighted_cols)

    depth = tokens.shape[1]
    columns = width + 2 * HEAD_SIZE
    heads = width // HEAD_SIZE
    tables = rotary_tables()

    def scaled(k, parts):
        side = ((zh * 4 + zl + k) % 8) // 4
        g = lax.dynamic_slice_in_dim(gain, (2 * side + core) * depth, depth, 0).astype(F32)
        t = parts.astype(F32)
        done = ((t * g).astype(BF16), jnp.sum(t * t, axis=1, keepdims=True))
        return (side, *lax.optimization_barrier(done))

    def project(side, block, square):
        weight = lax.dynamic_slice_in_dim(weights, side * columns, columns, 1)
        return jnp.dot(block, weight, preferred_element_type=F32), square

    def both_sides(near, far):
        return tuple(a + b for a, b in zip(near, far))

    def attend(low, high):
        kept = [jnp.where(first, a, b) for a, b in zip(low, high)]
        came = [swap_cores(jnp.where(first, b, a)) for a, b in zip(low, high)]
        return attention(heads, kept[0], came[0], kept[1] + came[1], tables)

    with jax.named_scope("project"):
        known = {k: scaled(k, parts) for k, parts in blocks.items() if k != 4}
        near = project(*known[0])
        next_1, next_2, next_3 = [
            both_sides(project(*known[a]), project(*known[b])) for a, b in ((1, -3), (2, -2), (-1, 3))
        ]
        mixed_1, total_1 = attend(next_1, next_3)
        last_block, near, next_2, mixed_1, back_w, token_cols = lax.optimization_barrier(
            (blocks[4], near, next_2, mixed_1, back_w, token_cols)
        )
        last_block = project(*scaled(4, jnp.concatenate(last_block, axis=0)))
        mixed_0, total_0 = attend(both_sides(near, last_block), next_2)

    with jax.named_scope("return_heads"):

        def owned(slot_0, slot_1):
            oa = send(slot_0, lambda z, c: (z, z // 2) if c == 0 else (z + 2, z // 2))
            ob = send(slot_1, lambda z, c: (z + 1, z // 2) if c == 0 else (z - 1, z // 2))
            return jnp.concatenate(
                [jnp.where(even, oa, ob), jnp.where(even, ob, oa)], axis=1
            )

        def summary(mixed, total):
            high = lax.reduce_precision(total, 8, 7)
            return jnp.concatenate(
                [mixed[-1:], high.astype(BF16), (total - high).astype(BF16)], axis=0
            )

        own = owned(summary(mixed_0, total_0), summary(mixed_1, total_1))
        own, mixed_0, mixed_1 = lax.optimization_barrier((own, mixed_0, mixed_1))
        head_out = owned(mixed_0, mixed_1)

    with jax.named_scope("tail"):
        every = from_everyone(own, DP)
        last = every[:, 0]
        part = jnp.dot(last, w_out, preferred_element_type=F32).astype(BF16)
        attn_last = sum_over_mp(part).astype(BF16)
        head_mean = jnp.sum(every[:, 1:].astype(F32), axis=(0, 1)) / TOKENS
        gap = head_mean[None] - last.astype(F32)

        def per_head(grads):
            return jnp.sum((gap * grads).reshape(64, 8, HEAD_SIZE), axis=2)

        residual = token_cols + attn_last.astype(F32)
        square = jnp.sum(residual * residual, axis=1, keepdims=True)
        product = jnp.sum(residual * weighted_cols, axis=1, keepdims=True)
        packed = jnp.concatenate(
            [
                per_head(back_w),
                per_head(back(residual)),
                jnp.broadcast_to(square, (64, 56)),
                jnp.broadcast_to(product, (64, 56)),
            ],
            axis=1,
        )
        mine = jnp.sum(lax.all_to_all(packed[:, None], DP, 0, 0, tiled=True), axis=0)
        inverse = lax.rsqrt(mine[:, 16] / MODEL_WIDTH + 1e-05)
        metric = inverse * mine[:, 72]
        scores = inverse * mine[:, :8] - (metric * inverse * inverse / MODEL_WIDTH) * mine[:, 8:16]
    return head_out, scores, metric


def solution(mesh):
    fine = Mesh(mesh.devices.reshape(4, 4, 4, 2, 2), (*DP, *MP))
    in_specs = (
        P(DP, MP),
        P(),
        P(DP, MP),
        P(DP, MP),
        P(DP, MP),
        P(MP, DP),
        P(MP),
        P(DP, MP),
        P(),
        P(),
    )
    out_specs = (P(DP, MP), P(DP, MP), P(DP))
    return jax.shard_map(
        per_device, mesh=fine, in_specs=in_specs, out_specs=out_specs, check_vma=False
    )
```

profile of v0, /device:TPU:1, one launch (start us, length us, event | category | flops | bytes accessed | tf_op | source)
XLA Modules:
  0.0 239.3 jit_solution(5431426067089946569)
XLA Ops:
  7.2 6.5 %collective-permute-start.4 = (bf16[256,2048]{1,0:T(8,128)(2,1)}, bf16[256,2048]{1,0:T(8,128)(2,1)}, u32[]{:S(2)}, u32[]{:S(2)}) collective-permute-start(bf16[256,2048]{1,0:T(8,128)(2,1)} %param.10), channel_id=1, source_target_pairs={{0,194},{64,0},{128,64},{192,128},{2,192},{66,2},{130,66},{194,130... | collective-permute-start | bytes 3145736 | tf_op jit(solution)/shard_map/tokens/ppermute | solution.py:40
  18.1 2.6 %collective-permute-start.9 = (bf16[128,768]{1,0:T(8,128)(2,1)S(1)}, bf16[128,768]{1,0:T(8,128)(2,1)}, u32[]{:S(2)}, u32[]{:S(2)}) collective-permute-start(bf16[128,768]{1,0:T(8,128)(2,1)S(1)} %get-tuple-element.107), channel_id=1, source_target_pairs={{0,64},{1,192},{64,65},{65,193},{128,0},{129,128},{192,1},{193,129... | collective-permute-start | bytes 589832 | tf_op jit(solution)/shard_map/weights/ppermute | solution.py:34
  20.7 3.1 %fusion.41 = bf16[8,8,16,128]{3,1,2,0:T(8,128)(2,1)S(1)} fusion(bf16[1002,2048]{1,0:T(8,128)(2,1)} %param.17, s32[1002]{0:T(1024)S(1)} %iota_add_fusion, s32[64]{0:T(128)} %param.19, s32[64]{0:T(128)} %param.18), kind=kOutput, calls=%fused_computation.52 | convolution fusion | flops 263184128 | bytes 4370856 | tf_op jit(solution)/shard_map/direction/dot_general | solution.py:163
  25.1 8.8 %all-to-all-start = ((bf16[64,17,128]{2,1,0:T(8,128)(2,1)}), bf16[64,17,128]{2,1,0:T(8,128)(2,1)S(1)}, u32[]{:S(2)}, u32[]{:S(2)}) async-start(bf16[64,17,128]{2,1,0:T(8,128)(2,1)} %pad_maximum_fusion.3), calls=%async_computation | async-start | bytes 786432 | tf_op jit(solution)/shard_map/direction/all_to_all | solution.py:168
  34.0 6.1 %collective-permute-done.8 = bf16[128,768]{1,0:T(8,128)(2,1)S(1)} collective-permute-done((bf16[128,768]{1,0:T(8,128)(2,1)}, bf16[128,768]{1,0:T(8,128)(2,1)S(1)}, u32[]{:S(2)}, u32[]{:S(2)}) %collective-permute-start.8) | collective-permute-done | bytes 196640 | tf_op jit(solution)/shard_map/weights/ppermute | solution.py:34
  40.1 5.5 %collective-permute-done.9 = bf16[128,768]{1,0:T(8,128)(2,1)} collective-permute-done((bf16[128,768]{1,0:T(8,128)(2,1)S(1)}, bf16[128,768]{1,0:T(8,128)(2,1)}, u32[]{:S(2)}, u32[]{:S(2)}) %collective-permute-start.9) | collective-permute-done | bytes 196640 | tf_op jit(solution)/shard_map/weights/ppermute | solution.py:34
  47.3 6.2 %all-to-all-done = bf16[64,17,128]{2,1,0:T(8,128)(2,1)S(1)} async-done(((bf16[64,17,128]{2,1,0:T(8,128)(2,1)}), bf16[64,17,128]{2,1,0:T(8,128)(2,1)S(1)}, u32[]{:S(2)}, u32[]{:S(2)}) %all-to-all-start) | async-done | bytes 278560 | tf_op jit(solution)/shard_map/direction/all_to_all | solution.py:168
  56.7 8.0 %collective-permute-start.5 = (bf16[256,2048]{1,0:T(8,128)(2,1)}, bf16[256,2048]{1,0:T(8,128)(2,1)}, u32[]{:S(2)}, u32[]{:S(2)}) collective-permute-start(bf16[256,2048]{1,0:T(8,128)(2,1)} %collective-permute-done.4), channel_id=1, source_target_pairs={{0,194},{64,0},{128,64},{192,128},{2,192},{66,2},{130,66},{194,130... | collective-permute-start | bytes 3145736 | tf_op jit(solution)/shard_map/tokens/ppermute | solution.py:40
  66.8 3.6 %collective-permute-start.13 = (f32[2,16,128]{2,1,0:T(8,128)S(1)}, f32[2,16,128]{2,1,0:T(8,128)S(1)}, u32[]{:S(2)}, u32[]{:S(2)}) collective-permute-start(f32[2,16,128]{2,1,0:T(8,128)S(1)} %pad_maximum_fusion.13), channel_id=1, source_target_pairs={{0,1},{1,65},{2,129},{3,193},{64,2},{65,66},{66,130},{67,194},{128... | collective-permute-start | bytes 49160 | tf_op jit(solution)/shard_map/direction/ppermute | solution.py:47
  70.3 2.6 %fusion.23 = (f32[256]{0:T(256)S(1)}, bf16[256,2048]{1,0:T(8,128)(2,1)}) fusion(bf16[256,2048]{1,0:T(8,128)(2,1)} %collective-permute-done.4, f32[2048]{0:T(1024)S(1)} %get-tuple-element.111), kind=kLoop, calls=%fused_computation.40 | loop fusion | flops 2621184 | bytes 2106368 | tf_op jit(solution)/shard_map/project/reduce_sum | solution.py:190
  72.9 13.7 %collective-permute-done.15 = f32[2,16,128]{2,1,0:T(8,128)S(1)} collective-permute-done((f32[2,16,128]{2,1,0:T(8,128)S(1)}, f32[2,16,128]{2,1,0:T(8,128)S(1)}, u32[]{:S(2)}, u32[]{:S(2)}) %collective-permute-start.15) | collective-permute-done | bytes 16416 | tf_op jit(solution)/shard_map/direction/ppermute | solution.py:47
  86.6 1.9 collective-permute-start.12
  94.3 2.6 %fusion.19 = (f32[256]{0:T(256)S(1)}, bf16[256,2048]{1,0:T(8,128)(2,1)}) fusion(bf16[256,2048]{1,0:T(8,128)(2,1)} %collective-permute-done.5, f32[2048]{0:T(1024)S(1)} %get-tuple-element.113), kind=kLoop, calls=%fused_computation.36 | loop fusion | flops 2621184 | bytes 2106368 | tf_op jit(solution)/shard_map/project/reduce_sum | solution.py:190
  96.9 19.6 %collective-permute-done.6 = bf16[256,2048]{1,0:T(8,128)(2,1)S(1)} collective-permute-done((bf16[256,2048]{1,0:T(8,128)(2,1)}, bf16[256,2048]{1,0:T(8,128)(2,1)S(1)}, u32[]{:S(2)}, u32[]{:S(2)}) %collective-permute-start.6) | collective-permute-done | bytes 1048608 | tf_op jit(solution)/shard_map/tokens/ppermute | solution.py:40
  117.0 2.5 %fusion.25 = (f32[256]{0:T(256)S(1)}, bf16[256,2048]{1,0:T(8,128)(2,1)}) fusion(bf16[256,2048]{1,0:T(8,128)(2,1)} %collective-permute-done.2, f32[2048]{0:T(1024)S(1)} %get-tuple-element.110), kind=kLoop, calls=%fused_computation.42 | loop fusion | flops 2621184 | bytes 2106368 | tf_op jit(solution)/shard_map/project/reduce_sum | solution.py:190
  120.4 2.1 collective-permute-start.11
  122.5 2.5 %fusion.21 = (f32[256]{0:T(256)S(1)}, bf16[256,2048]{1,0:T(8,128)(2,1)}) fusion(bf16[256,2048]{1,0:T(8,128)(2,1)} %collective-permute-done.1, f32[2048]{0:T(1024)S(1)} %get-tuple-element.112), kind=kLoop, calls=%fused_computation.38 | loop fusion | flops 2621184 | bytes 2106368 | tf_op jit(solution)/shard_map/project/reduce_sum | solution.py:190
  128.4 3.9 %collective-permute-start.7 = (bf16[128,2048]{1,0:T(8,128)(2,1)}, bf16[128,2048]{1,0:T(8,128)(2,1)}, u32[]{:S(2)}, u32[]{:S(2)}) collective-permute-start(bf16[128,2048]{1,0:T(8,128)(2,1)} %slice.61), channel_id=1, source_target_pairs={{0,194},{64,0},{128,64},{192,128},{2,192},{66,2},{130,66},{194,130... | collective-permute-start | bytes 1572872 | tf_op jit(solution)/shard_map/tokens/ppermute | solution.py:40
  135.2 3.3 %fusion.8 = f32[256,768]{1,0:T(8,128)S(1)} fusion(bf16[256,2048]{1,0:T(8,128)(2,1)} %get-tuple-element.44, bf16[2048,1536]{1,0:T(8,128)(2,1)} %all-gather.2.cloned.1.call-done, s32[]{:T(128)S(6)} %select_n.268), kind=kOutput, calls=%fused_computation.8 | convolution fusion | flops 805306368 | bytes 4980740 | tf_op jit(solution)/shard_map/project/dot_general | solution.py:195
  138.6 3.3 %fusion.4 = f32[256,768]{1,0:T(8,128)S(1)} fusion(bf16[256,2048]{1,0:T(8,128)(2,1)} %get-tuple-element.46, bf16[2048,1536]{1,0:T(8,128)(2,1)} %all-gather.2.cloned.1.call-done, s32[]{:T(128)S(6)} %select_n.276), kind=kOutput, calls=%fused_computation.4 | convolution fusion | flops 805306368 | bytes 4980740 | tf_op jit(solution)/shard_map/project/dot_general | solution.py:195
  153.0 3.0 %fusion = f32[256,768]{1,0:T(8,128)S(1)} fusion(bf16[256,2048]{1,0:T(8,128)(2,1)S(1)} %get-tuple-element.57, bf16[2048,1536]{1,0:T(8,128)(2,1)} %all-gather.2.cloned.1.call-done, s32[]{:T(128)S(6)} %select_n.298), kind=kOutput, calls=%fused_computation | convolution fusion | flops 805306368 | bytes 4980740 | tf_op jit(solution)/shard_map/project/dot_general | solution.py:195
  156.9 5.5 %collective-permute-start.19 = (bf16[3,512]{1,0:T(4,128)(2,1)S(1)}, bf16[3,512]{1,0:T(4,128)(2,1)S(1)}, u32[]{:S(2)}, u32[]{:S(2)}) collective-permute-start(bf16[3,512]{1,0:T(4,128)(2,1)S(1)} %pad_maximum_fusion.16), channel_id=1, source_target_pairs={{0,64},{1,192},{64,128},{65,0},{128,193},{129,65},{192,1},{193,129... | collective-permute-start | bytes 9224 | tf_op jit(solution)/shard_map/return_heads/ppermute | solution.py:34
  163.9 2.6 %collective-permute-start.18 = (bf16[3,512]{1,0:T(4,128)(2,1)S(1)}, bf16[3,512]{1,0:T(4,128)(2,1)S(1)}, u32[]{:S(2)}, u32[]{:S(2)}) collective-permute-start(bf16[3,512]{1,0:T(4,128)(2,1)S(1)} %pad_maximum_fusion.15), channel_id=1, source_target_pairs={{0,0},{1,128},{64,64},{65,192},{128,129},{129,1},{192,193},{193,65... | collective-permute-start | bytes 9224 | tf_op jit(solution)/shard_map/return_heads/ppermute | solution.py:34
  166.4 2.7 %collective-permute-done.18 = bf16[3,512]{1,0:T(4,128)(2,1)S(1)} collective-permute-done((bf16[3,512]{1,0:T(4,128)(2,1)S(1)}, bf16[3,512]{1,0:T(4,128)(2,1)S(1)}, u32[]{:S(2)}, u32[]{:S(2)}) %collective-permute-start.18) | collective-permute-done | bytes 3104 | tf_op jit(solution)/shard_map/return_heads/ppermute | solution.py:34
  170.1 4.6 %all-to-all-start.1 = ((bf16[64,3,1024]{2,1,0:T(4,128)(2,1)}), bf16[64,3,1024]{2,1,0:T(4,128)(2,1)S(1)}, u32[]{:S(2)}, u32[]{:S(2)}) async-start(bf16[64,3,1024]{2,1,0:T(4,128)(2,1)} %broadcast_in_dim.107), calls=%async_computation.1 | async-start | bytes 1048576 | tf_op jit(solution)/shard_map/tail/all_to_all | solution.py:23
  174.7 5.4 %collective-permute-start.20 = (bf16[256,512]{1,0:T(8,128)(2,1)S(1)}, bf16[256,512]{1,0:T(8,128)(2,1)S(1)}, u32[]{:S(2)}, u32[]{:S(2)}) collective-permute-start(bf16[256,512]{1,0:T(8,128)(2,1)S(1)} %get-tuple-element.66), channel_id=1, source_target_pairs={{0,0},{1,128},{64,64},{65,192},{128,129},{129,1},{192,193},{193,65... | collective-permute-start | bytes 786440 | tf_op jit(solution)/shard_map/return_heads/ppermute | solution.py:34
  181.3 16.2 %collective-permute-done.20 = bf16[256,512]{1,0:T(8,128)(2,1)S(1)} collective-permute-done((bf16[256,512]{1,0:T(8,128)(2,1)S(1)}, bf16[256,512]{1,0:T(8,128)(2,1)S(1)}, u32[]{:S(2)}, u32[]{:S(2)}) %collective-permute-start.20) | collective-permute-done | bytes 262176 | tf_op jit(solution)/shard_map/return_heads/ppermute | solution.py:34
  197.9 5.9 %collective-permute-start.24 = (bf16[64,128]{1,0:T(8,128)(2,1)S(1)}, bf16[64,128]{1,0:T(8,128)(2,1)S(1)}, u32[]{:S(2)}, u32[]{:S(2)}) collective-permute-start(bf16[64,128]{1,0:T(8,128)(2,1)S(1)} %convolution_convert_fusion.1), channel_id=1, source_target_pairs={{0,3},{1,2},{2,1},{3,0},{4,7},{5,6},{6,5},{7,4},{8,11},{9,10},{10,... | collective-permute-start | bytes 49160 | tf_op jit(solution)/shard_map/tail/ppermute | solution.py:54
  203.8 2.3 collective-permute-start.23
  206.7 3.6 %collective-permute-done.23 = bf16[64,128]{1,0:T(8,128)(2,1)S(1)} collective-permute-done((bf16[64,128]{1,0:T(8,128)(2,1)S(1)}, bf16[64,128]{1,0:T(8,128)(2,1)S(1)}, u32[]{:S(2)}, u32[]{:S(2)}) %collective-permute-start.23) | collective-permute-done | bytes 16416 | tf_op jit(solution)/shard_map/tail/ppermute | solution.py:54
  211.7 8.0 %all-to-all-start.2 = ((f32[64,1,128]{2,1,0:T(1,128)}), f32[64,1,128]{2,1,0:T(1,128)S(1)}, u32[]{:S(2)}, u32[]{:S(2)}) async-start(f32[64,1,128]{2,1,0:T(1,128)} %bitcast.21), calls=%async_computation.2 | async-start | bytes 65536 | tf_op jit(solution)/shard_map/tail/all_to_all | solution.py:260
  220.6 8.1 %all-to-all-done.2 = f32[64,1,128]{2,1,0:T(1,128)S(1)} async-done(((f32[64,1,128]{2,1,0:T(1,128)}), f32[64,1,128]{2,1,0:T(1,128)S(1)}, u32[]{:S(2)}, u32[]{:S(2)}) %all-to-all-start.2) | async-done | bytes 32800 | tf_op jit(solution)/shard_map/tail/all_to_all | solution.py:260
  (146 shorter events, 45.5 us)
Async XLA Ops:
  7.2 86.9 %copy-start = (bf16[1024,128]{1,0:T(8,128)(2,1)S(1)}, bf16[1024,128]{1,0:T(8,128)(2,1)}, u32[]{:S(2)}) copy-start(bf16[1024,128]{1,0:T(8,128)(2,1)} %param.15) | copy-start | bytes 786436
  7.2 46.3 %collective-permute-start.4 = (bf16[256,2048]{1,0:T(8,128)(2,1)}, bf16[256,2048]{1,0:T(8,128)(2,1)}, u32[]{:S(2)}, u32[]{:S(2)}) collective-permute-start(bf16[256,2048]{1,0:T(8,128)(2,1)} %param.10), channel_id=1, source_target_pairs={{0,194},{64,0},{128,64},{192,128},{2,192},{66,2},{130,66},{194,130... | collective-permute-start | bytes 3145736 | tf_op jit(solution)/shard_map/tokens/ppermute | solution.py:40
  13.7 39.8 %collective-permute-start = (bf16[256,2048]{1,0:T(8,128)(2,1)}, bf16[256,2048]{1,0:T(8,128)(2,1)S(1)}, u32[]{:S(2)}, u32[]{:S(2)}) collective-permute-start(bf16[256,2048]{1,0:T(8,128)(2,1)} %param.10), channel_id=1, source_target_pairs={{0,64},{64,128},{128,192},{192,2},{2,66},{66,130},{130,194},{194,0... | collective-permute-start | bytes 3145736 | tf_op jit(solution)/shard_map/tokens/ppermute | solution.py:40
  16.1 23.9 %collective-permute-start.8 = (bf16[128,768]{1,0:T(8,128)(2,1)}, bf16[128,768]{1,0:T(8,128)(2,1)S(1)}, u32[]{:S(2)}, u32[]{:S(2)}) collective-permute-start(bf16[128,768]{1,0:T(8,128)(2,1)} %get-tuple-element.106), channel_id=1, source_target_pairs={{0,0},{1,128},{64,1},{65,129},{128,64},{129,192},{192,65},{193,193... | collective-permute-start | bytes 589832 | tf_op jit(solution)/shard_map/weights/ppermute | solution.py:34
  18.1 27.5 %collective-permute-start.9 = (bf16[128,768]{1,0:T(8,128)(2,1)S(1)}, bf16[128,768]{1,0:T(8,128)(2,1)}, u32[]{:S(2)}, u32[]{:S(2)}) collective-permute-start(bf16[128,768]{1,0:T(8,128)(2,1)S(1)} %get-tuple-element.107), channel_id=1, source_target_pairs={{0,64},{1,192},{64,65},{65,193},{128,0},{129,128},{192,1},{193,129... | collective-permute-start | bytes 589832 | tf_op jit(solution)/shard_map/weights/ppermute | solution.py:34
  25.1 28.4 %all-to-all-start = ((bf16[64,17,128]{2,1,0:T(8,128)(2,1)}), bf16[64,17,128]{2,1,0:T(8,128)(2,1)S(1)}, u32[]{:S(2)}, u32[]{:S(2)}) async-start(bf16[64,17,128]{2,1,0:T(8,128)(2,1)} %pad_maximum_fusion.3), calls=%async_computation | async-start | bytes 786432 | tf_op jit(solution)/shard_map/direction/all_to_all | solution.py:168
  33.9 101.3 %all-gather.2.cloned.1.call-start = ((), (), s32[]{:S(2)}) async-start(), calls=%async_computation.3 | async-start | bytes 6684672 | tf_op jit(solution)/shard_map/direction/all_gather | solution.py:170
  56.7 35.0 %collective-permute-start.5 = (bf16[256,2048]{1,0:T(8,128)(2,1)}, bf16[256,2048]{1,0:T(8,128)(2,1)}, u32[]{:S(2)}, u32[]{:S(2)}) collective-permute-start(bf16[256,2048]{1,0:T(8,128)(2,1)} %collective-permute-done.4), channel_id=1, source_target_pairs={{0,194},{64,0},{128,64},{192,128},{2,192},{66,2},{130,66},{194,130... | collective-permute-start | bytes 3145736 | tf_op jit(solution)/shard_map/tokens/ppermute | solution.py:40
  64.7 27.2 %collective-permute-start.1 = (bf16[256,2048]{1,0:T(8,128)(2,1)S(1)}, bf16[256,2048]{1,0:T(8,128)(2,1)}, u32[]{:S(2)}, u32[]{:S(2)}) collective-permute-start(bf16[256,2048]{1,0:T(8,128)(2,1)S(1)} %collective-permute-done), channel_id=1, source_target_pairs={{0,64},{64,128},{128,192},{192,2},{2,66},{66,130},{130,194},{194,0... | collective-permute-start | bytes 3145736 | tf_op jit(solution)/shard_map/tokens/ppermute | solution.py:40
  64.8 21.7 %collective-permute-start.15 = (f32[2,16,128]{2,1,0:T(8,128)S(1)}, f32[2,16,128]{2,1,0:T(8,128)S(1)}, u32[]{:S(2)}, u32[]{:S(2)}) collective-permute-start(f32[2,16,128]{2,1,0:T(8,128)S(1)} %pad_maximum_fusion.13), channel_id=1, source_target_pairs={{0,3},{1,67},{2,131},{3,195},{64,0},{65,64},{66,128},{67,192},{128... | collective-permute-start | bytes 49160 | tf_op jit(solution)/shard_map/direction/ppermute | solution.py:47
  66.5 23.6 %collective-permute-start.14 = (f32[2,16,128]{2,1,0:T(8,128)S(1)}, f32[2,16,128]{2,1,0:T(8,128)S(1)}, u32[]{:S(2)}, u32[]{:S(2)}) collective-permute-start(f32[2,16,128]{2,1,0:T(8,128)S(1)} %pad_maximum_fusion.13), channel_id=1, source_target_pairs={{0,2},{1,66},{2,130},{3,194},{64,3},{65,67},{66,131},{67,195},{128... | collective-permute-start | bytes 49160 | tf_op jit(solution)/shard_map/direction/ppermute | solution.py:47
  66.8 23.3 %collective-permute-start.13 = (f32[2,16,128]{2,1,0:T(8,128)S(1)}, f32[2,16,128]{2,1,0:T(8,128)S(1)}, u32[]{:S(2)}, u32[]{:S(2)}) collective-permute-start(f32[2,16,128]{2,1,0:T(8,128)S(1)} %pad_maximum_fusion.13), channel_id=1, source_target_pairs={{0,1},{1,65},{2,129},{3,193},{64,2},{65,66},{66,130},{67,194},{128... | collective-permute-start | bytes 49160 | tf_op jit(solution)/shard_map/direction/ppermute | solution.py:47
  86.6 5.0 %collective-permute-start.12 = (f32[2,16,128]{2,1,0:T(8,128)S(1)}, f32[2,16,128]{2,1,0:T(8,128)S(1)}, u32[]{:S(2)}, u32[]{:S(2)}) collective-permute-start(f32[2,16,128]{2,1,0:T(8,128)S(1)} %pad_maximum_fusion.13), channel_id=1, source_target_pairs={{0,0},{1,64},{2,128},{3,192},{64,1},{65,65},{66,129},{67,193},{128... | collective-permute-start | bytes 49160 | tf_op jit(solution)/shard_map/direction/ppermute | solution.py:47
  91.7 24.8 %collective-permute-start.6 = (bf16[256,2048]{1,0:T(8,128)(2,1)}, bf16[256,2048]{1,0:T(8,128)(2,1)S(1)}, u32[]{:S(2)}, u32[]{:S(2)}) collective-permute-start(bf16[256,2048]{1,0:T(8,128)(2,1)} %collective-permute-done.5), channel_id=1, source_target_pairs={{0,194},{64,0},{128,64},{192,128},{2,192},{66,2},{130,66},{194,130... | collective-permute-start | bytes 3145736 | tf_op jit(solution)/shard_map/tokens/ppermute | solution.py:40
  91.9 25.1 %collective-permute-start.2 = (bf16[256,2048]{1,0:T(8,128)(2,1)}, bf16[256,2048]{1,0:T(8,128)(2,1)}, u32[]{:S(2)}, u32[]{:S(2)}) collective-permute-start(bf16[256,2048]{1,0:T(8,128)(2,1)} %collective-permute-done.1), channel_id=1, source_target_pairs={{0,64},{64,128},{128,192},{192,2},{2,66},{66,130},{130,194},{194,0... | collective-permute-start | bytes 3145736 | tf_op jit(solution)/shard_map/tokens/ppermute | solution.py:40
  120.4 13.9 %collective-permute-start.11 = (f32[256,1]{1,0:T(8,128)}, f32[256,1]{1,0:T(8,128)}, u32[]{:S(2)}, u32[]{:S(2)}) collective-permute-start(f32[256,1]{1,0:T(8,128)} %broadcast_select_fusion.10), channel_id=1, source_target_pairs={{0,1},{1,0},{2,3},{3,2},{4,5},{5,4},{6,7},{7,6},{8,9},{9,8},{10,11... | collective-permute-start | bytes 3080 | tf_op jit(solution)/shard_map/project/ppermute | solution.py:60
  128.4 22.7 %collective-permute-start.7 = (bf16[128,2048]{1,0:T(8,128)(2,1)}, bf16[128,2048]{1,0:T(8,128)(2,1)}, u32[]{:S(2)}, u32[]{:S(2)}) collective-permute-start(bf16[128,2048]{1,0:T(8,128)(2,1)} %slice.61), channel_id=1, source_target_pairs={{0,194},{64,0},{128,64},{192,128},{2,192},{66,2},{130,66},{194,130... | collective-permute-start | bytes 1572872 | tf_op jit(solution)/shard_map/tokens/ppermute | solution.py:40
  134.2 16.9 %collective-permute-start.3 = (bf16[128,2048]{1,0:T(8,128)(2,1)}, bf16[128,2048]{1,0:T(8,128)(2,1)}, u32[]{:S(2)}, u32[]{:S(2)}) collective-permute-start(bf16[128,2048]{1,0:T(8,128)(2,1)} %slice.60), channel_id=1, source_target_pairs={{0,64},{64,128},{128,192},{192,2},{2,66},{66,130},{130,194},{194,0... | collective-permute-start | bytes 1572872 | tf_op jit(solution)/shard_map/tokens/ppermute | solution.py:40
  143.9 5.9 %collective-permute-start.10 = (f32[256,768]{1,0:T(8,128)S(1)}, f32[256,768]{1,0:T(8,128)S(1)}, u32[]{:S(2)}, u32[]{:S(2)}) collective-permute-start(f32[256,768]{1,0:T(8,128)S(1)} %get-tuple-element.76), channel_id=1, source_target_pairs={{0,1},{1,0},{2,3},{3,2},{4,5},{5,4},{6,7},{7,6},{8,9},{9,8},{10,11... | collective-permute-start | bytes 2359304 | tf_op jit(solution)/shard_map/project/ppermute | solution.py:60
  156.2 6.3 %collective-permute-start.16 = (f32[256,768]{1,0:T(8,128)S(1)}, f32[256,768]{1,0:T(8,128)S(1)}, u32[]{:S(2)}, u32[]{:S(2)}) collective-permute-start(f32[256,768]{1,0:T(8,128)S(1)} %get-tuple-element.74), channel_id=1, source_target_pairs={{0,1},{1,0},{2,3},{3,2},{4,5},{5,4},{6,7},{7,6},{8,9},{9,8},{10,11... | collective-permute-start | bytes 2359304 | tf_op jit(solution)/shard_map/project/ppermute | solution.py:60
  156.3 6.1 %collective-permute-start.17 = (f32[256,1]{1,0:T(8,128)S(1)}, f32[256,1]{1,0:T(8,128)S(1)}, u32[]{:S(2)}, u32[]{:S(2)}) collective-permute-start(f32[256,1]{1,0:T(8,128)S(1)} %broadcast_select_fusion.9), channel_id=1, source_target_pairs={{0,1},{1,0},{2,3},{3,2},{4,5},{5,4},{6,7},{7,6},{8,9},{9,8},{10,11... | collective-permute-start | bytes 3080 | tf_op jit(solution)/shard_map/project/ppermute | solution.py:60
  156.9 9.5 %collective-permute-start.19 = (bf16[3,512]{1,0:T(4,128)(2,1)S(1)}, bf16[3,512]{1,0:T(4,128)(2,1)S(1)}, u32[]{:S(2)}, u32[]{:S(2)}) collective-permute-start(bf16[3,512]{1,0:T(4,128)(2,1)S(1)} %pad_maximum_fusion.16), channel_id=1, source_target_pairs={{0,64},{1,192},{64,128},{65,0},{128,193},{129,65},{192,1},{193,129... | collective-permute-start | bytes 9224 | tf_op jit(solution)/shard_map/return_heads/ppermute | solution.py:34
  163.8 46.5 %copy-start.10 = (f32[4,1,16,128]{3,2,1,0:T(8,128)S(1)}, f32[4,1,16,128]{3,2,1,0:T(8,128)}, u32[]{:S(2)}) copy-start(f32[4,1,16,128]{3,2,1,0:T(8,128)} %copy-done.9) | copy-start | bytes 98308
  163.8 46.5 %copy-start.11 = (f32[4,1,16,128]{3,2,1,0:T(8,128)S(1)}, f32[4,1,16,128]{3,2,1,0:T(8,128)}, u32[]{:S(2)}) copy-start(f32[4,1,16,128]{3,2,1,0:T(8,128)} %get-tuple-element.100) | copy-start | bytes 98308
  163.9 5.3 %collective-permute-start.18 = (bf16[3,512]{1,0:T(4,128)(2,1)S(1)}, bf16[3,512]{1,0:T(4,128)(2,1)S(1)}, u32[]{:S(2)}, u32[]{:S(2)}) collective-permute-start(bf16[3,512]{1,0:T(4,128)(2,1)S(1)} %pad_maximum_fusion.15), channel_id=1, source_target_pairs={{0,0},{1,128},{64,64},{65,192},{128,129},{129,1},{192,193},{193,65... | collective-permute-start | bytes 9224 | tf_op jit(solution)/shard_map/return_heads/ppermute | solution.py:34
  170.1 27.4 %all-to-all-start.1 = ((bf16[64,3,1024]{2,1,0:T(4,128)(2,1)}), bf16[64,3,1024]{2,1,0:T(4,128)(2,1)S(1)}, u32[]{:S(2)}, u32[]{:S(2)}) async-start(bf16[64,3,1024]{2,1,0:T(4,128)(2,1)} %broadcast_in_dim.107), calls=%async_computation.1 | async-start | bytes 1048576 | tf_op jit(solution)/shard_map/tail/all_to_all | solution.py:23
  174.7 22.8 %collective-permute-start.20 = (bf16[256,512]{1,0:T(8,128)(2,1)S(1)}, bf16[256,512]{1,0:T(8,128)(2,1)S(1)}, u32[]{:S(2)}, u32[]{:S(2)}) collective-permute-start(bf16[256,512]{1,0:T(8,128)(2,1)S(1)} %get-tuple-element.66), channel_id=1, source_target_pairs={{0,0},{1,128},{64,64},{65,192},{128,129},{129,1},{192,193},{193,65... | collective-permute-start | bytes 786440 | tf_op jit(solution)/shard_map/return_heads/ppermute | solution.py:34
  180.2 17.3 %collective-permute-start.21 = (bf16[256,512]{1,0:T(8,128)(2,1)S(1)}, bf16[256,512]{1,0:T(8,128)(2,1)S(1)}, u32[]{:S(2)}, u32[]{:S(2)}) collective-permute-start(bf16[256,512]{1,0:T(8,128)(2,1)S(1)} %get-tuple-element.67), channel_id=1, source_target_pairs={{0,64},{1,192},{64,128},{65,0},{128,193},{129,65},{192,1},{193,129... | collective-permute-start | bytes 786440 | tf_op jit(solution)/shard_map/return_heads/ppermute | solution.py:34
  197.9 8.8 %collective-permute-start.24 = (bf16[64,128]{1,0:T(8,128)(2,1)S(1)}, bf16[64,128]{1,0:T(8,128)(2,1)S(1)}, u32[]{:S(2)}, u32[]{:S(2)}) collective-permute-start(bf16[64,128]{1,0:T(8,128)(2,1)S(1)} %convolution_convert_fusion.1), channel_id=1, source_target_pairs={{0,3},{1,2},{2,1},{3,0},{4,7},{5,6},{6,5},{7,4},{8,11},{9,10},{10,... | collective-permute-start | bytes 49160 | tf_op jit(solution)/shard_map/tail/ppermute | solution.py:54
  203.8 6.5 %collective-permute-start.23 = (bf16[64,128]{1,0:T(8,128)(2,1)S(1)}, bf16[64,128]{1,0:T(8,128)(2,1)S(1)}, u32[]{:S(2)}, u32[]{:S(2)}) collective-permute-start(bf16[64,128]{1,0:T(8,128)(2,1)S(1)} %convolution_convert_fusion.1), channel_id=1, source_target_pairs={{0,2},{1,3},{2,0},{3,1},{4,6},{5,7},{6,4},{7,5},{8,10},{9,11},{10,... | collective-permute-start | bytes 49160 | tf_op jit(solution)/shard_map/tail/ppermute | solution.py:54
  206.0 4.2 %collective-permute-start.22 = (bf16[64,128]{1,0:T(8,128)(2,1)S(1)}, bf16[64,128]{1,0:T(8,128)(2,1)S(1)}, u32[]{:S(2)}, u32[]{:S(2)}) collective-permute-start(bf16[64,128]{1,0:T(8,128)(2,1)S(1)} %convolution_convert_fusion.1), channel_id=1, source_target_pairs={{0,1},{1,0},{2,3},{3,2},{4,5},{5,4},{6,7},{7,6},{8,9},{9,8},{10,11... | collective-permute-start | bytes 49160 | tf_op jit(solution)/shard_map/tail/ppermute | solution.py:54
  211.7 17.0 %all-to-all-start.2 = ((f32[64,1,128]{2,1,0:T(1,128)}), f32[64,1,128]{2,1,0:T(1,128)S(1)}, u32[]{:S(2)}, u32[]{:S(2)}) async-start(f32[64,1,128]{2,1,0:T(1,128)} %bitcast.21), calls=%async_computation.2 | async-start | bytes 65536 | tf_op jit(solution)/shard_map/tail/all_to_all | solution.py:260
  (10 other events, 91.7 us)
Sparse Core Ops, SparseCore 0:
  53.6 67.0 all-gather.1
where the time goes:
time: 240 us; the launch traced here: 239 us
  waiting for transfers between devices  83.2 us (35%)
  starting transfers between devices  80.2 us (33%)
  other arithmetic  26.4 us (11%)
  matrix products  20 us (8%)
  between operations  17.6 us (7%)
  local copies, waits for them, and re-layouts  9.3 us (4%)
  Pallas kernels  2.63 us (1%)
    ppermute x6, waiting for transfers between devices, send(): return lax.ppermute(value, ('zl', 'c'), pairs)  30.5 us
    ppermute x8, starting transfers between devices, along(): return lax.ppermute(value, ('zl', 'zh'), pairs)  20.2 us
    ppermute x8, waiting for transfers between devices, along(): return lax.ppermute(value, ('zl', 'zh'), pairs)  19.6 us
    ppermute x6, starting transfers between devices, send(): return lax.ppermute(value, ('zl', 'c'), pairs)  19.2 us
    dot_general x8, matrix products, project(): return (jnp.dot(block, weight, preferred_element_type=F32), square)  16.3 us
    ppermute x4, waiting for transfers between devices, to_column_owners(): got.append(lax.ppermute(value, ('zl', *MP), pairs))  15.2 us
    reduce_sum x8, other arithmetic, scaled(): done = ((t * g).astype(BF16), jnp.sum(t * t, axis=1, keepdims=True))  14.8 us
    all_to_all x1, starting transfers between devices, per_device(): packed = lax.all_to_all(packed, DP, 0, 0, tiled=True)  8.84 us
  transfers between devices with their start and end apart: 29, of which 10 were waited for; matrix products, arithmetic and copies ran while one was open for 19% of the time, Pallas kernels for 1%

commit v1 on v0

--- a/solution.py
+++ b/solution.py
@@ -115,14 +115,22 @@
     )(kept, came, squares, *tables)
 
 
-def ring_share(block):
-    got = {0: block}
-    for r in (1, 2, 3):
-        for sign in (1, -1):
-            got[-sign * r] = along(got[-sign * (r - 1)], sign)
-    cut = block.shape[0] // 2
-    got[4] = (along(got[-3][:cut], 1), along(got[3][cut:], -1))
-    return got
+def last_hop(value):
+    place = lambda z, c: (z % 4) * 4 + (z // 4) * 2 + c
+    pairs = [
+        (place(z, c), place((z + 1 - 2 * c) % 8, c)) for z in range(8) for c in range(2)
+    ]
+    return lax.ppermute(value, ("zl", *MP), pairs)
+
+
+def to_line(value, zl):
+    got = []
+    for i in range(4):
+        got.append(send(value, lambda z, c: (2 * (z % 2) + c + i, z // 2)))
+    got = jnp.stack(got)
+    return jnp.stack(
+        [lax.dynamic_index_in_dim(got, (zl - q) % 4, 0, keepdims=False) for q in range(4)]
+    )
 
 
 def per_device(tokens, gain, w_query, w_key, w_value, w_out, final_gain, unembed, clean, corrupt):
@@ -137,9 +145,6 @@
 
     even = zl % 2 == 0
     width = w_query.shape[1] // 2
-
-    with jax.named_scope("tokens"):
-        blocks = ring_share(tokens)
 
     with jax.named_scope("weights"):
         wkv = jnp.concatenate([w_key, w_value], axis=1)
@@ -153,6 +158,7 @@
         pa = send(pieces[0], lambda z, c: (2 * c + z // 2, z % 2))
         pb = send(pieces[1], lambda z, c: (2 * c + 1 - z // 2, z % 2))
         rows = jnp.concatenate([jnp.where(even, pa, pb), jnp.where(even, pb, pa)], axis=1)
+        weights = lax.all_gather(rows, ("y", "x"), axis=0, tiled=True)
 
     with jax.named_scope("direction"):
         vocab_rows = unembed.shape[0]
@@ -166,14 +172,21 @@
         own_last = jnp.where(here, tokens[LENGTH - 1].reshape(1, 16, 1, 128), 0).astype(BF16)
         packed = jnp.concatenate([found, own_last], axis=2).reshape(64, 17, 128)
         packed = lax.all_to_all(packed, DP, 0, 0, tiled=True)
-        rows, packed, *_ = lax.optimization_barrier((rows, packed, blocks[1], blocks[-1]))
-        weights = lax.all_gather(rows, ("y", "x"), axis=0, tiled=True)
         packed = packed.astype(F32)
         packed = jnp.sum(packed.reshape(4, 16, 17, 128), axis=0)
         gain_cols = lax.dynamic_slice_in_dim(final_gain, yx * 128, 128, 0).astype(F32)
         weighted = gain_cols * jnp.sum(packed[:, :16], axis=0)
         both = jnp.stack([weighted, packed[:, 16]])
         both = to_column_owners(both, zl, 2 * zh + core)
+        blocks = {0: tokens}
+        for r in (1, 2, 3):
+            for sign in (1, -1):
+                blocks[-sign * r] = along(blocks[-sign * (r - 1)], sign)
+            if r == 2:
+                both, blocks[2], blocks[-2] = lax.optimization_barrier(
+                    (both, blocks[2], blocks[-2])
+                )
+        blocks[4] = last_hop(jnp.where(first, blocks[-3], blocks[3]))
         weighted_cols = both[:, 0].reshape(64, 128)
         token_cols = both[:, 1].reshape(64, 128)
         back_w = back(weighted_cols)
@@ -212,7 +225,7 @@
         last_block, near, next_2, mixed_1, back_w, token_cols = lax.optimization_barrier(
             (blocks[4], near, next_2, mixed_1, back_w, token_cols)
         )
-        last_block = project(*scaled(4, jnp.concatenate(last_block, axis=0)))
+        last_block = project(*scaled(4, last_block))
         mixed_0, total_0 = attend(both_sides(near, last_block), next_2)
 
     with jax.named_scope("return_heads"):
@@ -224,22 +237,28 @@
                 [jnp.where(even, oa, ob), jnp.where(even, ob, oa)], axis=1
             )
 
-        def summary(mixed, total):
-            high = lax.reduce_precision(total, 8, 7)
-            return jnp.concatenate(
-                [mixed[-1:], high.astype(BF16), (total - high).astype(BF16)], axis=0
-            )
-
-        own = owned(summary(mixed_0, total_0), summary(mixed_1, total_1))
-        own, mixed_0, mixed_1 = lax.optimization_barrier((own, mixed_0, mixed_1))
+    with jax.named_scope("tail"):
+        total = total_0 + total_1
+        high = lax.reduce_precision(total, 8, 7)
+        line = jnp.concatenate(
+            [mixed_0[-1:], mixed_1[-1:], high.astype(BF16), (total - high).astype(BF16)], axis=0
+        )
+        every = from_everyone(to_line(line, zl), ("y", "x"))
+        every, mixed_0, mixed_1 = lax.optimization_barrier((every, mixed_0, mixed_1))
         head_out = owned(mixed_0, mixed_1)
-
-    with jax.named_scope("tail"):
-        every = from_everyone(own, DP)
-        last = every[:, 0]
+        every = every.reshape(16, 2, 2, 4, width)
+        last = every[:, :, :, :2].reshape(16, 2, 4, width)
+        last = jnp.concatenate(
+            [
+                jnp.where(first, jnp.roll(last[:, h], h, axis=1), jnp.roll(last[:, h], h + 2, axis=1))
+                for h in (0, 1)
+            ],
+            axis=2,
+        )
+        last = last.swapaxes(0, 1).reshape(64, 2 * width)
         part = jnp.dot(last, w_out, preferred_element_type=F32).astype(BF16)
         attn_last = sum_over_mp(part).astype(BF16)
-        head_mean = jnp.sum(every[:, 1:].astype(F32), axis=(0, 1)) / TOKENS
+        head_mean = jnp.sum(every[:, :, :, 2:].astype(F32), axis=(0, 2, 3)).reshape(-1) / TOKENS
         gap = head_mean[None] - last.astype(F32)
 
         def per_head(grads):

time: 240 us -> 221 us (0.921)
  blocking collectives: 0 us -> 10.1 us
  waiting for transfers between devices: 83.2 us -> 73.2 us
  starting transfers between devices: 80.2 us -> 72.9 us
  other arithmetic: 26.4 us -> 21.6 us
  local copies, waits for them, and re-layouts: 9.3 us -> 5.31 us
  matrix products: 20 us -> 16.4 us
    ppermute x6 -> x8, waiting for transfers between devices: 30.5 us -> 13.4 us  [send(): return lax.ppermute(value, ('zl', 'c'), pairs)]
    all_to_all x1, waiting for transfers between devices: 6.18 us -> 17.4 us  [per_device(): packed = lax.all_to_all(packed, DP, 0, 0, tiled=True)]
    all_to_all x0 -> x1, blocking collectives: none -> 10.1 us  [from_everyone(): lax.all_to_all(jnp.broadcast_to(value[None], (count, *value.shape)), axis...]
    ppermute x8 -> x6, starting transfers between devices: 20.2 us -> 10.1 us  [along(): return lax.ppermute(value, ('zl', 'zh'), pairs)]
    all_to_all x1, waiting for transfers between devices: 8.12 us -> 3.08 us  [per_device(): lax.all_to_all(packed[:, None], DP, 0, 0, tiled=True)]
    ppermute x4, starting transfers between devices: 7.42 us -> 12.2 us  [to_column_owners(): got.append(lax.ppermute(value, ('zl', *MP), pairs))]
    all_to_all x1 -> x0, starting transfers between devices: 4.63 us -> none  [from_everyone(): lax.all_to_all(jnp.broadcast_to(value[None], (count, *value.shape)), axis...]
    dot_general x8, matrix products: 16.3 us -> 12.7 us  [project(): return (jnp.dot(block, weight, preferred_element_type=F32), square)]
  transfers between devices with their start and end apart: 29 -> 29, of which waited for: 10 -> 15; matrix products, arithmetic and copies ran while one was open for 19% -> 15% of each run, Pallas kernels for 1% -> 1%
where the time goes in v1:
time: 221 us; the launch traced here: 220 us
  waiting for transfers between devices  73.2 us (33%)
  starting transfers between devices  72.9 us (33%)
  other arithmetic  21.6 us (10%)
  between operations  17.8 us (8%)
  matrix products  16.4 us (7%)
  blocking collectives  10.1 us (5%)
  local copies, waits for them, and re-layouts  5.31 us (2%)
  Pallas kernels  2.63 us (1%)
    ppermute x8, starting transfers between devices, send(): return lax.ppermute(value, ('zl', 'c'), pairs)  22.4 us
    ppermute x6, waiting for transfers between devices, along(): return lax.ppermute(value, ('zl', 'zh'), pairs)  18.4 us
    all_to_all x1, waiting for transfers between devices, per_device(): packed = lax.all_to_all(packed, DP, 0, 0, tiled=True)  17.4 us
    ppermute x4, waiting for transfers between devices, to_column_owners(): got.append(lax.ppermute(value, ('zl', *MP), pairs))  17.3 us
    ppermute x8, waiting for transfers between devices, send(): return lax.ppermute(value, ('zl', 'c'), pairs)  13.4 us
    dot_general x8, matrix products, project(): return (jnp.dot(block, weight, preferred_element_type=F32), square)  12.7 us
    reduce_sum x6, other arithmetic, scaled(): done = ((t * g).astype(BF16), jnp.sum(t * t, axis=1, keepdims=True))  12.2 us
    ppermute x4, starting transfers between devices, to_column_owners(): got.append(lax.ppermute(value, ('zl', *MP), pairs))  12.2 us
  transfers between devices with their start and end apart: 29, of which 15 were waited for; matrix products, arithmetic and copies ran while one was open for 15% of the time, Pallas kernels for 1%

profile of v1, /device:TPU:1, one launch (start us, length us, event | category | flops | bytes accessed | tf_op | source)
XLA Modules:
  0.0 220.0 jit_solution(1221693035522981958)
XLA Ops:
  9.2 6.3 %collective-permute-start.11 = (bf16[128,768]{1,0:T(8,128)(2,1)S(1)}, bf16[128,768]{1,0:T(8,128)(2,1)S(1)}, u32[]{:S(2)}, u32[]{:S(2)}) collective-permute-start(bf16[128,768]{1,0:T(8,128)(2,1)S(1)} %get-tuple-element.110), channel_id=1, source_target_pairs={{0,0},{1,128},{64,1},{65,129},{128,64},{129,192},{192,65},{193,193... | collective-permute-start | bytes 589832 | tf_op jit(solution)/shard_map/weights/ppermute | solution.py:34
  16.9 2.6 %collective-permute-done.11 = bf16[128,768]{1,0:T(8,128)(2,1)S(1)} collective-permute-done((bf16[128,768]{1,0:T(8,128)(2,1)S(1)}, bf16[128,768]{1,0:T(8,128)(2,1)S(1)}, u32[]{:S(2)}, u32[]{:S(2)}) %collective-permute-start.11) | collective-permute-done | bytes 196640 | tf_op jit(solution)/shard_map/weights/ppermute | solution.py:34
  19.5 4.9 %collective-permute-done.12 = bf16[128,768]{1,0:T(8,128)(2,1)S(1)} collective-permute-done((bf16[128,768]{1,0:T(8,128)(2,1)S(1)}, bf16[128,768]{1,0:T(8,128)(2,1)S(1)}, u32[]{:S(2)}, u32[]{:S(2)}) %collective-permute-start.12) | collective-permute-done | bytes 196640 | tf_op jit(solution)/shard_map/weights/ppermute | solution.py:34
  25.4 4.4 %collective-permute-start.4 = (bf16[256,2048]{1,0:T(8,128)(2,1)S(1)}, bf16[256,2048]{1,0:T(8,128)(2,1)S(1)}, u32[]{:S(2)}, u32[]{:S(2)}) collective-permute-start(bf16[256,2048]{1,0:T(8,128)(2,1)S(1)} %copy-done.3), channel_id=1, source_target_pairs={{0,194},{64,0},{128,64},{192,128},{2,192},{66,2},{130,66},{194,130... | collective-permute-start | bytes 3145736 | tf_op jit(solution)/shard_map/direction/ppermute | solution.py:40
  29.8 3.1 %fusion.41 = bf16[8,8,16,128]{3,1,2,0:T(8,128)(2,1)S(1)} fusion(bf16[1002,2048]{1,0:T(8,128)(2,1)} %param.17, s32[1002]{0:T(1024)S(1)} %iota_add_fusion, s32[64]{0:T(128)S(1)} %copy-done.13, s32[64]{0:T(128)S(1)} %copy-done.14), kind=kOutput, calls=%fused_computation.52 | convolution fusion | flops 263184128 | bytes 4370856 | tf_op jit(solution)/shard_map/direction/dot_general | solution.py:169
  34.1 8.3 %all-to-all-start = ((bf16[64,17,128]{2,1,0:T(8,128)(2,1)}), bf16[64,17,128]{2,1,0:T(8,128)(2,1)S(1)}, u32[]{:S(2)}, u32[]{:S(2)}) async-start(bf16[64,17,128]{2,1,0:T(8,128)(2,1)} %pad_maximum_fusion.1), calls=%async_computation | async-start | bytes 786432 | tf_op jit(solution)/shard_map/direction/all_to_all | solution.py:174
  44.8 17.4 %all-to-all-done = bf16[64,17,128]{2,1,0:T(8,128)(2,1)S(1)} async-done(((bf16[64,17,128]{2,1,0:T(8,128)(2,1)}), bf16[64,17,128]{2,1,0:T(8,128)(2,1)S(1)}, u32[]{:S(2)}, u32[]{:S(2)}) %all-to-all-start) | async-done | bytes 278560 | tf_op jit(solution)/shard_map/direction/all_to_all | solution.py:174
  62.3 2.6 %collective-permute-start.5 = (bf16[256,2048]{1,0:T(8,128)(2,1)S(1)}, bf16[256,2048]{1,0:T(8,128)(2,1)}, u32[]{:S(2)}, u32[]{:S(2)}) collective-permute-start(bf16[256,2048]{1,0:T(8,128)(2,1)S(1)} %collective-permute-done.4), channel_id=1, source_target_pairs={{0,194},{64,0},{128,64},{192,128},{2,192},{66,2},{130,66},{194,130... | collective-permute-start | bytes 3145736 | tf_op jit(solution)/shard_map/direction/ppermute | solution.py:40
  65.0 5.0 %collective-permute-start = (f32[2,16,128]{2,1,0:T(8,128)S(1)}, f32[2,16,128]{2,1,0:T(8,128)S(1)}, u32[]{:S(2)}, u32[]{:S(2)}) collective-permute-start(f32[2,16,128]{2,1,0:T(8,128)S(1)} %pad_maximum_fusion.13), channel_id=1, source_target_pairs={{0,0},{1,64},{2,128},{3,192},{64,1},{65,65},{66,129},{67,193},{128... | collective-permute-start | bytes 49160 | tf_op jit(solution)/shard_map/direction/ppermute | solution.py:47
  70.6 2.8 %collective-permute-start.2 = (f32[2,16,128]{2,1,0:T(8,128)S(1)}, f32[2,16,128]{2,1,0:T(8,128)S(1)}, u32[]{:S(2)}, u32[]{:S(2)}) collective-permute-start(f32[2,16,128]{2,1,0:T(8,128)S(1)} %pad_maximum_fusion.13), channel_id=1, source_target_pairs={{0,2},{1,66},{2,130},{3,194},{64,3},{65,67},{66,131},{67,195},{128... | collective-permute-start | bytes 49160 | tf_op jit(solution)/shard_map/direction/ppermute | solution.py:47
  73.4 15.3 %collective-permute-done = f32[2,16,128]{2,1,0:T(8,128)S(1)} collective-permute-done((f32[2,16,128]{2,1,0:T(8,128)S(1)}, f32[2,16,128]{2,1,0:T(8,128)S(1)}, u32[]{:S(2)}, u32[]{:S(2)}) %collective-permute-start) | collective-permute-done | bytes 16416 | tf_op jit(solution)/shard_map/direction/ppermute | solution.py:47
  88.7 4.3 %collective-permute-start.3 = (f32[2,16,128]{2,1,0:T(8,128)S(1)}, f32[2,16,128]{2,1,0:T(8,128)S(1)}, u32[]{:S(2)}, u32[]{:S(2)}) collective-permute-start(f32[2,16,128]{2,1,0:T(8,128)S(1)} %pad_maximum_fusion.13), channel_id=1, source_target_pairs={{0,3},{1,67},{2,131},{3,195},{64,0},{65,64},{66,128},{67,192},{128... | collective-permute-start | bytes 49160 | tf_op jit(solution)/shard_map/direction/ppermute | solution.py:47
  95.4 2.6 %fusion.27 = (f32[256]{0:T(256)S(1)}, bf16[256,2048]{1,0:T(8,128)(2,1)}) fusion(bf16[256,2048]{1,0:T(8,128)(2,1)} %collective-permute-done.6, f32[2048]{0:T(1024)S(1)} %get-tuple-element.121), kind=kLoop, calls=%fused_computation.44 | loop fusion | flops 2621184 | bytes 2106368 | tf_op jit(solution)/shard_map/project/reduce_sum | solution.py:203
  98.5 2.5 %collective-permute-start.9 = (bf16[256,2048]{1,0:T(8,128)(2,1)}, bf16[256,2048]{1,0:T(8,128)(2,1)S(1)}, u32[]{:S(2)}, u32[]{:S(2)}) collective-permute-start(bf16[256,2048]{1,0:T(8,128)(2,1)} %collective-permute-done.5), channel_id=1, source_target_pairs={{0,194},{64,0},{128,64},{192,128},{2,192},{66,2},{130,66},{194,130... | collective-permute-start | bytes 3145736 | tf_op jit(solution)/shard_map/direction/ppermute | solution.py:40
  101.0 2.5 %fusion.23 = (f32[256]{0:T(256)S(1)}, bf16[256,2048]{1,0:T(8,128)(2,1)}) fusion(bf16[256,2048]{1,0:T(8,128)(2,1)} %copy-done.4, f32[2048]{0:T(1024)S(1)} %get-tuple-element.123), kind=kLoop, calls=%fused_computation.40 | loop fusion | flops 2621184 | bytes 2106368 | tf_op jit(solution)/shard_map/project/reduce_sum | solution.py:203
  103.8 3.5 %fusion.19 = (f32[256]{0:T(256)S(1)}, bf16[256,2048]{1,0:T(8,128)(2,1)}, bf16[256,2048]{1,0:T(8,128)(2,1)}, f32[256]{0:T(256)S(1)}) fusion(bf16[256,2048]{1,0:T(8,128)(2,1)} %collective-permute-done.5, f32[2048]{0:T(1024)S(1)} %get-tuple-element.125, f32[2048]{0:T(1024)S(1)} %get-tuple-element.124, bf16[256,2048]{1,0:T(8,128)(2,1)} %collective-permute-done.7), kind=kLoop, calls=%fused_computation.36 | loop fusion | flops 5242368 | bytes 4212736 | tf_op jit(solution)/shard_map/project/reduce_sum | solution.py:203
  109.1 12.1 %collective-permute-done.8 = bf16[256,2048]{1,0:T(8,128)(2,1)S(1)} collective-permute-done((bf16[256,2048]{1,0:T(8,128)(2,1)}, bf16[256,2048]{1,0:T(8,128)(2,1)S(1)}, u32[]{:S(2)}, u32[]{:S(2)}) %collective-permute-start.8) | collective-permute-done | bytes 1048608 | tf_op jit(solution)/shard_map/direction/ppermute | solution.py:40
  121.2 6.3 %collective-permute-done.9 = bf16[256,2048]{1,0:T(8,128)(2,1)S(1)} collective-permute-done((bf16[256,2048]{1,0:T(8,128)(2,1)}, bf16[256,2048]{1,0:T(8,128)(2,1)S(1)}, u32[]{:S(2)}, u32[]{:S(2)}) %collective-permute-start.9) | collective-permute-done | bytes 1048608 | tf_op jit(solution)/shard_map/direction/ppermute | solution.py:40
  131.5 3.3 %fusion.2 = f32[256,768]{1,0:T(8,128)S(1)} fusion(bf16[256,2048]{1,0:T(8,128)(2,1)} %get-tuple-element.48, bf16[2048,1536]{1,0:T(8,128)(2,1)} %all-gather.2.cloned.1.call-done, s32[]{:T(128)S(6)} %select_n.327), kind=kOutput, calls=%fused_computation.2 | convolution fusion | flops 805306368 | bytes 4980740 | tf_op jit(solution)/shard_map/project/dot_general | solution.py:208
  134.8 3.3 %fusion.6 = f32[256,768]{1,0:T(8,128)S(1)} fusion(bf16[256,2048]{1,0:T(8,128)(2,1)} %get-tuple-element.46, bf16[2048,1536]{1,0:T(8,128)(2,1)} %all-gather.2.cloned.1.call-done, s32[]{:T(128)S(6)} %select_n.319), kind=kOutput, calls=%fused_computation.6 | convolution fusion | flops 805306368 | bytes 4980740 | tf_op jit(solution)/shard_map/project/dot_general | solution.py:208
  140.4 2.5 %collective-permute-start.13 = (f32[256,768]{1,0:T(8,128)S(1)}, f32[256,768]{1,0:T(8,128)S(1)}, u32[]{:S(2)}, u32[]{:S(2)}) collective-permute-start(f32[256,768]{1,0:T(8,128)S(1)} %get-tuple-element.76), channel_id=1, source_target_pairs={{0,1},{1,0},{2,3},{3,2},{4,5},{5,4},{6,7},{7,6},{8,9},{9,8},{10,11... | collective-permute-start | bytes 2359304 | tf_op jit(solution)/shard_map/project/ppermute | solution.py:60
  153.9 2.6 %collective-permute-start.17 = (bf16[4,512]{1,0:T(4,128)(2,1)S(1)}, bf16[4,512]{1,0:T(4,128)(2,1)S(1)}, u32[]{:S(2)}, u32[]{:S(2)}) collective-permute-start(bf16[4,512]{1,0:T(4,128)(2,1)S(1)} %pad_maximum_fusion.16), channel_id=1, source_target_pairs={{0,0},{1,64},{64,128},{65,192},{128,1},{129,65},{192,129},{193,193... | collective-permute-start | bytes 12296 | tf_op jit(solution)/shard_map/tail/ppermute | solution.py:34
  156.5 3.9 %collective-permute-start.18 = (bf16[4,512]{1,0:T(4,128)(2,1)S(1)}, bf16[4,512]{1,0:T(4,128)(2,1)S(1)}, u32[]{:S(2)}, u32[]{:S(2)}) collective-permute-start(bf16[4,512]{1,0:T(4,128)(2,1)S(1)} %pad_maximum_fusion.16), channel_id=1, source_target_pairs={{0,64},{1,128},{64,192},{65,0},{128,65},{129,129},{192,193},{193,1... | collective-permute-start | bytes 12296 | tf_op jit(solution)/shard_map/tail/ppermute | solution.py:34
  160.5 2.3 %collective-permute-start.20 = (bf16[4,512]{1,0:T(4,128)(2,1)S(1)}, bf16[4,512]{1,0:T(4,128)(2,1)S(1)}, u32[]{:S(2)}, u32[]{:S(2)}) collective-permute-start(bf16[4,512]{1,0:T(4,128)(2,1)S(1)} %pad_maximum_fusion.16), channel_id=1, source_target_pairs={{0,192},{1,0},{64,64},{65,128},{128,193},{129,1},{192,65},{193,129... | collective-permute-start | bytes 12296 | tf_op jit(solution)/shard_map/tail/ppermute | solution.py:34
  162.9 2.4 %collective-permute-done.19 = bf16[4,512]{1,0:T(4,128)(2,1)S(1)} collective-permute-done((bf16[4,512]{1,0:T(4,128)(2,1)S(1)}, bf16[4,512]{1,0:T(4,128)(2,1)S(1)}, u32[]{:S(2)}, u32[]{:S(2)}) %collective-permute-start.19) | collective-permute-done | bytes 4128 | tf_op jit(solution)/shard_map/tail/ppermute | solution.py:34
  165.9 10.1 %all_to_all.15 = bf16[16,4,4,512]{3,2,1,0:T(4,128)(2,1)S(1)} all-to-all(bf16[16,4,4,512]{3,2,1,0:T(4,128)(2,1)S(1)} %broadcast_in_dim.107), channel_id=1, replica_groups=mesh['zl'=4,'y'=4,'x'=4,'zh'=2,'c'=2] {'y','x'}, dimensions={0} | all-to-all | bytes 524288 | tf_op jit(solution)/shard_map/tail/all_to_all | solution.py:23
  176.7 3.3 %collective-permute-start.23 = (bf16[64,128]{1,0:T(8,128)(2,1)S(1)}, bf16[64,128]{1,0:T(8,128)(2,1)S(1)}, u32[]{:S(2)}, u32[]{:S(2)}) collective-permute-start(bf16[64,128]{1,0:T(8,128)(2,1)S(1)} %convolution_convert_fusion.1), channel_id=1, source_target_pairs={{0,1},{1,0},{2,3},{3,2},{4,5},{5,4},{6,7},{7,6},{8,9},{9,8},{10,11... | collective-permute-start | bytes 49160 | tf_op jit(solution)/shard_map/tail/ppermute | solution.py:54
  180.9 4.8 %collective-permute-start.25 = (bf16[64,128]{1,0:T(8,128)(2,1)S(1)}, bf16[64,128]{1,0:T(8,128)(2,1)S(1)}, u32[]{:S(2)}, u32[]{:S(2)}) collective-permute-start(bf16[64,128]{1,0:T(8,128)(2,1)S(1)} %convolution_convert_fusion.1), channel_id=1, source_target_pairs={{0,3},{1,2},{2,1},{3,0},{4,7},{5,6},{6,5},{7,4},{8,11},{9,10},{10,... | collective-permute-start | bytes 49160 | tf_op jit(solution)/shard_map/tail/ppermute | solution.py:54
  189.4 7.2 %all-to-all-start.2 = ((f32[64,1,128]{2,1,0:T(1,128)}), f32[64,1,128]{2,1,0:T(1,128)S(1)}, u32[]{:S(2)}, u32[]{:S(2)}) async-start(f32[64,1,128]{2,1,0:T(1,128)} %bitcast.31), calls=%async_computation.2 | async-start | bytes 65536 | tf_op jit(solution)/shard_map/tail/all_to_all | solution.py:279
  196.6 4.7 %collective-permute-start.21 = (bf16[256,512]{1,0:T(8,128)(2,1)S(1)}, bf16[256,512]{1,0:T(8,128)(2,1)S(1)}, u32[]{:S(2)}, u32[]{:S(2)}) collective-permute-start(bf16[256,512]{1,0:T(8,128)(2,1)S(1)} %get-tuple-element.66), channel_id=1, source_target_pairs={{0,0},{1,128},{64,64},{65,192},{128,129},{129,1},{192,193},{193,65... | collective-permute-start | bytes 786440 | tf_op jit(solution)/shard_map/tail/ppermute | solution.py:34
  202.4 3.1 %all-to-all-done.2 = f32[64,1,128]{2,1,0:T(1,128)S(1)} async-done(((f32[64,1,128]{2,1,0:T(1,128)}), f32[64,1,128]{2,1,0:T(1,128)S(1)}, u32[]{:S(2)}, u32[]{:S(2)}) %all-to-all-start.2) | async-done | bytes 32800 | tf_op jit(solution)/shard_map/tail/all_to_all | solution.py:279
  208.7 2.4 %collective-permute-done.22 = bf16[256,512]{1,0:T(8,128)(2,1)S(1)} collective-permute-done((bf16[256,512]{1,0:T(8,128)(2,1)S(1)}, bf16[256,512]{1,0:T(8,128)(2,1)S(1)}, u32[]{:S(2)}, u32[]{:S(2)}) %collective-permute-start.22) | collective-permute-done | bytes 262176 | tf_op jit(solution)/shard_map/tail/ppermute | solution.py:34
  (156 shorter events, 39.7 us)
Async XLA Ops:
  7.2 101.7 %copy-start = (bf16[1024,128]{1,0:T(8,128)(2,1)S(1)}, bf16[1024,128]{1,0:T(8,128)(2,1)}, u32[]{:S(2)}) copy-start(bf16[1024,128]{1,0:T(8,128)(2,1)} %param.15) | copy-start | bytes 786436
  7.2 124.3 %all-gather.2.cloned.1.call-start = ((), (), s32[]{:S(2)}) async-start(), calls=%async_computation.3 | async-start | bytes 6684672 | tf_op jit(solution)/shard_map/weights/all_gather | solution.py:161
  9.2 10.3 %collective-permute-start.11 = (bf16[128,768]{1,0:T(8,128)(2,1)S(1)}, bf16[128,768]{1,0:T(8,128)(2,1)S(1)}, u32[]{:S(2)}, u32[]{:S(2)}) collective-permute-start(bf16[128,768]{1,0:T(8,128)(2,1)S(1)} %get-tuple-element.110), channel_id=1, source_target_pairs={{0,0},{1,128},{64,1},{65,129},{128,64},{129,192},{192,65},{193,193... | collective-permute-start | bytes 589832 | tf_op jit(solution)/shard_map/weights/ppermute | solution.py:34
  15.5 9.0 %collective-permute-start.12 = (bf16[128,768]{1,0:T(8,128)(2,1)S(1)}, bf16[128,768]{1,0:T(8,128)(2,1)S(1)}, u32[]{:S(2)}, u32[]{:S(2)}) collective-permute-start(bf16[128,768]{1,0:T(8,128)(2,1)S(1)} %get-tuple-element.111), channel_id=1, source_target_pairs={{0,64},{1,192},{64,65},{65,193},{128,0},{129,128},{192,1},{193,129... | collective-permute-start | bytes 589832 | tf_op jit(solution)/shard_map/weights/ppermute | solution.py:34
  25.3 39.7 %collective-permute-start.6 = (bf16[256,2048]{1,0:T(8,128)(2,1)S(1)}, bf16[256,2048]{1,0:T(8,128)(2,1)}, u32[]{:S(2)}, u32[]{:S(2)}) collective-permute-start(bf16[256,2048]{1,0:T(8,128)(2,1)S(1)} %copy-done.3), channel_id=1, source_target_pairs={{0,64},{64,128},{128,192},{192,2},{2,66},{66,130},{130,194},{194,0... | collective-permute-start | bytes 3145736 | tf_op jit(solution)/shard_map/direction/ppermute | solution.py:40
  25.4 36.9 %collective-permute-start.4 = (bf16[256,2048]{1,0:T(8,128)(2,1)S(1)}, bf16[256,2048]{1,0:T(8,128)(2,1)S(1)}, u32[]{:S(2)}, u32[]{:S(2)}) collective-permute-start(bf16[256,2048]{1,0:T(8,128)(2,1)S(1)} %copy-done.3), channel_id=1, source_target_pairs={{0,194},{64,0},{128,64},{192,128},{2,192},{66,2},{130,66},{194,130... | collective-permute-start | bytes 3145736 | tf_op jit(solution)/shard_map/direction/ppermute | solution.py:40
  34.1 28.0 %all-to-all-start = ((bf16[64,17,128]{2,1,0:T(8,128)(2,1)}), bf16[64,17,128]{2,1,0:T(8,128)(2,1)S(1)}, u32[]{:S(2)}, u32[]{:S(2)}) async-start(bf16[64,17,128]{2,1,0:T(8,128)(2,1)} %pad_maximum_fusion.1), calls=%async_computation | async-start | bytes 786432 | tf_op jit(solution)/shard_map/direction/all_to_all | solution.py:174
  62.3 35.7 %copy-start.4 = (bf16[256,2048]{1,0:T(8,128)(2,1)}, bf16[256,2048]{1,0:T(8,128)(2,1)S(1)}, u32[]{:S(2)}) copy-start(bf16[256,2048]{1,0:T(8,128)(2,1)S(1)} %collective-permute-done.4) | copy-start | bytes 3145732
  62.3 35.6 %collective-permute-start.5 = (bf16[256,2048]{1,0:T(8,128)(2,1)S(1)}, bf16[256,2048]{1,0:T(8,128)(2,1)}, u32[]{:S(2)}, u32[]{:S(2)}) collective-permute-start(bf16[256,2048]{1,0:T(8,128)(2,1)S(1)} %collective-permute-done.4), channel_id=1, source_target_pairs={{0,194},{64,0},{128,64},{192,128},{2,192},{66,2},{130,66},{194,130... | collective-permute-start | bytes 3145736 | tf_op jit(solution)/shard_map/direction/ppermute | solution.py:40
  64.9 33.0 %collective-permute-start.7 = (bf16[256,2048]{1,0:T(8,128)(2,1)}, bf16[256,2048]{1,0:T(8,128)(2,1)}, u32[]{:S(2)}, u32[]{:S(2)}) collective-permute-start(bf16[256,2048]{1,0:T(8,128)(2,1)} %collective-permute-done.6), channel_id=1, source_target_pairs={{0,64},{64,128},{128,192},{192,2},{2,66},{66,130},{130,194},{194,0... | collective-permute-start | bytes 3145736 | tf_op jit(solution)/shard_map/direction/ppermute | solution.py:40
  65.0 23.8 %collective-permute-start = (f32[2,16,128]{2,1,0:T(8,128)S(1)}, f32[2,16,128]{2,1,0:T(8,128)S(1)}, u32[]{:S(2)}, u32[]{:S(2)}) collective-permute-start(f32[2,16,128]{2,1,0:T(8,128)S(1)} %pad_maximum_fusion.13), channel_id=1, source_target_pairs={{0,0},{1,64},{2,128},{3,192},{64,1},{65,65},{66,129},{67,193},{128... | collective-permute-start | bytes 49160 | tf_op jit(solution)/shard_map/direction/ppermute | solution.py:47
  70.5 22.8 %collective-permute-start.1 = (f32[2,16,128]{2,1,0:T(8,128)S(1)}, f32[2,16,128]{2,1,0:T(8,128)S(1)}, u32[]{:S(2)}, u32[]{:S(2)}) collective-permute-start(f32[2,16,128]{2,1,0:T(8,128)S(1)} %pad_maximum_fusion.13), channel_id=1, source_target_pairs={{0,1},{1,65},{2,129},{3,193},{64,2},{65,66},{66,130},{67,194},{128... | collective-permute-start | bytes 49160 | tf_op jit(solution)/shard_map/direction/ppermute | solution.py:47
  70.6 22.7 %collective-permute-start.2 = (f32[2,16,128]{2,1,0:T(8,128)S(1)}, f32[2,16,128]{2,1,0:T(8,128)S(1)}, u32[]{:S(2)}, u32[]{:S(2)}) collective-permute-start(f32[2,16,128]{2,1,0:T(8,128)S(1)} %pad_maximum_fusion.13), channel_id=1, source_target_pairs={{0,2},{1,66},{2,130},{3,194},{64,3},{65,67},{66,131},{67,195},{128... | collective-permute-start | bytes 49160 | tf_op jit(solution)/shard_map/direction/ppermute | solution.py:47
  88.7 6.6 %collective-permute-start.3 = (f32[2,16,128]{2,1,0:T(8,128)S(1)}, f32[2,16,128]{2,1,0:T(8,128)S(1)}, u32[]{:S(2)}, u32[]{:S(2)}) collective-permute-start(f32[2,16,128]{2,1,0:T(8,128)S(1)} %pad_maximum_fusion.13), channel_id=1, source_target_pairs={{0,3},{1,67},{2,131},{3,195},{64,0},{65,64},{66,128},{67,192},{128... | collective-permute-start | bytes 49160 | tf_op jit(solution)/shard_map/direction/ppermute | solution.py:47
  98.0 23.3 %collective-permute-start.8 = (bf16[256,2048]{1,0:T(8,128)(2,1)}, bf16[256,2048]{1,0:T(8,128)(2,1)S(1)}, u32[]{:S(2)}, u32[]{:S(2)}) collective-permute-start(bf16[256,2048]{1,0:T(8,128)(2,1)} %collective-permute-done.7), channel_id=1, source_target_pairs={{0,64},{64,128},{128,192},{192,2},{2,66},{66,130},{130,194},{194,0... | collective-permute-start | bytes 3145736 | tf_op jit(solution)/shard_map/direction/ppermute | solution.py:40
  98.5 29.0 %collective-permute-start.9 = (bf16[256,2048]{1,0:T(8,128)(2,1)}, bf16[256,2048]{1,0:T(8,128)(2,1)S(1)}, u32[]{:S(2)}, u32[]{:S(2)}) collective-permute-start(bf16[256,2048]{1,0:T(8,128)(2,1)} %collective-permute-done.5), channel_id=1, source_target_pairs={{0,194},{64,0},{128,64},{192,128},{2,192},{66,2},{130,66},{194,130... | collective-permute-start | bytes 3145736 | tf_op jit(solution)/shard_map/direction/ppermute | solution.py:40
  129.7 1.7 collective-permute-start.14
  131.3 16.2 %collective-permute-start.10 = (bf16[256,2048]{1,0:T(8,128)(2,1)}, bf16[256,2048]{1,0:T(8,128)(2,1)S(1)}, u32[]{:S(2)}, u32[]{:S(2)}) collective-permute-start(bf16[256,2048]{1,0:T(8,128)(2,1)} %broadcast_select_fusion), channel_id=1, source_target_pairs={{0,64},{1,195},{64,128},{65,1},{128,192},{129,65},{192,2},{193,129... | collective-permute-start | bytes 3145736 | tf_op jit(solution)/shard_map/direction/ppermute | solution.py:123
  140.4 5.8 %collective-permute-start.13 = (f32[256,768]{1,0:T(8,128)S(1)}, f32[256,768]{1,0:T(8,128)S(1)}, u32[]{:S(2)}, u32[]{:S(2)}) collective-permute-start(f32[256,768]{1,0:T(8,128)S(1)} %get-tuple-element.76), channel_id=1, source_target_pairs={{0,1},{1,0},{2,3},{3,2},{4,5},{5,4},{6,7},{7,6},{8,9},{9,8},{10,11... | collective-permute-start | bytes 2359304 | tf_op jit(solution)/shard_map/project/ppermute | solution.py:60
  150.0 2.5 %collective-permute-start.15 = (f32[256,768]{1,0:T(8,128)}, f32[256,768]{1,0:T(8,128)S(1)}, u32[]{:S(2)}, u32[]{:S(2)}) collective-permute-start(f32[256,768]{1,0:T(8,128)} %get-tuple-element.74), channel_id=1, source_target_pairs={{0,1},{1,0},{2,3},{3,2},{4,5},{5,4},{6,7},{7,6},{8,9},{9,8},{10,11... | collective-permute-start | bytes 2359304 | tf_op jit(solution)/shard_map/project/ppermute | solution.py:60
  150.4 2.1 collective-permute-start.16
  152.5 35.4 %copy-start.10 = (f32[4,1,16,128]{3,2,1,0:T(8,128)S(1)}, f32[4,1,16,128]{3,2,1,0:T(8,128)}, u32[]{:S(2)}) copy-start(f32[4,1,16,128]{3,2,1,0:T(8,128)} %copy-done.9) | copy-start | bytes 98308
  153.9 9.0 %collective-permute-start.17 = (bf16[4,512]{1,0:T(4,128)(2,1)S(1)}, bf16[4,512]{1,0:T(4,128)(2,1)S(1)}, u32[]{:S(2)}, u32[]{:S(2)}) collective-permute-start(bf16[4,512]{1,0:T(4,128)(2,1)S(1)} %pad_maximum_fusion.16), channel_id=1, source_target_pairs={{0,0},{1,64},{64,128},{65,192},{128,1},{129,65},{192,129},{193,193... | collective-permute-start | bytes 12296 | tf_op jit(solution)/shard_map/tail/ppermute | solution.py:34
  156.5 6.4 %collective-permute-start.18 = (bf16[4,512]{1,0:T(4,128)(2,1)S(1)}, bf16[4,512]{1,0:T(4,128)(2,1)S(1)}, u32[]{:S(2)}, u32[]{:S(2)}) collective-permute-start(bf16[4,512]{1,0:T(4,128)(2,1)S(1)} %pad_maximum_fusion.16), channel_id=1, source_target_pairs={{0,64},{1,128},{64,192},{65,0},{128,65},{129,129},{192,193},{193,1... | collective-permute-start | bytes 12296 | tf_op jit(solution)/shard_map/tail/ppermute | solution.py:34
  160.4 4.9 %collective-permute-start.19 = (bf16[4,512]{1,0:T(4,128)(2,1)S(1)}, bf16[4,512]{1,0:T(4,128)(2,1)S(1)}, u32[]{:S(2)}, u32[]{:S(2)}) collective-permute-start(bf16[4,512]{1,0:T(4,128)(2,1)S(1)} %pad_maximum_fusion.16), channel_id=1, source_target_pairs={{0,128},{1,192},{64,0},{65,64},{128,129},{129,193},{192,1},{193,65... | collective-permute-start | bytes 12296 | tf_op jit(solution)/shard_map/tail/ppermute | solution.py:34
  160.5 5.3 %collective-permute-start.20 = (bf16[4,512]{1,0:T(4,128)(2,1)S(1)}, bf16[4,512]{1,0:T(4,128)(2,1)S(1)}, u32[]{:S(2)}, u32[]{:S(2)}) collective-permute-start(bf16[4,512]{1,0:T(4,128)(2,1)S(1)} %pad_maximum_fusion.16), channel_id=1, source_target_pairs={{0,192},{1,0},{64,64},{65,128},{128,193},{129,1},{192,65},{193,129... | collective-permute-start | bytes 12296 | tf_op jit(solution)/shard_map/tail/ppermute | solution.py:34
  176.7 9.2 %collective-permute-start.23 = (bf16[64,128]{1,0:T(8,128)(2,1)S(1)}, bf16[64,128]{1,0:T(8,128)(2,1)S(1)}, u32[]{:S(2)}, u32[]{:S(2)}) collective-permute-start(bf16[64,128]{1,0:T(8,128)(2,1)S(1)} %convolution_convert_fusion.1), channel_id=1, source_target_pairs={{0,1},{1,0},{2,3},{3,2},{4,5},{5,4},{6,7},{7,6},{8,9},{9,8},{10,11... | collective-permute-start | bytes 49160 | tf_op jit(solution)/shard_map/tail/ppermute | solution.py:54
  180.0 6.5 %collective-permute-start.24 = (bf16[64,128]{1,0:T(8,128)(2,1)S(1)}, bf16[64,128]{1,0:T(8,128)(2,1)S(1)}, u32[]{:S(2)}, u32[]{:S(2)}) collective-permute-start(bf16[64,128]{1,0:T(8,128)(2,1)S(1)} %convolution_convert_fusion.1), channel_id=1, source_target_pairs={{0,2},{1,3},{2,0},{3,1},{4,6},{5,7},{6,4},{7,5},{8,10},{9,11},{10,... | collective-permute-start | bytes 49160 | tf_op jit(solution)/shard_map/tail/ppermute | solution.py:54
  180.9 7.1 %collective-permute-start.25 = (bf16[64,128]{1,0:T(8,128)(2,1)S(1)}, bf16[64,128]{1,0:T(8,128)(2,1)S(1)}, u32[]{:S(2)}, u32[]{:S(2)}) collective-permute-start(bf16[64,128]{1,0:T(8,128)(2,1)S(1)} %convolution_convert_fusion.1), channel_id=1, source_target_pairs={{0,3},{1,2},{2,1},{3,0},{4,7},{5,6},{6,5},{7,4},{8,11},{9,10},{10,... | collective-permute-start | bytes 49160 | tf_op jit(solution)/shard_map/tail/ppermute | solution.py:54
  189.4 16.2 %all-to-all-start.2 = ((f32[64,1,128]{2,1,0:T(1,128)}), f32[64,1,128]{2,1,0:T(1,128)S(1)}, u32[]{:S(2)}, u32[]{:S(2)}) async-start(f32[64,1,128]{2,1,0:T(1,128)} %bitcast.31), calls=%async_computation.2 | async-start | bytes 65536 | tf_op jit(solution)/shard_map/tail/all_to_all | solution.py:279
  196.6 12.1 %collective-permute-start.21 = (bf16[256,512]{1,0:T(8,128)(2,1)S(1)}, bf16[256,512]{1,0:T(8,128)(2,1)S(1)}, u32[]{:S(2)}, u32[]{:S(2)}) collective-permute-start(bf16[256,512]{1,0:T(8,128)(2,1)S(1)} %get-tuple-element.66), channel_id=1, source_target_pairs={{0,0},{1,128},{64,64},{65,192},{128,129},{129,1},{192,193},{193,65... | collective-permute-start | bytes 786440 | tf_op jit(solution)/shard_map/tail/ppermute | solution.py:34
  201.3 9.8 %collective-permute-start.22 = (bf16[256,512]{1,0:T(8,128)(2,1)S(1)}, bf16[256,512]{1,0:T(8,128)(2,1)S(1)}, u32[]{:S(2)}, u32[]{:S(2)}) collective-permute-start(bf16[256,512]{1,0:T(8,128)(2,1)S(1)} %get-tuple-element.67), channel_id=1, source_target_pairs={{0,64},{1,192},{64,128},{65,0},{128,193},{129,65},{192,1},{193,129... | collective-permute-start | bytes 786440 | tf_op jit(solution)/shard_map/tail/ppermute | solution.py:34
  (12 other events, 132.6 us)
Sparse Core Ops, SparseCore 0:
  25.4 70.0 all-gather.1

commit v2 on v1

--- a/solution.py
+++ b/solution.py
@@ -123,16 +123,6 @@
     return lax.ppermute(value, ("zl", *MP), pairs)
 
 
-def to_line(value, zl):
-    got = []
-    for i in range(4):
-        got.append(send(value, lambda z, c: (2 * (z % 2) + c + i, z // 2)))
-    got = jnp.stack(got)
-    return jnp.stack(
-        [lax.dynamic_index_in_dim(got, (zl - q) % 4, 0, keepdims=False) for q in range(4)]
-    )
-
-
 def per_device(tokens, gain, w_query, w_key, w_value, w_out, final_gain, unembed, clean, corrupt):
     zh, zl, core = lax.axis_index("zh"), lax.axis_index("zl"), lax.axis_index("c")
     yx = lax.axis_index(("y", "x"))
@@ -172,20 +162,19 @@
         own_last = jnp.where(here, tokens[LENGTH - 1].reshape(1, 16, 1, 128), 0).astype(BF16)
         packed = jnp.concatenate([found, own_last], axis=2).reshape(64, 17, 128)
         packed = lax.all_to_all(packed, DP, 0, 0, tiled=True)
+        blocks = {0: tokens}
+        for r in (1, 2, 3):
+            for sign in (1, -1):
+                blocks[-sign * r] = along(blocks[-sign * (r - 1)], sign)
+            if r == 2:
+                packed, *_ = lax.optimization_barrier((packed, blocks[2], blocks[-2]))
         packed = packed.astype(F32)
         packed = jnp.sum(packed.reshape(4, 16, 17, 128), axis=0)
         gain_cols = lax.dynamic_slice_in_dim(final_gain, yx * 128, 128, 0).astype(F32)
         weighted = gain_cols * jnp.sum(packed[:, :16], axis=0)
         both = jnp.stack([weighted, packed[:, 16]])
         both = to_column_owners(both, zl, 2 * zh + core)
-        blocks = {0: tokens}
-        for r in (1, 2, 3):
-            for sign in (1, -1):
-                blocks[-sign * r] = along(blocks[-sign * (r - 1)], sign)
-            if r == 2:
-                both, blocks[2], blocks[-2] = lax.optimization_barrier(
-                    (both, blocks[2], blocks[-2])
-                )
+        both, blocks[3], blocks[-3] = lax.optimization_barrier((both, blocks[3], blocks[-3]))
         blocks[4] = last_hop(jnp.where(first, blocks[-3], blocks[3]))
         weighted_cols = both[:, 0].reshape(64, 128)
         token_cols = both[:, 1].reshape(64, 128)
@@ -243,7 +232,8 @@
         line = jnp.concatenate(
             [mixed_0[-1:], mixed_1[-1:], high.astype(BF16), (total - high).astype(BF16)], axis=0
         )
-        every = from_everyone(to_line(line, zl), ("y", "x"))
+        line = lax.dynamic_slice_in_dim(from_everyone(line, ("zl", "c")), 4 * core, 4, 0)
+        every = from_everyone(line, ("y", "x"))
         every, mixed_0, mixed_1 = lax.optimization_barrier((every, mixed_0, mixed_1))
         head_out = owned(mixed_0, mixed_1)
         every = every.reshape(16, 2, 2, 4, width)

time: 221 us -> 209 us (0.946)
  starting transfers between devices: 72.9 us -> 60.9 us
  waiting for transfers between devices: 73.2 us -> 69.1 us
  blocking collectives: 10.1 us -> 14.1 us
    all_to_all x1, waiting for transfers between devices: 17.4 us -> 0.93 us  [per_device(): packed = lax.all_to_all(packed, DP, 0, 0, tiled=True)]
    ppermute x8 -> x4, starting transfers between devices: 22.4 us -> 13.1 us  [send(): return lax.ppermute(value, ('zl', 'c'), pairs)]
    ppermute x6, waiting for transfers between devices: 18.4 us -> 26.7 us  [along(): return lax.ppermute(value, ('zl', 'zh'), pairs)]
    all_to_all x0 -> x1, starting transfers between devices: none -> 6.23 us  [from_everyone(): lax.all_to_all(jnp.broadcast_to(value[None], (count, *value.shape)), axis...]
    all_to_all x0 -> x1, waiting for transfers between devices: none -> 4.97 us  [from_everyone(): lax.all_to_all(jnp.broadcast_to(value[None], (count, *value.shape)), axis...]
    ppermute x4, starting transfers between devices: 12.2 us -> 7.75 us  [to_column_owners(): got.append(lax.ppermute(value, ('zl', *MP), pairs))]
    all_to_all x1, blocking collectives: 10.1 us -> 14.1 us  [from_everyone(): lax.all_to_all(jnp.broadcast_to(value[None], (count, *value.shape)), axis...]
    ppermute x8 -> x4, waiting for transfers between devices: 13.4 us -> 9.96 us  [send(): return lax.ppermute(value, ('zl', 'c'), pairs)]
  transfers between devices with their start and end apart: 29 -> 26, of which waited for: 15 -> 15; matrix products, arithmetic and copies ran while one was open for 15% -> 16% of each run, Pallas kernels for 1% -> 1%
where the time goes in v2:
time: 209 us; the launch traced here: 208 us
  waiting for transfers between devices  69.1 us (33%)
  starting transfers between devices  60.9 us (29%)
  other arithmetic  23.1 us (11%)
  between operations  17.7 us (8%)
  matrix products  16 us (8%)
  blocking collectives  14.1 us (7%)
  local copies, waits for them, and re-layouts  4.71 us (2%)
  Pallas kernels  2.63 us (1%)
    ppermute x6, waiting for transfers between devices, along(): return lax.ppermute(value, ('zl', 'zh'), pairs)  26.7 us
    ppermute x4, waiting for transfers between devices, to_column_owners(): got.append(lax.ppermute(value, ('zl', *MP), pairs))  17.9 us
    all_to_all x1, blocking collectives, from_everyone(): lax.all_to_all(jnp.broadcast_to(value[None], (count, *value.shape)), axis...  14.1 us
    reduce_sum x7, other arithmetic, scaled(): done = ((t * g).astype(BF16), jnp.sum(t * t, axis=1, keepdims=True))  13.7 us
    ppermute x4, starting transfers between devices, send(): return lax.ppermute(value, ('zl', 'c'), pairs)  13.1 us
    dot_general x8, matrix products, project(): return (jnp.dot(block, weight, preferred_element_type=F32), square)  12.3 us
    ppermute x6, starting transfers between devices, along(): return lax.ppermute(value, ('zl', 'zh'), pairs)  10.1 us
    ppermute x4, waiting for transfers between devices, send(): return lax.ppermute(value, ('zl', 'c'), pairs)  9.96 us
  transfers between devices with their start and end apart: 26, of which 15 were waited for; matrix products, arithmetic and copies ran while one was open for 16% of the time, Pallas kernels for 1%

profile of v2, /device:TPU:1, one launch (start us, length us, event | category | flops | bytes accessed | tf_op | source)
XLA Modules:
  0.0 208.2 jit_solution(7141717934395762902)
XLA Ops:
  9.2 6.3 %collective-permute-start.11 = (bf16[128,768]{1,0:T(8,128)(2,1)S(1)}, bf16[128,768]{1,0:T(8,128)(2,1)S(1)}, u32[]{:S(2)}, u32[]{:S(2)}) collective-permute-start(bf16[128,768]{1,0:T(8,128)(2,1)S(1)} %get-tuple-element.112), channel_id=1, source_target_pairs={{0,0},{1,128},{64,1},{65,129},{128,64},{129,192},{192,65},{193,193... | collective-permute-start | bytes 589832 | tf_op jit(solution)/shard_map/weights/ppermute | solution.py:34
  16.9 2.6 %collective-permute-done.11 = bf16[128,768]{1,0:T(8,128)(2,1)S(1)} collective-permute-done((bf16[128,768]{1,0:T(8,128)(2,1)S(1)}, bf16[128,768]{1,0:T(8,128)(2,1)S(1)}, u32[]{:S(2)}, u32[]{:S(2)}) %collective-permute-start.11) | collective-permute-done | bytes 196640 | tf_op jit(solution)/shard_map/weights/ppermute | solution.py:34
  19.5 4.9 %collective-permute-done.12 = bf16[128,768]{1,0:T(8,128)(2,1)S(1)} collective-permute-done((bf16[128,768]{1,0:T(8,128)(2,1)S(1)}, bf16[128,768]{1,0:T(8,128)(2,1)S(1)}, u32[]{:S(2)}, u32[]{:S(2)}) %collective-permute-start.12) | collective-permute-done | bytes 196640 | tf_op jit(solution)/shard_map/weights/ppermute | solution.py:34
  25.3 4.4 %collective-permute-start = (bf16[256,2048]{1,0:T(8,128)(2,1)S(1)}, bf16[256,2048]{1,0:T(8,128)(2,1)S(1)}, u32[]{:S(2)}, u32[]{:S(2)}) collective-permute-start(bf16[256,2048]{1,0:T(8,128)(2,1)S(1)} %copy-done.3), channel_id=1, source_target_pairs={{0,194},{64,0},{128,64},{192,128},{2,192},{66,2},{130,66},{194,130... | collective-permute-start | bytes 3145736 | tf_op jit(solution)/shard_map/direction/ppermute | solution.py:40
  29.9 3.1 %fusion.41 = bf16[8,8,16,128]{3,1,2,0:T(8,128)(2,1)S(1)} fusion(bf16[1002,2048]{1,0:T(8,128)(2,1)} %param.17, s32[1002]{0:T(1024)S(1)} %iota_add_fusion, s32[64]{0:T(128)S(1)} %copy-done.10, s32[64]{0:T(128)S(1)} %copy-done.11), kind=kOutput, calls=%fused_computation.52 | convolution fusion | flops 263184128 | bytes 4370856 | tf_op jit(solution)/shard_map/direction/dot_general | solution.py:159
  34.1 8.5 %all-to-all-start = ((bf16[64,17,128]{2,1,0:T(8,128)(2,1)}), bf16[64,17,128]{2,1,0:T(8,128)(2,1)S(1)}, u32[]{:S(2)}, u32[]{:S(2)}) async-start(bf16[64,17,128]{2,1,0:T(8,128)(2,1)} %pad_maximum_fusion.1), calls=%async_computation | async-start | bytes 786432 | tf_op jit(solution)/shard_map/direction/all_to_all | solution.py:164
  44.2 8.0 %collective-permute-done = bf16[256,2048]{1,0:T(8,128)(2,1)S(1)} collective-permute-done((bf16[256,2048]{1,0:T(8,128)(2,1)S(1)}, bf16[256,2048]{1,0:T(8,128)(2,1)S(1)}, u32[]{:S(2)}, u32[]{:S(2)}) %collective-permute-start) | collective-permute-done | bytes 1048608 | tf_op jit(solution)/shard_map/direction/ppermute | solution.py:40
  52.2 3.5 %collective-permute-start.1 = (bf16[256,2048]{1,0:T(8,128)(2,1)S(1)}, bf16[256,2048]{1,0:T(8,128)(2,1)}, u32[]{:S(2)}, u32[]{:S(2)}) collective-permute-start(bf16[256,2048]{1,0:T(8,128)(2,1)S(1)} %collective-permute-done), channel_id=1, source_target_pairs={{0,194},{64,0},{128,64},{192,128},{2,192},{66,2},{130,66},{194,130... | collective-permute-start | bytes 3145736 | tf_op jit(solution)/shard_map/direction/ppermute | solution.py:40
  58.7 2.6 %fusion.27 = (f32[256]{0:T(256)S(1)}, bf16[256,2048]{1,0:T(8,128)(2,1)}) fusion(bf16[256,2048]{1,0:T(8,128)(2,1)} %collective-permute-done.2, f32[2048]{0:T(1024)S(1)} %get-tuple-element.119), kind=kLoop, calls=%fused_computation.44 | loop fusion | flops 2621184 | bytes 2106368 | tf_op jit(solution)/shard_map/project/reduce_sum | solution.py:192
  62.5 16.2 %collective-permute-done.1 = bf16[256,2048]{1,0:T(8,128)(2,1)} collective-permute-done((bf16[256,2048]{1,0:T(8,128)(2,1)S(1)}, bf16[256,2048]{1,0:T(8,128)(2,1)}, u32[]{:S(2)}, u32[]{:S(2)}) %collective-permute-start.1) | collective-permute-done | bytes 1048608 | tf_op jit(solution)/shard_map/direction/ppermute | solution.py:40
  78.7 2.5 %collective-permute-done.3 = bf16[256,2048]{1,0:T(8,128)(2,1)} collective-permute-done((bf16[256,2048]{1,0:T(8,128)(2,1)}, bf16[256,2048]{1,0:T(8,128)(2,1)}, u32[]{:S(2)}, u32[]{:S(2)}) %collective-permute-start.3) | collective-permute-done | bytes 1048608 | tf_op jit(solution)/shard_map/direction/ppermute | solution.py:40
  81.5 1.8 collective-permute-start.9
  83.4 2.4 %collective-permute-start.7 = (f32[2,16,128]{2,1,0:T(8,128)S(1)}, f32[2,16,128]{2,1,0:T(8,128)S(1)}, u32[]{:S(2)}, u32[]{:S(2)}) collective-permute-start(f32[2,16,128]{2,1,0:T(8,128)S(1)} %pad_maximum_fusion.13), channel_id=1, source_target_pairs={{0,3},{1,67},{2,131},{3,195},{64,0},{65,64},{66,128},{67,192},{128... | collective-permute-start | bytes 49160 | tf_op jit(solution)/shard_map/direction/ppermute | solution.py:47
  85.8 3.4 %collective-permute-start.6 = (f32[2,16,128]{2,1,0:T(8,128)S(1)}, f32[2,16,128]{2,1,0:T(8,128)S(1)}, u32[]{:S(2)}, u32[]{:S(2)}) collective-permute-start(f32[2,16,128]{2,1,0:T(8,128)S(1)} %pad_maximum_fusion.13), channel_id=1, source_target_pairs={{0,2},{1,66},{2,130},{3,194},{64,3},{65,67},{66,131},{67,195},{128... | collective-permute-start | bytes 49160 | tf_op jit(solution)/shard_map/direction/ppermute | solution.py:47
  89.3 2.5 %fusion.21 = (f32[256]{0:T(256)S(1)}, bf16[256,2048]{1,0:T(8,128)(2,1)}) fusion(bf16[256,2048]{1,0:T(8,128)(2,1)} %collective-permute-done.3, f32[2048]{0:T(1024)S(1)} %get-tuple-element.122), kind=kLoop, calls=%fused_computation.38 | loop fusion | flops 2621184 | bytes 2106368 | tf_op jit(solution)/shard_map/project/reduce_sum | solution.py:192
  91.8 17.6 %collective-permute-done.7 = f32[2,16,128]{2,1,0:T(8,128)S(1)} collective-permute-done((f32[2,16,128]{2,1,0:T(8,128)S(1)}, f32[2,16,128]{2,1,0:T(8,128)S(1)}, u32[]{:S(2)}, u32[]{:S(2)}) %collective-permute-start.7) | collective-permute-done | bytes 16416 | tf_op jit(solution)/shard_map/direction/ppermute | solution.py:47
  109.4 1.9 collective-permute-start.4
  111.3 2.5 %fusion.19 = (f32[256]{0:T(256)S(1)}, bf16[256,2048]{1,0:T(8,128)(2,1)}) fusion(bf16[256,2048]{1,0:T(8,128)(2,1)} %collective-permute-done.1, f32[2048]{0:T(1024)S(1)} %get-tuple-element.123), kind=kLoop, calls=%fused_computation.36 | loop fusion | flops 2621184 | bytes 2106368 | tf_op jit(solution)/shard_map/project/reduce_sum | solution.py:192
  115.6 1.9 fusion.25
  117.8 1.9 collective-permute-start.14
  120.8 3.3 %fusion.6 = f32[256,768]{1,0:T(8,128)S(1)} fusion(bf16[256,2048]{1,0:T(8,128)(2,1)} %get-tuple-element.48, bf16[2048,1536]{1,0:T(8,128)(2,1)} %all-gather.2.cloned.1.call-done, s32[]{:T(128)S(6)} %select_n.293), kind=kOutput, calls=%fused_computation.6 | convolution fusion | flops 805306368 | bytes 4980740 | tf_op jit(solution)/shard_map/project/dot_general | solution.py:197
  124.2 3.0 %fusion.2 = f32[256,768]{1,0:T(8,128)S(1)} fusion(bf16[256,2048]{1,0:T(8,128)(2,1)S(1)} %copy-done.8, bf16[2048,1536]{1,0:T(8,128)(2,1)} %all-gather.2.cloned.1.call-done, s32[]{:T(128)S(6)} %select_n.301), kind=kOutput, calls=%fused_computation.2 | convolution fusion | flops 805306368 | bytes 4980740 | tf_op jit(solution)/shard_map/project/dot_general | solution.py:197
  142.7 6.2 %all-to-all-start.1 = ((bf16[8,4,512]{2,1,0:T(4,128)(2,1)}), bf16[8,4,512]{2,1,0:T(4,128)(2,1)S(1)}, u32[]{:S(2)}, u32[]{:S(2)}) async-start(bf16[8,4,512]{2,1,0:T(4,128)(2,1)} %broadcast_in_dim.113), calls=%async_computation.1 | async-start | bytes 65536 | tf_op jit(solution)/shard_map/tail/all_to_all | solution.py:23
  148.9 5.0 %all-to-all-done.1 = bf16[8,4,512]{2,1,0:T(4,128)(2,1)S(1)} async-done(((bf16[8,4,512]{2,1,0:T(4,128)(2,1)}), bf16[8,4,512]{2,1,0:T(4,128)(2,1)S(1)}, u32[]{:S(2)}, u32[]{:S(2)}) %all-to-all-start.1) | async-done | bytes 32800 | tf_op jit(solution)/shard_map/tail/all_to_all | solution.py:23
  154.0 14.1 %all_to_all.20 = bf16[16,4,4,512]{3,2,1,0:T(4,128)(2,1)S(1)} all-to-all(bf16[16,4,4,512]{3,2,1,0:T(4,128)(2,1)S(1)} %broadcast_in_dim.114), channel_id=1, replica_groups=mesh['zl'=4,'y'=4,'x'=4,'zh'=2,'c'=2] {'y','x'}, dimensions={0} | all-to-all | bytes 524288 | tf_op jit(solution)/shard_map/tail/all_to_all | solution.py:23
  168.5 4.2 %collective-permute-start.21 = (bf16[64,128]{1,0:T(8,128)(2,1)S(1)}, bf16[64,128]{1,0:T(8,128)(2,1)S(1)}, u32[]{:S(2)}, u32[]{:S(2)}) collective-permute-start(bf16[64,128]{1,0:T(8,128)(2,1)S(1)} %convolution_convert_fusion.1), channel_id=1, source_target_pairs={{0,3},{1,2},{2,1},{3,0},{4,7},{5,6},{6,5},{7,4},{8,11},{9,10},{10,... | collective-permute-start | bytes 49160 | tf_op jit(solution)/shard_map/tail/ppermute | solution.py:54
  172.8 3.3 %collective-permute-start.20 = (bf16[64,128]{1,0:T(8,128)(2,1)S(1)}, bf16[64,128]{1,0:T(8,128)(2,1)S(1)}, u32[]{:S(2)}, u32[]{:S(2)}) collective-permute-start(bf16[64,128]{1,0:T(8,128)(2,1)S(1)} %convolution_convert_fusion.1), channel_id=1, source_target_pairs={{0,2},{1,3},{2,0},{3,1},{4,6},{5,7},{6,4},{7,5},{8,10},{9,11},{10,... | collective-permute-start | bytes 49160 | tf_op jit(solution)/shard_map/tail/ppermute | solution.py:54
  176.6 2.8 %collective-permute-done.20 = bf16[64,128]{1,0:T(8,128)(2,1)S(1)} collective-permute-done((bf16[64,128]{1,0:T(8,128)(2,1)S(1)}, bf16[64,128]{1,0:T(8,128)(2,1)S(1)}, u32[]{:S(2)}, u32[]{:S(2)}) %collective-permute-start.20) | collective-permute-done | bytes 16416 | tf_op jit(solution)/shard_map/tail/ppermute | solution.py:54
  180.8 4.6 %all-to-all-start.3 = ((f32[64,1,128]{2,1,0:T(1,128)}), f32[64,1,128]{2,1,0:T(1,128)S(1)}, u32[]{:S(2)}, u32[]{:S(2)}) async-start(f32[64,1,128]{2,1,0:T(1,128)} %bitcast.27), calls=%async_computation.3 | async-start | bytes 65536 | tf_op jit(solution)/shard_map/tail/all_to_all | solution.py:269
  185.4 3.4 %collective-permute-start.17 = (bf16[256,512]{1,0:T(8,128)(2,1)S(1)}, bf16[256,512]{1,0:T(8,128)(2,1)S(1)}, u32[]{:S(2)}, u32[]{:S(2)}) collective-permute-start(bf16[256,512]{1,0:T(8,128)(2,1)S(1)} %get-tuple-element.68), channel_id=1, source_target_pairs={{0,0},{1,128},{64,64},{65,192},{128,129},{129,1},{192,193},{193,65... | collective-permute-start | bytes 786440 | tf_op jit(solution)/shard_map/tail/ppermute | solution.py:34
  188.8 2.0 collective-permute-start.18
  190.8 3.5 %all-to-all-done.3 = f32[64,1,128]{2,1,0:T(1,128)S(1)} async-done(((f32[64,1,128]{2,1,0:T(1,128)}), f32[64,1,128]{2,1,0:T(1,128)S(1)}, u32[]{:S(2)}, u32[]{:S(2)}) %all-to-all-start.3) | async-done | bytes 32800 | tf_op jit(solution)/shard_map/tail/all_to_all | solution.py:269
  (144 shorter events, 36.5 us)
Async XLA Ops:
  7.2 112.6 %copy-start = (bf16[1024,128]{1,0:T(8,128)(2,1)S(1)}, bf16[1024,128]{1,0:T(8,128)(2,1)}, u32[]{:S(2)}) copy-start(bf16[1024,128]{1,0:T(8,128)(2,1)} %param.15) | copy-start | bytes 786436
  7.2 18.1 %copy-start.3 = (bf16[256,2048]{1,0:T(8,128)(2,1)S(1)}, bf16[256,2048]{1,0:T(8,128)(2,1)}, u32[]{:S(2)}) copy-start(bf16[256,2048]{1,0:T(8,128)(2,1)} %param.10) | copy-start | bytes 3145732
  7.2 22.7 %copy-start.10 = (s32[64]{0:T(128)S(1)}, s32[64]{0:T(128)}, u32[]{:S(2)}) copy-start(s32[64]{0:T(128)} %param.19) | copy-start | bytes 772
  7.2 22.7 %copy-start.11 = (s32[64]{0:T(128)S(1)}, s32[64]{0:T(128)}, u32[]{:S(2)}) copy-start(s32[64]{0:T(128)} %param.18) | copy-start | bytes 772
  7.2 113.6 %all-gather.2.cloned.1.call-start = ((), (), s32[]{:S(2)}) async-start(), calls=%async_computation.4 | async-start | bytes 6684672 | tf_op jit(solution)/shard_map/weights/all_gather | solution.py:151
  9.2 10.3 %collective-permute-start.11 = (bf16[128,768]{1,0:T(8,128)(2,1)S(1)}, bf16[128,768]{1,0:T(8,128)(2,1)S(1)}, u32[]{:S(2)}, u32[]{:S(2)}) collective-permute-start(bf16[128,768]{1,0:T(8,128)(2,1)S(1)} %get-tuple-element.112), channel_id=1, source_target_pairs={{0,0},{1,128},{64,1},{65,129},{128,64},{129,192},{192,65},{193,193... | collective-permute-start | bytes 589832 | tf_op jit(solution)/shard_map/weights/ppermute | solution.py:34
  15.5 9.0 %collective-permute-start.12 = (bf16[128,768]{1,0:T(8,128)(2,1)S(1)}, bf16[128,768]{1,0:T(8,128)(2,1)S(1)}, u32[]{:S(2)}, u32[]{:S(2)}) collective-permute-start(bf16[128,768]{1,0:T(8,128)(2,1)S(1)} %get-tuple-element.113), channel_id=1, source_target_pairs={{0,64},{1,192},{64,65},{65,193},{128,0},{129,128},{192,1},{193,129... | collective-permute-start | bytes 589832 | tf_op jit(solution)/shard_map/weights/ppermute | solution.py:34
  25.3 26.9 %collective-permute-start = (bf16[256,2048]{1,0:T(8,128)(2,1)S(1)}, bf16[256,2048]{1,0:T(8,128)(2,1)S(1)}, u32[]{:S(2)}, u32[]{:S(2)}) collective-permute-start(bf16[256,2048]{1,0:T(8,128)(2,1)S(1)} %copy-done.3), channel_id=1, source_target_pairs={{0,194},{64,0},{128,64},{192,128},{2,192},{66,2},{130,66},{194,130... | collective-permute-start | bytes 3145736 | tf_op jit(solution)/shard_map/direction/ppermute | solution.py:40
  29.7 26.1 %collective-permute-start.2 = (bf16[256,2048]{1,0:T(8,128)(2,1)S(1)}, bf16[256,2048]{1,0:T(8,128)(2,1)}, u32[]{:S(2)}, u32[]{:S(2)}) collective-permute-start(bf16[256,2048]{1,0:T(8,128)(2,1)S(1)} %copy-done.3), channel_id=1, source_target_pairs={{0,64},{64,128},{128,192},{192,2},{2,66},{66,130},{130,194},{194,0... | collective-permute-start | bytes 3145736 | tf_op jit(solution)/shard_map/direction/ppermute | solution.py:40
  29.9 13.0 %copy-start.9 = (bf16[8192]{0:T(1024)(128)(2,1)S(1)}, bf16[8192]{0:T(1024)(128)(2,1)}, u32[]{:S(2)}) copy-start(bf16[8192]{0:T(1024)(128)(2,1)} %param.11) | copy-start | bytes 49156
  34.1 28.4 %all-to-all-start = ((bf16[64,17,128]{2,1,0:T(8,128)(2,1)}), bf16[64,17,128]{2,1,0:T(8,128)(2,1)S(1)}, u32[]{:S(2)}, u32[]{:S(2)}) async-start(bf16[64,17,128]{2,1,0:T(8,128)(2,1)} %pad_maximum_fusion.1), calls=%async_computation | async-start | bytes 786432 | tf_op jit(solution)/shard_map/direction/all_to_all | solution.py:164
  52.2 26.4 %collective-permute-start.1 = (bf16[256,2048]{1,0:T(8,128)(2,1)S(1)}, bf16[256,2048]{1,0:T(8,128)(2,1)}, u32[]{:S(2)}, u32[]{:S(2)}) collective-permute-start(bf16[256,2048]{1,0:T(8,128)(2,1)S(1)} %collective-permute-done), channel_id=1, source_target_pairs={{0,194},{64,0},{128,64},{192,128},{2,192},{66,2},{130,66},{194,130... | collective-permute-start | bytes 3145736 | tf_op jit(solution)/shard_map/direction/ppermute | solution.py:40
  55.7 25.4 %collective-permute-start.3 = (bf16[256,2048]{1,0:T(8,128)(2,1)}, bf16[256,2048]{1,0:T(8,128)(2,1)}, u32[]{:S(2)}, u32[]{:S(2)}) collective-permute-start(bf16[256,2048]{1,0:T(8,128)(2,1)} %collective-permute-done.2), channel_id=1, source_target_pairs={{0,64},{64,128},{128,192},{192,2},{2,66},{66,130},{130,194},{194,0... | collective-permute-start | bytes 3145736 | tf_op jit(solution)/shard_map/direction/ppermute | solution.py:40
  81.1 33.3 %collective-permute-start.8 = (bf16[256,2048]{1,0:T(8,128)(2,1)}, bf16[256,2048]{1,0:T(8,128)(2,1)S(1)}, u32[]{:S(2)}, u32[]{:S(2)}) collective-permute-start(bf16[256,2048]{1,0:T(8,128)(2,1)} %collective-permute-done.1), channel_id=1, source_target_pairs={{0,194},{64,0},{128,64},{192,128},{2,192},{66,2},{130,66},{194,130... | collective-permute-start | bytes 3145736 | tf_op jit(solution)/shard_map/direction/ppermute | solution.py:40
  81.5 32.9 %collective-permute-start.9 = (bf16[256,2048]{1,0:T(8,128)(2,1)}, bf16[256,2048]{1,0:T(8,128)(2,1)S(1)}, u32[]{:S(2)}, u32[]{:S(2)}) collective-permute-start(bf16[256,2048]{1,0:T(8,128)(2,1)} %collective-permute-done.3), channel_id=1, source_target_pairs={{0,64},{64,128},{128,192},{192,2},{2,66},{66,130},{130,194},{194,0... | collective-permute-start | bytes 3145736 | tf_op jit(solution)/shard_map/direction/ppermute | solution.py:40
  83.4 25.9 %collective-permute-start.7 = (f32[2,16,128]{2,1,0:T(8,128)S(1)}, f32[2,16,128]{2,1,0:T(8,128)S(1)}, u32[]{:S(2)}, u32[]{:S(2)}) collective-permute-start(f32[2,16,128]{2,1,0:T(8,128)S(1)} %pad_maximum_fusion.13), channel_id=1, source_target_pairs={{0,3},{1,67},{2,131},{3,195},{64,0},{65,64},{66,128},{67,192},{128... | collective-permute-start | bytes 49160 | tf_op jit(solution)/shard_map/direction/ppermute | solution.py:47
  85.8 28.2 %collective-permute-start.6 = (f32[2,16,128]{2,1,0:T(8,128)S(1)}, f32[2,16,128]{2,1,0:T(8,128)S(1)}, u32[]{:S(2)}, u32[]{:S(2)}) collective-permute-start(f32[2,16,128]{2,1,0:T(8,128)S(1)} %pad_maximum_fusion.13), channel_id=1, source_target_pairs={{0,2},{1,66},{2,130},{3,194},{64,3},{65,67},{66,131},{67,195},{128... | collective-permute-start | bytes 49160 | tf_op jit(solution)/shard_map/direction/ppermute | solution.py:47
  89.3 24.8 %collective-permute-start.5 = (f32[2,16,128]{2,1,0:T(8,128)S(1)}, f32[2,16,128]{2,1,0:T(8,128)S(1)}, u32[]{:S(2)}, u32[]{:S(2)}) collective-permute-start(f32[2,16,128]{2,1,0:T(8,128)S(1)} %pad_maximum_fusion.13), channel_id=1, source_target_pairs={{0,1},{1,65},{2,129},{3,193},{64,2},{65,66},{66,130},{67,194},{128... | collective-permute-start | bytes 49160 | tf_op jit(solution)/shard_map/direction/ppermute | solution.py:47
  109.4 5.0 %collective-permute-start.4 = (f32[2,16,128]{2,1,0:T(8,128)S(1)}, f32[2,16,128]{2,1,0:T(8,128)S(1)}, u32[]{:S(2)}, u32[]{:S(2)}) collective-permute-start(f32[2,16,128]{2,1,0:T(8,128)S(1)} %pad_maximum_fusion.13), channel_id=1, source_target_pairs={{0,0},{1,64},{2,128},{3,192},{64,1},{65,65},{66,129},{67,193},{128... | collective-permute-start | bytes 49160 | tf_op jit(solution)/shard_map/direction/ppermute | solution.py:47
  115.6 18.9 %collective-permute-start.10 = (bf16[256,2048]{1,0:T(8,128)(2,1)}, bf16[256,2048]{1,0:T(8,128)(2,1)}, u32[]{:S(2)}, u32[]{:S(2)}) collective-permute-start(bf16[256,2048]{1,0:T(8,128)(2,1)} %broadcast_select_fusion), channel_id=1, source_target_pairs={{0,64},{1,195},{64,128},{65,1},{128,192},{129,65},{192,2},{193,129... | collective-permute-start | bytes 3145736 | tf_op jit(solution)/shard_map/direction/ppermute | solution.py:123
  117.8 2.9 %collective-permute-start.14 = (f32[256,1]{1,0:T(8,128)S(1)}, f32[256,1]{1,0:T(8,128)S(1)}, u32[]{:S(2)}, u32[]{:S(2)}) collective-permute-start(f32[256,1]{1,0:T(8,128)S(1)} %broadcast_select_fusion.11), channel_id=1, source_target_pairs={{0,1},{1,0},{2,3},{3,2},{4,5},{5,4},{6,7},{7,6},{8,9},{9,8},{10,11... | collective-permute-start | bytes 3080 | tf_op jit(solution)/shard_map/project/ppermute | solution.py:60
  120.8 6.3 %copy-start.2 = (bf16[2048,1536]{1,0:T(8,128)(2,1)S(1)}, bf16[2048,1536]{1,0:T(8,128)(2,1)}, u32[]{:S(2)}) copy-start(bf16[2048,1536]{1,0:T(8,128)(2,1)} %all-gather.2.cloned.1.call-done) | copy-start | bytes 18874372
  129.5 3.7 %collective-permute-start.13 = (f32[256,768]{1,0:T(8,128)S(1)}, f32[256,768]{1,0:T(8,128)S(1)}, u32[]{:S(2)}, u32[]{:S(2)}) collective-permute-start(f32[256,768]{1,0:T(8,128)S(1)} %get-tuple-element.78), channel_id=1, source_target_pairs={{0,1},{1,0},{2,3},{3,2},{4,5},{5,4},{6,7},{7,6},{8,9},{9,8},{10,11... | collective-permute-start | bytes 2359304 | tf_op jit(solution)/shard_map/project/ppermute | solution.py:60
  138.1 2.5 %collective-permute-start.15 = (f32[256,768]{1,0:T(8,128)}, f32[256,768]{1,0:T(8,128)S(1)}, u32[]{:S(2)}, u32[]{:S(2)}) collective-permute-start(f32[256,768]{1,0:T(8,128)} %get-tuple-element.76), channel_id=1, source_target_pairs={{0,1},{1,0},{2,3},{3,2},{4,5},{5,4},{6,7},{7,6},{8,9},{9,8},{10,11... | collective-permute-start | bytes 2359304 | tf_op jit(solution)/shard_map/project/ppermute | solution.py:60
  138.6 2.0 collective-permute-start.16
  142.7 11.2 %all-to-all-start.1 = ((bf16[8,4,512]{2,1,0:T(4,128)(2,1)}), bf16[8,4,512]{2,1,0:T(4,128)(2,1)S(1)}, u32[]{:S(2)}, u32[]{:S(2)}) async-start(bf16[8,4,512]{2,1,0:T(4,128)(2,1)} %broadcast_in_dim.113), calls=%async_computation.1 | async-start | bytes 65536 | tf_op jit(solution)/shard_map/tail/all_to_all | solution.py:23
  168.5 8.0 %collective-permute-start.21 = (bf16[64,128]{1,0:T(8,128)(2,1)S(1)}, bf16[64,128]{1,0:T(8,128)(2,1)S(1)}, u32[]{:S(2)}, u32[]{:S(2)}) collective-permute-start(bf16[64,128]{1,0:T(8,128)(2,1)S(1)} %convolution_convert_fusion.1), channel_id=1, source_target_pairs={{0,3},{1,2},{2,1},{3,0},{4,7},{5,6},{6,5},{7,4},{8,11},{9,10},{10,... | collective-permute-start | bytes 49160 | tf_op jit(solution)/shard_map/tail/ppermute | solution.py:54
  172.8 6.6 %collective-permute-start.20 = (bf16[64,128]{1,0:T(8,128)(2,1)S(1)}, bf16[64,128]{1,0:T(8,128)(2,1)S(1)}, u32[]{:S(2)}, u32[]{:S(2)}) collective-permute-start(bf16[64,128]{1,0:T(8,128)(2,1)S(1)} %convolution_convert_fusion.1), channel_id=1, source_target_pairs={{0,2},{1,3},{2,0},{3,1},{4,6},{5,7},{6,4},{7,5},{8,10},{9,11},{10,... | collective-permute-start | bytes 49160 | tf_op jit(solution)/shard_map/tail/ppermute | solution.py:54
  176.1 3.3 %collective-permute-start.19 = (bf16[64,128]{1,0:T(8,128)(2,1)S(1)}, bf16[64,128]{1,0:T(8,128)(2,1)S(1)}, u32[]{:S(2)}, u32[]{:S(2)}) collective-permute-start(bf16[64,128]{1,0:T(8,128)(2,1)S(1)} %convolution_convert_fusion.1), channel_id=1, source_target_pairs={{0,1},{1,0},{2,3},{3,2},{4,5},{5,4},{6,7},{7,6},{8,9},{9,8},{10,11... | collective-permute-start | bytes 49160 | tf_op jit(solution)/shard_map/tail/ppermute | solution.py:54
  180.8 13.5 %all-to-all-start.3 = ((f32[64,1,128]{2,1,0:T(1,128)}), f32[64,1,128]{2,1,0:T(1,128)S(1)}, u32[]{:S(2)}, u32[]{:S(2)}) async-start(f32[64,1,128]{2,1,0:T(1,128)} %bitcast.27), calls=%async_computation.3 | async-start | bytes 65536 | tf_op jit(solution)/shard_map/tail/all_to_all | solution.py:269
  185.4 13.3 %collective-permute-start.17 = (bf16[256,512]{1,0:T(8,128)(2,1)S(1)}, bf16[256,512]{1,0:T(8,128)(2,1)S(1)}, u32[]{:S(2)}, u32[]{:S(2)}) collective-permute-start(bf16[256,512]{1,0:T(8,128)(2,1)S(1)} %get-tuple-element.68), channel_id=1, source_target_pairs={{0,0},{1,128},{64,64},{65,192},{128,129},{129,1},{192,193},{193,65... | collective-permute-start | bytes 786440 | tf_op jit(solution)/shard_map/tail/ppermute | solution.py:34
  188.8 10.5 %collective-permute-start.18 = (bf16[256,512]{1,0:T(8,128)(2,1)S(1)}, bf16[256,512]{1,0:T(8,128)(2,1)S(1)}, u32[]{:S(2)}, u32[]{:S(2)}) collective-permute-start(bf16[256,512]{1,0:T(8,128)(2,1)S(1)} %get-tuple-element.69), channel_id=1, source_target_pairs={{0,64},{1,192},{64,128},{65,0},{128,193},{129,65},{192,1},{193,129... | collective-permute-start | bytes 786440 | tf_op jit(solution)/shard_map/tail/ppermute | solution.py:34
  (6 other events, 12.6 us)
Sparse Core Ops, SparseCore 0:
  25.4 70.3 all-gather.1

commit v3 on v2

--- a/solution.py
+++ b/solution.py
@@ -173,12 +173,8 @@
         gain_cols = lax.dynamic_slice_in_dim(final_gain, yx * 128, 128, 0).astype(F32)
         weighted = gain_cols * jnp.sum(packed[:, :16], axis=0)
         both = jnp.stack([weighted, packed[:, 16]])
+        both, weights = lax.optimization_barrier((both, weights))
         both = to_column_owners(both, zl, 2 * zh + core)
-        both, blocks[3], blocks[-3] = lax.optimization_barrier((both, blocks[3], blocks[-3]))
-        blocks[4] = last_hop(jnp.where(first, blocks[-3], blocks[3]))
-        weighted_cols = both[:, 0].reshape(64, 128)
-        token_cols = both[:, 1].reshape(64, 128)
-        back_w = back(weighted_cols)
 
     depth = tokens.shape[1]
     columns = width + 2 * HEAD_SIZE
@@ -205,11 +201,15 @@
         return attention(heads, kept[0], came[0], kept[1] + came[1], tables)
 
     with jax.named_scope("project"):
-        known = {k: scaled(k, parts) for k, parts in blocks.items() if k != 4}
-        near = project(*known[0])
-        next_1, next_2, next_3 = [
-            both_sides(project(*known[a]), project(*known[b])) for a, b in ((1, -3), (2, -2), (-1, 3))
-        ]
+        known = {k: project(*scaled(k, blocks[k])) for k in (0, 1, -1, 2, -2)}
+        known, blocks[3], blocks[-3] = lax.optimization_barrier((known, blocks[3], blocks[-3]))
+        blocks[4] = last_hop(jnp.where(first, blocks[-3], blocks[3]))
+        weighted_cols = both[:, 0].reshape(64, 128)
+        token_cols = both[:, 1].reshape(64, 128)
+        back_w = back(weighted_cols)
+        near, next_2 = known[0], both_sides(known[2], known[-2])
+        next_1 = both_sides(known[1], project(*scaled(-3, blocks[-3])))
+        next_3 = both_sides(known[-1], project(*scaled(3, blocks[3])))
         mixed_1, total_1 = attend(next_1, next_3)
         last_block, near, next_2, mixed_1, back_w, token_cols = lax.optimization_barrier(
             (blocks[4], near, next_2, mixed_1, back_w, token_cols)
@@ -218,13 +218,8 @@
         mixed_0, total_0 = attend(both_sides(near, last_block), next_2)
 
     with jax.named_scope("return_heads"):
-
-        def owned(slot_0, slot_1):
-            oa = send(slot_0, lambda z, c: (z, z // 2) if c == 0 else (z + 2, z // 2))
-            ob = send(slot_1, lambda z, c: (z + 1, z // 2) if c == 0 else (z - 1, z // 2))
-            return jnp.concatenate(
-                [jnp.where(even, oa, ob), jnp.where(even, ob, oa)], axis=1
-            )
+        oa = send(mixed_0, lambda z, c: (z, z // 2) if c == 0 else (z + 2, z // 2))
+        ob = send(mixed_1, lambda z, c: (z + 1, z // 2) if c == 0 else (z - 1, z // 2))
 
     with jax.named_scope("tail"):
         total = total_0 + total_1
@@ -232,10 +227,13 @@
         line = jnp.concatenate(
             [mixed_0[-1:], mixed_1[-1:], high.astype(BF16), (total - high).astype(BF16)], axis=0
         )
+        line, ob = lax.optimization_barrier((line, ob))
         line = lax.dynamic_slice_in_dim(from_everyone(line, ("zl", "c")), 4 * core, 4, 0)
+        line, oa = lax.optimization_barrier((line, oa))
+        head_out = jnp.concatenate(
+            [jnp.where(even, oa, ob), jnp.where(even, ob, oa)], axis=1
+        )
         every = from_everyone(line, ("y", "x"))
-        every, mixed_0, mixed_1 = lax.optimization_barrier((every, mixed_0, mixed_1))
-        head_out = owned(mixed_0, mixed_1)
         every = every.reshape(16, 2, 2, 4, width)
         last = every[:, :, :, :2].reshape(16, 2, 4, width)
         last = jnp.concatenate(

time: 209 us -> 228 us (1.091)
  blocking collectives: 14.1 us -> 0 us
  matrix products: 16 us -> 26.6 us
  waiting for transfers between devices: 69.1 us -> 78.1 us
  starting transfers between devices: 60.9 us -> 69.2 us
  other arithmetic: 23.1 us -> 26.3 us
    ppermute x4, waiting for transfers between devices: 17.9 us -> 0.01 us  [to_column_owners(): got.append(lax.ppermute(value, ('zl', *MP), pairs))]
    all_to_all x1 -> x0, blocking collectives: 14.1 us -> none  [from_everyone(): lax.all_to_all(jnp.broadcast_to(value[None], (count, *value.shape)), axis...]
    dot_general x8, matrix products: 12.3 us -> 23 us  [project(): return (jnp.dot(block, weight, preferred_element_type=F32), square)]
    all_gather x1, waiting for transfers between devices: 0.02 us -> 8.13 us  [per_device(): weights = lax.all_gather(rows, ('y', 'x'), axis=0, tiled=True)]
    ppermute x1, waiting for transfers between devices: 0.01 us -> 7.77 us  [last_hop(): return lax.ppermute(value, ('zl', *MP), pairs)]
    all_to_all x1 -> x2, waiting for transfers between devices: 4.97 us -> 11.5 us  [from_everyone(): lax.all_to_all(jnp.broadcast_to(value[None], (count, *value.shape)), axis...]
    all_to_all x1, waiting for transfers between devices: 3.51 us -> 8.2 us  [per_device(): lax.all_to_all(packed[:, None], DP, 0, 0, tiled=True)]
    all_to_all x1 -> x2, starting transfers between devices: 6.23 us -> 10 us  [from_everyone(): lax.all_to_all(jnp.broadcast_to(value[None], (count, *value.shape)), axis...]
  transfers between devices with their start and end apart: 26 -> 27, of which waited for: 15 -> 14; matrix products, arithmetic and copies ran while one was open for 16% -> 21% of each run, Pallas kernels for 1% -> 1%
where the time goes in v3:
time: 228 us; the launch traced here: 227 us
  waiting for transfers between devices  78.1 us (34%)
  starting transfers between devices  69.2 us (30%)
  matrix products  26.6 us (12%)
  other arithmetic  26.3 us (12%)
  between operations  17.7 us (8%)
  local copies, waits for them, and re-layouts  6.33 us (3%)
  Pallas kernels  2.63 us (1%)
    ppermute x6, waiting for transfers between devices, along(): return lax.ppermute(value, ('zl', 'zh'), pairs)  25.6 us
    dot_general x8, matrix products, project(): return (jnp.dot(block, weight, preferred_element_type=F32), square)  23 us
    ppermute x6, starting transfers between devices, along(): return lax.ppermute(value, ('zl', 'zh'), pairs)  12.1 us
    reduce_sum x7, other arithmetic, scaled(): done = ((t * g).astype(BF16), jnp.sum(t * t, axis=1, keepdims=True))  12 us
    all_to_all x2, waiting for transfers between devices, from_everyone(): lax.all_to_all(jnp.broadcast_to(value[None], (count, *value.shape)), axis...  11.5 us
    ppermute x4, starting transfers between devices, to_column_owners(): got.append(lax.ppermute(value, ('zl', *MP), pairs))  10.7 us
    ppermute x4, starting transfers between devices, send(): return lax.ppermute(value, ('zl', 'c'), pairs)  10.6 us
    ppermute x4, waiting for transfers between devices, send(): return lax.ppermute(value, ('zl', 'c'), pairs)  10.3 us
  transfers between devices with their start and end apart: 27, of which 14 were waited for; matrix products, arithmetic and copies ran while one was open for 21% of the time, Pallas kernels for 1%

profile of v3, /device:TPU:1, one launch (start us, length us, event | category | flops | bytes accessed | tf_op | source)
XLA Modules:
  0.0 226.9 jit_solution(10482923023955653793)
XLA Ops:
  9.2 6.3 %collective-permute-start.4 = (bf16[128,768]{1,0:T(8,128)(2,1)S(1)}, bf16[128,768]{1,0:T(8,128)(2,1)S(1)}, u32[]{:S(2)}, u32[]{:S(2)}) collective-permute-start(bf16[128,768]{1,0:T(8,128)(2,1)S(1)} %get-tuple-element.140), channel_id=1, source_target_pairs={{0,0},{1,128},{64,1},{65,129},{128,64},{129,192},{192,65},{193,193... | collective-permute-start | bytes 589832 | tf_op jit(solution)/shard_map/weights/ppermute | solution.py:34
  16.9 2.6 %collective-permute-done.4 = bf16[128,768]{1,0:T(8,128)(2,1)S(1)} collective-permute-done((bf16[128,768]{1,0:T(8,128)(2,1)S(1)}, bf16[128,768]{1,0:T(8,128)(2,1)S(1)}, u32[]{:S(2)}, u32[]{:S(2)}) %collective-permute-start.4) | collective-permute-done | bytes 196640 | tf_op jit(solution)/shard_map/weights/ppermute | solution.py:34
  19.5 4.9 %collective-permute-done.5 = bf16[128,768]{1,0:T(8,128)(2,1)S(1)} collective-permute-done((bf16[128,768]{1,0:T(8,128)(2,1)S(1)}, bf16[128,768]{1,0:T(8,128)(2,1)S(1)}, u32[]{:S(2)}, u32[]{:S(2)}) %collective-permute-start.5) | collective-permute-done | bytes 196640 | tf_op jit(solution)/shard_map/weights/ppermute | solution.py:34
  25.4 4.4 %collective-permute-start.2 = (bf16[256,2048]{1,0:T(8,128)(2,1)S(1)}, bf16[256,2048]{1,0:T(8,128)(2,1)S(1)}, u32[]{:S(2)}, u32[]{:S(2)}) collective-permute-start(bf16[256,2048]{1,0:T(8,128)(2,1)S(1)} %copy-done.1), channel_id=1, source_target_pairs={{0,194},{64,0},{128,64},{192,128},{2,192},{66,2},{130,66},{194,130... | collective-permute-start | bytes 3145736 | tf_op jit(solution)/shard_map/direction/ppermute | solution.py:40
  30.0 3.1 %fusion.32 = bf16[8,8,16,128]{3,1,2,0:T(8,128)(2,1)S(1)} fusion(bf16[1002,2048]{1,0:T(8,128)(2,1)} %param.17, s32[1002]{0:T(1024)S(1)} %iota_add_fusion, s32[64]{0:T(128)S(1)} %copy-done.19, s32[64]{0:T(128)S(1)} %copy-done.20), kind=kOutput, calls=%fused_computation.49 | convolution fusion | flops 263184128 | bytes 4370856 | tf_op jit(solution)/shard_map/direction/dot_general | solution.py:159
  34.1 8.3 %all-to-all-start = ((bf16[64,17,128]{2,1,0:T(8,128)(2,1)}), bf16[64,17,128]{2,1,0:T(8,128)(2,1)S(1)}, u32[]{:S(2)}, u32[]{:S(2)}) async-start(bf16[64,17,128]{2,1,0:T(8,128)(2,1)} %pad_maximum_fusion.1), calls=%async_computation | async-start | bytes 786432 | tf_op jit(solution)/shard_map/direction/all_to_all | solution.py:164
  44.2 9.0 %collective-permute-done = bf16[256,2048]{1,0:T(8,128)(2,1)} collective-permute-done((bf16[256,2048]{1,0:T(8,128)(2,1)S(1)}, bf16[256,2048]{1,0:T(8,128)(2,1)}, u32[]{:S(2)}, u32[]{:S(2)}) %collective-permute-start) | collective-permute-done | bytes 1048608 | tf_op jit(solution)/shard_map/direction/ppermute | solution.py:40
  53.9 3.3 %collective-permute-start.3 = (bf16[256,2048]{1,0:T(8,128)(2,1)S(1)}, bf16[256,2048]{1,0:T(8,128)(2,1)S(1)}, u32[]{:S(2)}, u32[]{:S(2)}) collective-permute-start(bf16[256,2048]{1,0:T(8,128)(2,1)S(1)} %collective-permute-done.2), channel_id=1, source_target_pairs={{0,194},{64,0},{128,64},{192,128},{2,192},{66,2},{130,66},{194,130... | collective-permute-start | bytes 3145736 | tf_op jit(solution)/shard_map/direction/ppermute | solution.py:40
  58.1 2.5 %fusion.19 = (f32[256]{0:T(256)S(1)}, bf16[256,2048]{1,0:T(8,128)(2,1)}) fusion(bf16[256,2048]{1,0:T(8,128)(2,1)} %collective-permute-done, f32[2048]{0:T(1024)S(1)} %get-tuple-element.147), kind=kLoop, calls=%fused_computation.36 | loop fusion | flops 2621184 | bytes 2106368 | tf_op jit(solution)/shard_map/project/reduce_sum | solution.py:188
  61.9 16.6 %collective-permute-done.1 = bf16[256,2048]{1,0:T(8,128)(2,1)} collective-permute-done((bf16[256,2048]{1,0:T(8,128)(2,1)}, bf16[256,2048]{1,0:T(8,128)(2,1)}, u32[]{:S(2)}, u32[]{:S(2)}) %collective-permute-start.1) | collective-permute-done | bytes 1048608 | tf_op jit(solution)/shard_map/direction/ppermute | solution.py:40
  78.5 2.6 %fusion.17 = (f32[256]{0:T(256)S(1)}, bf16[256,2048]{1,0:T(8,128)(2,1)}) fusion(bf16[256,2048]{1,0:T(8,128)(2,1)} %collective-permute-done.1, f32[2048]{0:T(1024)S(1)} %get-tuple-element.148), kind=kLoop, calls=%fused_computation.34 | loop fusion | flops 2621184 | bytes 2106368 | tf_op jit(solution)/shard_map/project/reduce_sum | solution.py:188
  82.4 4.3 %collective-permute-start.6 = (bf16[256,2048]{1,0:T(8,128)(2,1)}, bf16[256,2048]{1,0:T(8,128)(2,1)S(1)}, u32[]{:S(2)}, u32[]{:S(2)}) collective-permute-start(bf16[256,2048]{1,0:T(8,128)(2,1)} %copy-done.4), channel_id=1, source_target_pairs={{0,194},{64,0},{128,64},{192,128},{2,192},{66,2},{130,66},{194,130... | collective-permute-start | bytes 3145736 | tf_op jit(solution)/shard_map/direction/ppermute | solution.py:40
  87.4 8.1 %all-gather.2.cloned.1.call-done = bf16[2048,1536]{1,0:T(8,128)(2,1)} async-done(((bf16[128,1536]{1,0:T(8,128)(2,1)}), bf16[2048,1536]{1,0:T(8,128)(2,1)}) %all-gather.2.cloned.1.call-update) | async-done | bytes 6291472 | tf_op jit(solution)/shard_map/weights/all_gather | solution.py:151
  95.5 4.6 %collective-permute-start.14 = (f32[2,16,128]{2,1,0:T(8,128)}, f32[2,16,128]{2,1,0:T(8,128)}, u32[]{:S(2)}, u32[]{:S(2)}) collective-permute-start(f32[2,16,128]{2,1,0:T(8,128)} %pad_maximum_fusion.13), channel_id=1, source_target_pairs={{0,3},{1,67},{2,131},{3,195},{64,0},{65,64},{66,128},{67,192},{128... | collective-permute-start | bytes 49160 | tf_op jit(solution)/shard_map/direction/ppermute | solution.py:47
  102.9 4.2 %fusion.14 = f32[256,768]{1,0:T(8,128)} fusion(bf16[256,2048]{1,0:T(8,128)(2,1)} %get-tuple-element.50, bf16[2048,1536]{1,0:T(8,128)(2,1)} %all-gather.2.cloned.1.call-done, s32[]{:T(128)S(6)} %select_n.268), kind=kOutput, calls=%fused_computation.14 | convolution fusion | flops 805306368 | bytes 4980740 | tf_op jit(solution)/shard_map/project/dot_general | solution.py:193
  107.1 3.9 %fusion.12 = f32[256,768]{1,0:T(8,128)} fusion(bf16[256,2048]{1,0:T(8,128)(2,1)S(1)} %copy-done.6, bf16[2048,1536]{1,0:T(8,128)(2,1)} %all-gather.2.cloned.1.call-done, s32[]{:T(128)S(6)} %select_n.272), kind=kOutput, calls=%fused_computation.12 | convolution fusion | flops 805306368 | bytes 4980740 | tf_op jit(solution)/shard_map/project/dot_general | solution.py:193
  116.7 3.3 %collective-permute-start.11 = (f32[2,16,128]{2,1,0:T(8,128)}, f32[2,16,128]{2,1,0:T(8,128)}, u32[]{:S(2)}, u32[]{:S(2)}) collective-permute-start(f32[2,16,128]{2,1,0:T(8,128)} %pad_maximum_fusion.13), channel_id=1, source_target_pairs={{0,0},{1,64},{2,128},{3,192},{64,1},{65,65},{66,129},{67,193},{128... | collective-permute-start | bytes 49160 | tf_op jit(solution)/shard_map/direction/ppermute | solution.py:47
  123.8 3.3 %fusion.2 = f32[256,768]{1,0:T(8,128)S(1)} fusion(bf16[256,2048]{1,0:T(8,128)(2,1)} %get-tuple-element.73, bf16[2048,1536]{1,0:T(8,128)(2,1)} %all-gather.2.cloned.1.call-done, s32[]{:T(128)S(6)} %select_n.293), kind=kOutput, calls=%fused_computation.2 | convolution fusion | flops 805306368 | bytes 4980740 | tf_op jit(solution)/shard_map/project/dot_general | solution.py:193
  127.1 3.0 %fusion.4 = f32[256,768]{1,0:T(8,128)S(1)} fusion(bf16[256,2048]{1,0:T(8,128)(2,1)S(1)} %copy-done.8, bf16[2048,1536]{1,0:T(8,128)(2,1)} %all-gather.2.cloned.1.call-done, s32[]{:T(128)S(6)} %select_n.289), kind=kOutput, calls=%fused_computation.4 | convolution fusion | flops 805306368 | bytes 4980740 | tf_op jit(solution)/shard_map/project/dot_general | solution.py:193
  133.1 2.4 %collective-permute-start.8 = (bf16[256,2048]{1,0:T(8,128)(2,1)S(1)}, bf16[256,2048]{1,0:T(8,128)(2,1)S(1)}, u32[]{:S(2)}, u32[]{:S(2)}) collective-permute-start(bf16[256,2048]{1,0:T(8,128)(2,1)S(1)} %copy-done.2), channel_id=1, source_target_pairs={{0,64},{1,195},{64,128},{65,1},{128,192},{129,65},{192,2},{193,129... | collective-permute-start | bytes 3145736 | tf_op jit(solution)/shard_map/project/ppermute | solution.py:123
  139.5 7.8 %collective-permute-done.8 = bf16[256,2048]{1,0:T(8,128)(2,1)S(1)} collective-permute-done((bf16[256,2048]{1,0:T(8,128)(2,1)S(1)}, bf16[256,2048]{1,0:T(8,128)(2,1)S(1)}, u32[]{:S(2)}, u32[]{:S(2)}) %collective-permute-start.8) | collective-permute-done | bytes 1048608 | tf_op jit(solution)/shard_map/project/ppermute | solution.py:123
  148.2 3.0 %fusion = f32[256,768]{1,0:T(8,128)S(1)} fusion(bf16[256,2048]{1,0:T(8,128)(2,1)S(1)} %get-tuple-element.82, bf16[2048,1536]{1,0:T(8,128)(2,1)} %all-gather.2.cloned.1.call-done, s32[]{:T(128)S(6)} %select_n.310), kind=kOutput, calls=%fused_computation | convolution fusion | flops 805306368 | bytes 4980740 | tf_op jit(solution)/shard_map/project/dot_general | solution.py:193
  152.2 2.3 %collective-permute-start.15 = (f32[256,768]{1,0:T(8,128)}, f32[256,768]{1,0:T(8,128)S(1)}, u32[]{:S(2)}, u32[]{:S(2)}) collective-permute-start(f32[256,768]{1,0:T(8,128)} %get-tuple-element.102), channel_id=1, source_target_pairs={{0,1},{1,0},{2,3},{3,2},{4,5},{5,4},{6,7},{7,6},{8,9},{9,8},{10,11... | collective-permute-start | bytes 2359304 | tf_op jit(solution)/shard_map/project/ppermute | solution.py:60
  160.1 2.7 %collective-permute-done.17 = bf16[256,512]{1,0:T(8,128)(2,1)S(1)} collective-permute-done((bf16[256,512]{1,0:T(8,128)(2,1)S(1)}, bf16[256,512]{1,0:T(8,128)(2,1)S(1)}, u32[]{:S(2)}, u32[]{:S(2)}) %collective-permute-start.17) | collective-permute-done | bytes 262176 | tf_op jit(solution)/shard_map/return_heads/ppermute | solution.py:34
  164.1 5.1 %all-to-all-start.1 = ((bf16[8,4,512]{2,1,0:T(4,128)(2,1)}), bf16[8,4,512]{2,1,0:T(4,128)(2,1)S(1)}, u32[]{:S(2)}, u32[]{:S(2)}) async-start(bf16[8,4,512]{2,1,0:T(4,128)(2,1)} %broadcast_in_dim.113), calls=%async_computation.1 | async-start | bytes 65536 | tf_op jit(solution)/shard_map/tail/all_to_all | solution.py:23
  169.2 5.0 %all-to-all-done.1 = bf16[8,4,512]{2,1,0:T(4,128)(2,1)S(1)} async-done(((bf16[8,4,512]{2,1,0:T(4,128)(2,1)}), bf16[8,4,512]{2,1,0:T(4,128)(2,1)S(1)}, u32[]{:S(2)}, u32[]{:S(2)}) %all-to-all-start.1) | async-done | bytes 32800 | tf_op jit(solution)/shard_map/tail/all_to_all | solution.py:23
  175.0 5.0 %all-to-all-start.2 = ((bf16[16,4,4,512]{3,2,1,0:T(4,128)(2,1)}), bf16[16,4,4,512]{3,2,1,0:T(4,128)(2,1)S(1)}, u32[]{:S(2)}, u32[]{:S(2)}) async-start(bf16[16,4,4,512]{3,2,1,0:T(4,128)(2,1)} %broadcast_in_dim.114), calls=%async_computation.2 | async-start | bytes 524288 | tf_op jit(solution)/shard_map/tail/all_to_all | solution.py:23
  181.0 6.6 %all-to-all-done.2 = bf16[16,4,4,512]{3,2,1,0:T(4,128)(2,1)S(1)} async-done(((bf16[16,4,4,512]{3,2,1,0:T(4,128)(2,1)}), bf16[16,4,4,512]{3,2,1,0:T(4,128)(2,1)S(1)}, u32[]{:S(2)}, u32[]{:S(2)}) %all-to-all-start.2) | async-done | bytes 262176 | tf_op jit(solution)/shard_map/tail/all_to_all | solution.py:23
  188.0 6.7 %collective-permute-start.21 = (bf16[64,128]{1,0:T(8,128)(2,1)S(1)}, bf16[64,128]{1,0:T(8,128)(2,1)S(1)}, u32[]{:S(2)}, u32[]{:S(2)}) collective-permute-start(bf16[64,128]{1,0:T(8,128)(2,1)S(1)} %convolution_convert_fusion.1), channel_id=1, source_target_pairs={{0,3},{1,2},{2,1},{3,0},{4,7},{5,6},{6,5},{7,4},{8,11},{9,10},{10,... | collective-permute-start | bytes 49160 | tf_op jit(solution)/shard_map/tail/ppermute | solution.py:54
  196.1 5.1 %collective-permute-done.20 = bf16[64,128]{1,0:T(8,128)(2,1)S(1)} collective-permute-done((bf16[64,128]{1,0:T(8,128)(2,1)S(1)}, bf16[64,128]{1,0:T(8,128)(2,1)S(1)}, u32[]{:S(2)}, u32[]{:S(2)}) %collective-permute-start.20) | collective-permute-done | bytes 16416 | tf_op jit(solution)/shard_map/tail/ppermute | solution.py:54
  202.6 4.6 %all-to-all-start.3 = ((f32[64,1,128]{2,1,0:T(1,128)}), f32[64,1,128]{2,1,0:T(1,128)S(1)}, u32[]{:S(2)}, u32[]{:S(2)}) async-start(f32[64,1,128]{2,1,0:T(1,128)} %bitcast.27), calls=%async_computation.3 | async-start | bytes 65536 | tf_op jit(solution)/shard_map/tail/all_to_all | solution.py:267
  208.1 8.2 %all-to-all-done.3 = f32[64,1,128]{2,1,0:T(1,128)S(1)} async-done(((f32[64,1,128]{2,1,0:T(1,128)}), f32[64,1,128]{2,1,0:T(1,128)S(1)}, u32[]{:S(2)}, u32[]{:S(2)}) %all-to-all-start.3) | async-done | bytes 32800 | tf_op jit(solution)/shard_map/tail/all_to_all | solution.py:267
  (167 shorter events, 46.4 us)
Async XLA Ops:
  7.2 130.2 %copy-start = (bf16[1024,128]{1,0:T(8,128)(2,1)S(1)}, bf16[1024,128]{1,0:T(8,128)(2,1)}, u32[]{:S(2)}) copy-start(bf16[1024,128]{1,0:T(8,128)(2,1)} %param.15) | copy-start | bytes 786436
  7.2 22.7 %copy-start.19 = (s32[64]{0:T(128)S(1)}, s32[64]{0:T(128)}, u32[]{:S(2)}) copy-start(s32[64]{0:T(128)} %param.19) | copy-start | bytes 772
  7.2 22.7 %copy-start.20 = (s32[64]{0:T(128)S(1)}, s32[64]{0:T(128)}, u32[]{:S(2)}) copy-start(s32[64]{0:T(128)} %param.18) | copy-start | bytes 772
  7.2 88.3 %all-gather.2.cloned.1.call-start = ((), (), s32[]{:S(2)}) async-start(), calls=%async_computation.4 | async-start | bytes 6684672 | tf_op jit(solution)/shard_map/weights/all_gather | solution.py:151
  9.2 10.3 %collective-permute-start.4 = (bf16[128,768]{1,0:T(8,128)(2,1)S(1)}, bf16[128,768]{1,0:T(8,128)(2,1)S(1)}, u32[]{:S(2)}, u32[]{:S(2)}) collective-permute-start(bf16[128,768]{1,0:T(8,128)(2,1)S(1)} %get-tuple-element.140), channel_id=1, source_target_pairs={{0,0},{1,128},{64,1},{65,129},{128,64},{129,192},{192,65},{193,193... | collective-permute-start | bytes 589832 | tf_op jit(solution)/shard_map/weights/ppermute | solution.py:34
  15.5 9.0 %collective-permute-start.5 = (bf16[128,768]{1,0:T(8,128)(2,1)S(1)}, bf16[128,768]{1,0:T(8,128)(2,1)S(1)}, u32[]{:S(2)}, u32[]{:S(2)}) collective-permute-start(bf16[128,768]{1,0:T(8,128)(2,1)S(1)} %get-tuple-element.141), channel_id=1, source_target_pairs={{0,64},{1,192},{64,65},{65,193},{128,0},{129,128},{192,1},{193,129... | collective-permute-start | bytes 589832 | tf_op jit(solution)/shard_map/weights/ppermute | solution.py:34
  25.3 27.9 %collective-permute-start = (bf16[256,2048]{1,0:T(8,128)(2,1)S(1)}, bf16[256,2048]{1,0:T(8,128)(2,1)}, u32[]{:S(2)}, u32[]{:S(2)}) collective-permute-start(bf16[256,2048]{1,0:T(8,128)(2,1)S(1)} %copy-done.1), channel_id=1, source_target_pairs={{0,64},{64,128},{128,192},{192,2},{2,66},{66,130},{130,194},{194,0... | collective-permute-start | bytes 3145736 | tf_op jit(solution)/shard_map/direction/ppermute | solution.py:40
  25.4 28.5 %collective-permute-start.2 = (bf16[256,2048]{1,0:T(8,128)(2,1)S(1)}, bf16[256,2048]{1,0:T(8,128)(2,1)S(1)}, u32[]{:S(2)}, u32[]{:S(2)}) collective-permute-start(bf16[256,2048]{1,0:T(8,128)(2,1)S(1)} %copy-done.1), channel_id=1, source_target_pairs={{0,194},{64,0},{128,64},{192,128},{2,192},{66,2},{130,66},{194,130... | collective-permute-start | bytes 3145736 | tf_op jit(solution)/shard_map/direction/ppermute | solution.py:40
  34.1 46.9 %all-to-all-start = ((bf16[64,17,128]{2,1,0:T(8,128)(2,1)}), bf16[64,17,128]{2,1,0:T(8,128)(2,1)S(1)}, u32[]{:S(2)}, u32[]{:S(2)}) async-start(bf16[64,17,128]{2,1,0:T(8,128)(2,1)} %pad_maximum_fusion.1), calls=%async_computation | async-start | bytes 786432 | tf_op jit(solution)/shard_map/direction/all_to_all | solution.py:164
  53.2 25.3 %collective-permute-start.1 = (bf16[256,2048]{1,0:T(8,128)(2,1)}, bf16[256,2048]{1,0:T(8,128)(2,1)}, u32[]{:S(2)}, u32[]{:S(2)}) collective-permute-start(bf16[256,2048]{1,0:T(8,128)(2,1)} %collective-permute-done), channel_id=1, source_target_pairs={{0,64},{64,128},{128,192},{192,2},{2,66},{66,130},{130,194},{194,0... | collective-permute-start | bytes 3145736 | tf_op jit(solution)/shard_map/direction/ppermute | solution.py:40
  53.9 27.1 %collective-permute-start.3 = (bf16[256,2048]{1,0:T(8,128)(2,1)S(1)}, bf16[256,2048]{1,0:T(8,128)(2,1)S(1)}, u32[]{:S(2)}, u32[]{:S(2)}) collective-permute-start(bf16[256,2048]{1,0:T(8,128)(2,1)S(1)} %collective-permute-done.2), channel_id=1, source_target_pairs={{0,194},{64,0},{128,64},{192,128},{2,192},{66,2},{130,66},{194,130... | collective-permute-start | bytes 3145736 | tf_op jit(solution)/shard_map/direction/ppermute | solution.py:40
  82.4 34.3 %collective-permute-start.6 = (bf16[256,2048]{1,0:T(8,128)(2,1)}, bf16[256,2048]{1,0:T(8,128)(2,1)S(1)}, u32[]{:S(2)}, u32[]{:S(2)}) collective-permute-start(bf16[256,2048]{1,0:T(8,128)(2,1)} %copy-done.4), channel_id=1, source_target_pairs={{0,194},{64,0},{128,64},{192,128},{2,192},{66,2},{130,66},{194,130... | collective-permute-start | bytes 3145736 | tf_op jit(solution)/shard_map/direction/ppermute | solution.py:40
  86.7 33.2 %collective-permute-start.7 = (bf16[256,2048]{1,0:T(8,128)(2,1)}, bf16[256,2048]{1,0:T(8,128)(2,1)S(1)}, u32[]{:S(2)}, u32[]{:S(2)}) collective-permute-start(bf16[256,2048]{1,0:T(8,128)(2,1)} %collective-permute-done.1), channel_id=1, source_target_pairs={{0,64},{64,128},{128,192},{192,2},{2,66},{66,130},{130,194},{194,0... | collective-permute-start | bytes 3145736 | tf_op jit(solution)/shard_map/direction/ppermute | solution.py:40
  95.5 40.0 %collective-permute-start.14 = (f32[2,16,128]{2,1,0:T(8,128)}, f32[2,16,128]{2,1,0:T(8,128)}, u32[]{:S(2)}, u32[]{:S(2)}) collective-permute-start(f32[2,16,128]{2,1,0:T(8,128)} %pad_maximum_fusion.13), channel_id=1, source_target_pairs={{0,3},{1,67},{2,131},{3,195},{64,0},{65,64},{66,128},{67,192},{128... | collective-permute-start | bytes 49160 | tf_op jit(solution)/shard_map/direction/ppermute | solution.py:47
  100.2 35.7 %collective-permute-start.13 = (f32[2,16,128]{2,1,0:T(8,128)}, f32[2,16,128]{2,1,0:T(8,128)}, u32[]{:S(2)}, u32[]{:S(2)}) collective-permute-start(f32[2,16,128]{2,1,0:T(8,128)} %pad_maximum_fusion.13), channel_id=1, source_target_pairs={{0,2},{1,66},{2,130},{3,194},{64,3},{65,67},{66,131},{67,195},{128... | collective-permute-start | bytes 49160 | tf_op jit(solution)/shard_map/direction/ppermute | solution.py:47
  101.9 34.0 %collective-permute-start.12 = (f32[2,16,128]{2,1,0:T(8,128)}, f32[2,16,128]{2,1,0:T(8,128)}, u32[]{:S(2)}, u32[]{:S(2)}) collective-permute-start(f32[2,16,128]{2,1,0:T(8,128)} %pad_maximum_fusion.13), channel_id=1, source_target_pairs={{0,1},{1,65},{2,129},{3,193},{64,2},{65,66},{66,130},{67,194},{128... | collective-permute-start | bytes 49160 | tf_op jit(solution)/shard_map/direction/ppermute | solution.py:47
  116.7 19.2 %collective-permute-start.11 = (f32[2,16,128]{2,1,0:T(8,128)}, f32[2,16,128]{2,1,0:T(8,128)}, u32[]{:S(2)}, u32[]{:S(2)}) collective-permute-start(f32[2,16,128]{2,1,0:T(8,128)} %pad_maximum_fusion.13), channel_id=1, source_target_pairs={{0,0},{1,64},{2,128},{3,192},{64,1},{65,65},{66,129},{67,193},{128... | collective-permute-start | bytes 49160 | tf_op jit(solution)/shard_map/direction/ppermute | solution.py:47
  123.7 9.4 %collective-permute-start.10 = (f32[256,1]{1,0:T(8,128)S(1)}, f32[256,1]{1,0:T(8,128)S(1)}, u32[]{:S(2)}, u32[]{:S(2)}) collective-permute-start(f32[256,1]{1,0:T(8,128)S(1)} %broadcast_select_fusion.11), channel_id=1, source_target_pairs={{0,1},{1,0},{2,3},{3,2},{4,5},{5,4},{6,7},{7,6},{8,9},{9,8},{10,11... | collective-permute-start | bytes 3080 | tf_op jit(solution)/shard_map/project/ppermute | solution.py:60
  133.1 14.2 %collective-permute-start.8 = (bf16[256,2048]{1,0:T(8,128)(2,1)S(1)}, bf16[256,2048]{1,0:T(8,128)(2,1)S(1)}, u32[]{:S(2)}, u32[]{:S(2)}) collective-permute-start(bf16[256,2048]{1,0:T(8,128)(2,1)S(1)} %copy-done.2), channel_id=1, source_target_pairs={{0,64},{1,195},{64,128},{65,1},{128,192},{129,65},{192,2},{193,129... | collective-permute-start | bytes 3145736 | tf_op jit(solution)/shard_map/project/ppermute | solution.py:123
  135.6 2.6 %collective-permute-start.9 = (f32[256,768]{1,0:T(8,128)S(1)}, f32[256,768]{1,0:T(8,128)S(1)}, u32[]{:S(2)}, u32[]{:S(2)}) collective-permute-start(f32[256,768]{1,0:T(8,128)S(1)} %copy-done.9), channel_id=1, source_target_pairs={{0,1},{1,0},{2,3},{3,2},{4,5},{5,4},{6,7},{7,6},{8,9},{9,8},{10,11... | collective-permute-start | bytes 2359304 | tf_op jit(solution)/shard_map/project/ppermute | solution.py:60
  152.2 4.5 %collective-permute-start.15 = (f32[256,768]{1,0:T(8,128)}, f32[256,768]{1,0:T(8,128)S(1)}, u32[]{:S(2)}, u32[]{:S(2)}) collective-permute-start(f32[256,768]{1,0:T(8,128)} %get-tuple-element.102), channel_id=1, source_target_pairs={{0,1},{1,0},{2,3},{3,2},{4,5},{5,4},{6,7},{7,6},{8,9},{9,8},{10,11... | collective-permute-start | bytes 2359304 | tf_op jit(solution)/shard_map/project/ppermute | solution.py:60
  154.9 1.8 collective-permute-start.16
  155.0 7.8 %collective-permute-start.17 = (bf16[256,512]{1,0:T(8,128)(2,1)S(1)}, bf16[256,512]{1,0:T(8,128)(2,1)S(1)}, u32[]{:S(2)}, u32[]{:S(2)}) collective-permute-start(bf16[256,512]{1,0:T(8,128)(2,1)S(1)} %get-tuple-element.88), channel_id=1, source_target_pairs={{0,64},{1,192},{64,128},{65,0},{128,193},{129,65},{192,1},{193,129... | collective-permute-start | bytes 786440 | tf_op jit(solution)/shard_map/return_heads/ppermute | solution.py:34
  158.1 43.1 %copy-start.14 = (f32[4,1,16,128]{3,2,1,0:T(8,128)S(1)}, f32[4,1,16,128]{3,2,1,0:T(8,128)}, u32[]{:S(2)}) copy-start(f32[4,1,16,128]{3,2,1,0:T(8,128)} %copy-done.13) | copy-start | bytes 98308
  158.1 43.1 %copy-start.16 = (f32[4,1,16,128]{3,2,1,0:T(8,128)S(1)}, f32[4,1,16,128]{3,2,1,0:T(8,128)}, u32[]{:S(2)}) copy-start(f32[4,1,16,128]{3,2,1,0:T(8,128)} %get-tuple-element.134) | copy-start | bytes 98308
  158.1 16.1 %collective-permute-start.18 = (bf16[256,512]{1,0:T(8,128)(2,1)S(1)}, bf16[256,512]{1,0:T(8,128)(2,1)S(1)}, u32[]{:S(2)}, u32[]{:S(2)}) collective-permute-start(bf16[256,512]{1,0:T(8,128)(2,1)S(1)} %get-tuple-element.87), channel_id=1, source_target_pairs={{0,0},{1,128},{64,64},{65,192},{128,129},{129,1},{192,193},{193,65... | collective-permute-start | bytes 786440 | tf_op jit(solution)/shard_map/return_heads/ppermute | solution.py:34
  164.1 10.0 %all-to-all-start.1 = ((bf16[8,4,512]{2,1,0:T(4,128)(2,1)}), bf16[8,4,512]{2,1,0:T(4,128)(2,1)S(1)}, u32[]{:S(2)}, u32[]{:S(2)}) async-start(bf16[8,4,512]{2,1,0:T(4,128)(2,1)} %broadcast_in_dim.113), calls=%async_computation.1 | async-start | bytes 65536 | tf_op jit(solution)/shard_map/tail/all_to_all | solution.py:23
  175.0 12.5 %all-to-all-start.2 = ((bf16[16,4,4,512]{3,2,1,0:T(4,128)(2,1)}), bf16[16,4,4,512]{3,2,1,0:T(4,128)(2,1)S(1)}, u32[]{:S(2)}, u32[]{:S(2)}) async-start(bf16[16,4,4,512]{3,2,1,0:T(4,128)(2,1)} %broadcast_in_dim.114), calls=%async_computation.2 | async-start | bytes 524288 | tf_op jit(solution)/shard_map/tail/all_to_all | solution.py:23
  188.0 8.1 %collective-permute-start.21 = (bf16[64,128]{1,0:T(8,128)(2,1)S(1)}, bf16[64,128]{1,0:T(8,128)(2,1)S(1)}, u32[]{:S(2)}, u32[]{:S(2)}) collective-permute-start(bf16[64,128]{1,0:T(8,128)(2,1)S(1)} %convolution_convert_fusion.1), channel_id=1, source_target_pairs={{0,3},{1,2},{2,1},{3,0},{4,7},{5,6},{6,5},{7,4},{8,11},{9,10},{10,... | collective-permute-start | bytes 49160 | tf_op jit(solution)/shard_map/tail/ppermute | solution.py:54
  194.7 6.5 %collective-permute-start.20 = (bf16[64,128]{1,0:T(8,128)(2,1)S(1)}, bf16[64,128]{1,0:T(8,128)(2,1)S(1)}, u32[]{:S(2)}, u32[]{:S(2)}) collective-permute-start(bf16[64,128]{1,0:T(8,128)(2,1)S(1)} %convolution_convert_fusion.1), channel_id=1, source_target_pairs={{0,2},{1,3},{2,0},{3,1},{4,6},{5,7},{6,4},{7,5},{8,10},{9,11},{10,... | collective-permute-start | bytes 49160 | tf_op jit(solution)/shard_map/tail/ppermute | solution.py:54
  195.5 5.7 %collective-permute-start.19 = (bf16[64,128]{1,0:T(8,128)(2,1)S(1)}, bf16[64,128]{1,0:T(8,128)(2,1)S(1)}, u32[]{:S(2)}, u32[]{:S(2)}) collective-permute-start(bf16[64,128]{1,0:T(8,128)(2,1)S(1)} %convolution_convert_fusion.1), channel_id=1, source_target_pairs={{0,1},{1,0},{2,3},{3,2},{4,5},{5,4},{6,7},{7,6},{8,9},{9,8},{10,11... | collective-permute-start | bytes 49160 | tf_op jit(solution)/shard_map/tail/ppermute | solution.py:54
  202.6 13.7 %all-to-all-start.3 = ((f32[64,1,128]{2,1,0:T(1,128)}), f32[64,1,128]{2,1,0:T(1,128)S(1)}, u32[]{:S(2)}, u32[]{:S(2)}) async-start(f32[64,1,128]{2,1,0:T(1,128)} %bitcast.27), calls=%async_computation.3 | async-start | bytes 65536 | tf_op jit(solution)/shard_map/tail/all_to_all | solution.py:267
  (17 other events, 84.2 us)
Sparse Core Ops, SparseCore 0:
  25.4 70.0 all-gather.1

commit v4 on v2

--- a/solution.py
+++ b/solution.py
@@ -234,8 +234,8 @@
         )
         line = lax.dynamic_slice_in_dim(from_everyone(line, ("zl", "c")), 4 * core, 4, 0)
         every = from_everyone(line, ("y", "x"))
-        every, mixed_0, mixed_1 = lax.optimization_barrier((every, mixed_0, mixed_1))
         head_out = owned(mixed_0, mixed_1)
+        every, head_out = lax.optimization_barrier((every, head_out))
         every = every.reshape(16, 2, 2, 4, width)
         last = every[:, :, :, :2].reshape(16, 2, 4, width)
         last = jnp.concatenate(

time: 209 us -> 209 us (level)
    all_to_all x1 -> x2, waiting for transfers between devices: 4.97 us -> 11.6 us  [from_everyone(): lax.all_to_all(jnp.broadcast_to(value[None], (count, *value.shape)), axis...]
    all_to_all x1 -> x0, starting transfers between devices: 4.59 us -> none  [per_device(): lax.all_to_all(packed[:, None], DP, 0, 0, tiled=True)]
    all_to_all x1 -> x2, starting transfers between devices: 6.23 us -> 10.4 us  [from_everyone(): lax.all_to_all(jnp.broadcast_to(value[None], (count, *value.shape)), axis...]
    all_to_all x1 -> x0, waiting for transfers between devices: 3.51 us -> none  [per_device(): lax.all_to_all(packed[:, None], DP, 0, 0, tiled=True)]
    ppermute x4, waiting for transfers between devices: 9.96 us -> 7.52 us  [send(): return lax.ppermute(value, ('zl', 'c'), pairs)]
  transfers between devices with their start and end apart: 26 -> 26, of which waited for: 15 -> 12; matrix products, arithmetic and copies ran while one was open for 16% -> 17% of each run, Pallas kernels for 1% -> 1%
where the time goes in v4:
time: 209 us; the launch traced here: 208 us
  waiting for transfers between devices  67.9 us (32%)
  starting transfers between devices  61.9 us (30%)
  other arithmetic  22.5 us (11%)
  between operations  17.7 us (8%)
  matrix products  16 us (8%)
  blocking collectives  13.9 us (7%)
  local copies, waits for them, and re-layouts  5.4 us (3%)
  Pallas kernels  2.63 us (1%)
    ppermute x6, waiting for transfers between devices, along(): return lax.ppermute(value, ('zl', 'zh'), pairs)  26.7 us
    ppermute x4, waiting for transfers between devices, to_column_owners(): got.append(lax.ppermute(value, ('zl', *MP), pairs))  17.9 us
    ppermute x4, starting transfers between devices, send(): return lax.ppermute(value, ('zl', 'c'), pairs)  14.6 us
    all_to_all x1, blocking collectives, per_device(): lax.all_to_all(packed[:, None], DP, 0, 0, tiled=True)  13.9 us
    reduce_sum x7, other arithmetic, scaled(): done = ((t * g).astype(BF16), jnp.sum(t * t, axis=1, keepdims=True))  13.7 us
    dot_general x8, matrix products, project(): return (jnp.dot(block, weight, preferred_element_type=F32), square)  12.3 us
    all_to_all x2, waiting for transfers between devices, from_everyone(): lax.all_to_all(jnp.broadcast_to(value[None], (count, *value.shape)), axis...  11.6 us
    all_to_all x2, starting transfers between devices, from_everyone(): lax.all_to_all(jnp.broadcast_to(value[None], (count, *value.shape)), axis...  10.4 us
  transfers between devices with their start and end apart: 26, of which 12 were waited for; matrix products, arithmetic and copies ran while one was open for 17% of the time, Pallas kernels for 1%

profile of v4, /device:TPU:1, one launch (start us, length us, event | category | flops | bytes accessed | tf_op | source)
XLA Modules:
  0.0 208.0 jit_solution(3376445993451655134)
XLA Ops:
  9.2 6.3 %collective-permute-start.11 = (bf16[128,768]{1,0:T(8,128)(2,1)S(1)}, bf16[128,768]{1,0:T(8,128)(2,1)S(1)}, u32[]{:S(2)}, u32[]{:S(2)}) collective-permute-start(bf16[128,768]{1,0:T(8,128)(2,1)S(1)} %get-tuple-element.110), channel_id=1, source_target_pairs={{0,0},{1,128},{64,1},{65,129},{128,64},{129,192},{192,65},{193,193... | collective-permute-start | bytes 589832 | tf_op jit(solution)/shard_map/weights/ppermute | solution.py:34
  16.9 2.6 %collective-permute-done.11 = bf16[128,768]{1,0:T(8,128)(2,1)S(1)} collective-permute-done((bf16[128,768]{1,0:T(8,128)(2,1)S(1)}, bf16[128,768]{1,0:T(8,128)(2,1)S(1)}, u32[]{:S(2)}, u32[]{:S(2)}) %collective-permute-start.11) | collective-permute-done | bytes 196640 | tf_op jit(solution)/shard_map/weights/ppermute | solution.py:34
  19.5 4.9 %collective-permute-done.12 = bf16[128,768]{1,0:T(8,128)(2,1)S(1)} collective-permute-done((bf16[128,768]{1,0:T(8,128)(2,1)S(1)}, bf16[128,768]{1,0:T(8,128)(2,1)S(1)}, u32[]{:S(2)}, u32[]{:S(2)}) %collective-permute-start.12) | collective-permute-done | bytes 196640 | tf_op jit(solution)/shard_map/weights/ppermute | solution.py:34
  25.3 4.4 %collective-permute-start = (bf16[256,2048]{1,0:T(8,128)(2,1)S(1)}, bf16[256,2048]{1,0:T(8,128)(2,1)S(1)}, u32[]{:S(2)}, u32[]{:S(2)}) collective-permute-start(bf16[256,2048]{1,0:T(8,128)(2,1)S(1)} %copy-done.3), channel_id=1, source_target_pairs={{0,194},{64,0},{128,64},{192,128},{2,192},{66,2},{130,66},{194,130... | collective-permute-start | bytes 3145736 | tf_op jit(solution)/shard_map/direction/ppermute | solution.py:40
  29.9 3.1 %fusion.41 = bf16[8,8,16,128]{3,1,2,0:T(8,128)(2,1)S(1)} fusion(bf16[1002,2048]{1,0:T(8,128)(2,1)} %param.17, s32[1002]{0:T(1024)S(1)} %iota_add_fusion, s32[64]{0:T(128)S(1)} %copy-done.10, s32[64]{0:T(128)S(1)} %copy-done.11), kind=kOutput, calls=%fused_computation.52 | convolution fusion | flops 263184128 | bytes 4370856 | tf_op jit(solution)/shard_map/direction/dot_general | solution.py:159
  34.1 8.5 %all-to-all-start = ((bf16[64,17,128]{2,1,0:T(8,128)(2,1)}), bf16[64,17,128]{2,1,0:T(8,128)(2,1)S(1)}, u32[]{:S(2)}, u32[]{:S(2)}) async-start(bf16[64,17,128]{2,1,0:T(8,128)(2,1)} %pad_maximum_fusion.1), calls=%async_computation | async-start | bytes 786432 | tf_op jit(solution)/shard_map/direction/all_to_all | solution.py:164
  44.2 8.0 %collective-permute-done = bf16[256,2048]{1,0:T(8,128)(2,1)S(1)} collective-permute-done((bf16[256,2048]{1,0:T(8,128)(2,1)S(1)}, bf16[256,2048]{1,0:T(8,128)(2,1)S(1)}, u32[]{:S(2)}, u32[]{:S(2)}) %collective-permute-start) | collective-permute-done | bytes 1048608 | tf_op jit(solution)/shard_map/direction/ppermute | solution.py:40
  52.2 3.5 %collective-permute-start.1 = (bf16[256,2048]{1,0:T(8,128)(2,1)S(1)}, bf16[256,2048]{1,0:T(8,128)(2,1)}, u32[]{:S(2)}, u32[]{:S(2)}) collective-permute-start(bf16[256,2048]{1,0:T(8,128)(2,1)S(1)} %collective-permute-done), channel_id=1, source_target_pairs={{0,194},{64,0},{128,64},{192,128},{2,192},{66,2},{130,66},{194,130... | collective-permute-start | bytes 3145736 | tf_op jit(solution)/shard_map/direction/ppermute | solution.py:40
  58.7 2.6 %fusion.27 = (f32[256]{0:T(256)S(1)}, bf16[256,2048]{1,0:T(8,128)(2,1)}) fusion(bf16[256,2048]{1,0:T(8,128)(2,1)} %collective-permute-done.2, f32[2048]{0:T(1024)S(1)} %get-tuple-element.117), kind=kLoop, calls=%fused_computation.44 | loop fusion | flops 2621184 | bytes 2106368 | tf_op jit(solution)/shard_map/project/reduce_sum | solution.py:192
  62.5 16.2 %collective-permute-done.1 = bf16[256,2048]{1,0:T(8,128)(2,1)} collective-permute-done((bf16[256,2048]{1,0:T(8,128)(2,1)S(1)}, bf16[256,2048]{1,0:T(8,128)(2,1)}, u32[]{:S(2)}, u32[]{:S(2)}) %collective-permute-start.1) | collective-permute-done | bytes 1048608 | tf_op jit(solution)/shard_map/direction/ppermute | solution.py:40
  78.7 2.5 %collective-permute-done.3 = bf16[256,2048]{1,0:T(8,128)(2,1)} collective-permute-done((bf16[256,2048]{1,0:T(8,128)(2,1)}, bf16[256,2048]{1,0:T(8,128)(2,1)}, u32[]{:S(2)}, u32[]{:S(2)}) %collective-permute-start.3) | collective-permute-done | bytes 1048608 | tf_op jit(solution)/shard_map/direction/ppermute | solution.py:40
  81.5 1.8 collective-permute-start.9
  83.4 2.4 %collective-permute-start.7 = (f32[2,16,128]{2,1,0:T(8,128)S(1)}, f32[2,16,128]{2,1,0:T(8,128)S(1)}, u32[]{:S(2)}, u32[]{:S(2)}) collective-permute-start(f32[2,16,128]{2,1,0:T(8,128)S(1)} %pad_maximum_fusion.13), channel_id=1, source_target_pairs={{0,3},{1,67},{2,131},{3,195},{64,0},{65,64},{66,128},{67,192},{128... | collective-permute-start | bytes 49160 | tf_op jit(solution)/shard_map/direction/ppermute | solution.py:47
  85.8 3.4 %collective-permute-start.6 = (f32[2,16,128]{2,1,0:T(8,128)S(1)}, f32[2,16,128]{2,1,0:T(8,128)S(1)}, u32[]{:S(2)}, u32[]{:S(2)}) collective-permute-start(f32[2,16,128]{2,1,0:T(8,128)S(1)} %pad_maximum_fusion.13), channel_id=1, source_target_pairs={{0,2},{1,66},{2,130},{3,194},{64,3},{65,67},{66,131},{67,195},{128... | collective-permute-start | bytes 49160 | tf_op jit(solution)/shard_map/direction/ppermute | solution.py:47
  89.3 2.5 %fusion.21 = (f32[256]{0:T(256)S(1)}, bf16[256,2048]{1,0:T(8,128)(2,1)}) fusion(bf16[256,2048]{1,0:T(8,128)(2,1)} %collective-permute-done.3, f32[2048]{0:T(1024)S(1)} %get-tuple-element.120), kind=kLoop, calls=%fused_computation.38 | loop fusion | flops 2621184 | bytes 2106368 | tf_op jit(solution)/shard_map/project/reduce_sum | solution.py:192
  91.8 17.6 %collective-permute-done.7 = f32[2,16,128]{2,1,0:T(8,128)S(1)} collective-permute-done((f32[2,16,128]{2,1,0:T(8,128)S(1)}, f32[2,16,128]{2,1,0:T(8,128)S(1)}, u32[]{:S(2)}, u32[]{:S(2)}) %collective-permute-start.7) | collective-permute-done | bytes 16416 | tf_op jit(solution)/shard_map/direction/ppermute | solution.py:47
  109.4 1.9 collective-permute-start.4
  111.3 2.5 %fusion.19 = (f32[256]{0:T(256)S(1)}, bf16[256,2048]{1,0:T(8,128)(2,1)}) fusion(bf16[256,2048]{1,0:T(8,128)(2,1)} %collective-permute-done.1, f32[2048]{0:T(1024)S(1)} %get-tuple-element.121), kind=kLoop, calls=%fused_computation.36 | loop fusion | flops 2621184 | bytes 2106368 | tf_op jit(solution)/shard_map/project/reduce_sum | solution.py:192
  115.6 1.9 fusion.25
  117.8 1.9 collective-permute-start.14
  120.8 3.3 %fusion.6 = f32[256,768]{1,0:T(8,128)S(1)} fusion(bf16[256,2048]{1,0:T(8,128)(2,1)} %get-tuple-element.47, bf16[2048,1536]{1,0:T(8,128)(2,1)} %all-gather.2.cloned.1.call-done, s32[]{:T(128)S(6)} %select_n.292), kind=kOutput, calls=%fused_computation.6 | convolution fusion | flops 805306368 | bytes 4980740 | tf_op jit(solution)/shard_map/project/dot_general | solution.py:197
  124.2 3.0 %fusion.2 = f32[256,768]{1,0:T(8,128)S(1)} fusion(bf16[256,2048]{1,0:T(8,128)(2,1)S(1)} %copy-done.8, bf16[2048,1536]{1,0:T(8,128)(2,1)} %all-gather.2.cloned.1.call-done, s32[]{:T(128)S(6)} %select_n.300), kind=kOutput, calls=%fused_computation.2 | convolution fusion | flops 805306368 | bytes 4980740 | tf_op jit(solution)/shard_map/project/dot_general | solution.py:197
  139.1 4.6 %collective-permute-start.18 = (bf16[256,512]{1,0:T(8,128)(2,1)S(1)}, bf16[256,512]{1,0:T(8,128)(2,1)S(1)}, u32[]{:S(2)}, u32[]{:S(2)}) collective-permute-start(bf16[256,512]{1,0:T(8,128)(2,1)S(1)} %get-tuple-element.64), channel_id=1, source_target_pairs={{0,64},{1,192},{64,128},{65,0},{128,193},{129,65},{192,1},{193,129... | collective-permute-start | bytes 786440 | tf_op jit(solution)/shard_map/tail/ppermute | solution.py:34
  145.0 2.3 %collective-permute-start.17 = (bf16[256,512]{1,0:T(8,128)(2,1)S(1)}, bf16[256,512]{1,0:T(8,128)(2,1)S(1)}, u32[]{:S(2)}, u32[]{:S(2)}) collective-permute-start(bf16[256,512]{1,0:T(8,128)(2,1)S(1)} %get-tuple-element.63), channel_id=1, source_target_pairs={{0,0},{1,128},{64,64},{65,192},{128,129},{129,1},{192,193},{193,65... | collective-permute-start | bytes 786440 | tf_op jit(solution)/shard_map/tail/ppermute | solution.py:34
  148.0 3.7 %all-to-all-start.1 = ((bf16[8,4,512]{2,1,0:T(4,128)(2,1)}), bf16[8,4,512]{2,1,0:T(4,128)(2,1)S(1)}, u32[]{:S(2)}, u32[]{:S(2)}) async-start(bf16[8,4,512]{2,1,0:T(4,128)(2,1)} %broadcast_in_dim.113), calls=%async_computation.1 | async-start | bytes 65536 | tf_op jit(solution)/shard_map/tail/all_to_all | solution.py:23
  151.6 5.0 %all-to-all-done.1 = bf16[8,4,512]{2,1,0:T(4,128)(2,1)S(1)} async-done(((bf16[8,4,512]{2,1,0:T(4,128)(2,1)}), bf16[8,4,512]{2,1,0:T(4,128)(2,1)S(1)}, u32[]{:S(2)}, u32[]{:S(2)}) %all-to-all-start.1) | async-done | bytes 32800 | tf_op jit(solution)/shard_map/tail/all_to_all | solution.py:23
  157.4 6.8 %all-to-all-start.2 = ((bf16[16,4,4,512]{3,2,1,0:T(4,128)(2,1)}), bf16[16,4,4,512]{3,2,1,0:T(4,128)(2,1)S(1)}, u32[]{:S(2)}, u32[]{:S(2)}) async-start(bf16[16,4,4,512]{3,2,1,0:T(4,128)(2,1)} %broadcast_in_dim.114), calls=%async_computation.2 | async-start | bytes 524288 | tf_op jit(solution)/shard_map/tail/all_to_all | solution.py:23
  165.1 6.6 %all-to-all-done.2 = bf16[16,4,4,512]{3,2,1,0:T(4,128)(2,1)S(1)} async-done(((bf16[16,4,4,512]{3,2,1,0:T(4,128)(2,1)}), bf16[16,4,4,512]{3,2,1,0:T(4,128)(2,1)S(1)}, u32[]{:S(2)}, u32[]{:S(2)}) %all-to-all-start.2) | async-done | bytes 262176 | tf_op jit(solution)/shard_map/tail/all_to_all | solution.py:23
  172.2 4.0 %collective-permute-start.21 = (bf16[64,128]{1,0:T(8,128)(2,1)S(1)}, bf16[64,128]{1,0:T(8,128)(2,1)S(1)}, u32[]{:S(2)}, u32[]{:S(2)}) collective-permute-start(bf16[64,128]{1,0:T(8,128)(2,1)S(1)} %convolution_convert_fusion.1), channel_id=1, source_target_pairs={{0,3},{1,2},{2,1},{3,0},{4,7},{5,6},{6,5},{7,4},{8,11},{9,10},{10,... | collective-permute-start | bytes 49160 | tf_op jit(solution)/shard_map/tail/ppermute | solution.py:54
  176.2 3.5 %collective-permute-start.20 = (bf16[64,128]{1,0:T(8,128)(2,1)S(1)}, bf16[64,128]{1,0:T(8,128)(2,1)S(1)}, u32[]{:S(2)}, u32[]{:S(2)}) collective-permute-start(bf16[64,128]{1,0:T(8,128)(2,1)S(1)} %convolution_convert_fusion.1), channel_id=1, source_target_pairs={{0,2},{1,3},{2,0},{3,1},{4,6},{5,7},{6,4},{7,5},{8,10},{9,11},{10,... | collective-permute-start | bytes 49160 | tf_op jit(solution)/shard_map/tail/ppermute | solution.py:54
  180.2 2.5 %collective-permute-done.20 = bf16[64,128]{1,0:T(8,128)(2,1)S(1)} collective-permute-done((bf16[64,128]{1,0:T(8,128)(2,1)S(1)}, bf16[64,128]{1,0:T(8,128)(2,1)S(1)}, u32[]{:S(2)}, u32[]{:S(2)}) %collective-permute-start.20) | collective-permute-done | bytes 16416 | tf_op jit(solution)/shard_map/tail/ppermute | solution.py:54
  183.5 13.9 %all_to_all.20 = f32[64,1,128]{2,1,0:T(1,128)S(1)} all-to-all(f32[64,1,128]{2,1,0:T(1,128)S(1)} %bitcast.85), channel_id=1, replica_groups=mesh['zl'=4,'y'=4,'x'=4,'zh'=2,'c'=2] {'zl','y','x'}, dimensions={0} | all-to-all | bytes 65536 | tf_op jit(solution)/shard_map/tail/all_to_all | solution.py:269
  (144 shorter events, 32.6 us)
Async XLA Ops:
  7.2 112.6 %copy-start = (bf16[1024,128]{1,0:T(8,128)(2,1)S(1)}, bf16[1024,128]{1,0:T(8,128)(2,1)}, u32[]{:S(2)}) copy-start(bf16[1024,128]{1,0:T(8,128)(2,1)} %param.15) | copy-start | bytes 786436
  7.2 18.1 %copy-start.3 = (bf16[256,2048]{1,0:T(8,128)(2,1)S(1)}, bf16[256,2048]{1,0:T(8,128)(2,1)}, u32[]{:S(2)}) copy-start(bf16[256,2048]{1,0:T(8,128)(2,1)} %param.10) | copy-start | bytes 3145732
  7.2 22.7 %copy-start.10 = (s32[64]{0:T(128)S(1)}, s32[64]{0:T(128)}, u32[]{:S(2)}) copy-start(s32[64]{0:T(128)} %param.19) | copy-start | bytes 772
  7.2 22.7 %copy-start.11 = (s32[64]{0:T(128)S(1)}, s32[64]{0:T(128)}, u32[]{:S(2)}) copy-start(s32[64]{0:T(128)} %param.18) | copy-start | bytes 772
  7.2 113.6 %all-gather.2.cloned.1.call-start = ((), (), s32[]{:S(2)}) async-start(), calls=%async_computation.4 | async-start | bytes 6684672 | tf_op jit(solution)/shard_map/weights/all_gather | solution.py:151
  9.2 10.3 %collective-permute-start.11 = (bf16[128,768]{1,0:T(8,128)(2,1)S(1)}, bf16[128,768]{1,0:T(8,128)(2,1)S(1)}, u32[]{:S(2)}, u32[]{:S(2)}) collective-permute-start(bf16[128,768]{1,0:T(8,128)(2,1)S(1)} %get-tuple-element.110), channel_id=1, source_target_pairs={{0,0},{1,128},{64,1},{65,129},{128,64},{129,192},{192,65},{193,193... | collective-permute-start | bytes 589832 | tf_op jit(solution)/shard_map/weights/ppermute | solution.py:34
  15.5 9.0 %collective-permute-start.12 = (bf16[128,768]{1,0:T(8,128)(2,1)S(1)}, bf16[128,768]{1,0:T(8,128)(2,1)S(1)}, u32[]{:S(2)}, u32[]{:S(2)}) collective-permute-start(bf16[128,768]{1,0:T(8,128)(2,1)S(1)} %get-tuple-element.111), channel_id=1, source_target_pairs={{0,64},{1,192},{64,65},{65,193},{128,0},{129,128},{192,1},{193,129... | collective-permute-start | bytes 589832 | tf_op jit(solution)/shard_map/weights/ppermute | solution.py:34
  25.3 26.9 %collective-permute-start = (bf16[256,2048]{1,0:T(8,128)(2,1)S(1)}, bf16[256,2048]{1,0:T(8,128)(2,1)S(1)}, u32[]{:S(2)}, u32[]{:S(2)}) collective-permute-start(bf16[256,2048]{1,0:T(8,128)(2,1)S(1)} %copy-done.3), channel_id=1, source_target_pairs={{0,194},{64,0},{128,64},{192,128},{2,192},{66,2},{130,66},{194,130... | collective-permute-start | bytes 3145736 | tf_op jit(solution)/shard_map/direction/ppermute | solution.py:40
  29.7 26.1 %collective-permute-start.2 = (bf16[256,2048]{1,0:T(8,128)(2,1)S(1)}, bf16[256,2048]{1,0:T(8,128)(2,1)}, u32[]{:S(2)}, u32[]{:S(2)}) collective-permute-start(bf16[256,2048]{1,0:T(8,128)(2,1)S(1)} %copy-done.3), channel_id=1, source_target_pairs={{0,64},{64,128},{128,192},{192,2},{2,66},{66,130},{130,194},{194,0... | collective-permute-start | bytes 3145736 | tf_op jit(solution)/shard_map/direction/ppermute | solution.py:40
  29.9 13.0 %copy-start.9 = (bf16[8192]{0:T(1024)(128)(2,1)S(1)}, bf16[8192]{0:T(1024)(128)(2,1)}, u32[]{:S(2)}) copy-start(bf16[8192]{0:T(1024)(128)(2,1)} %param.11) | copy-start | bytes 49156
  34.1 28.4 %all-to-all-start = ((bf16[64,17,128]{2,1,0:T(8,128)(2,1)}), bf16[64,17,128]{2,1,0:T(8,128)(2,1)S(1)}, u32[]{:S(2)}, u32[]{:S(2)}) async-start(bf16[64,17,128]{2,1,0:T(8,128)(2,1)} %pad_maximum_fusion.1), calls=%async_computation | async-start | bytes 786432 | tf_op jit(solution)/shard_map/direction/all_to_all | solution.py:164
  52.2 26.4 %collective-permute-start.1 = (bf16[256,2048]{1,0:T(8,128)(2,1)S(1)}, bf16[256,2048]{1,0:T(8,128)(2,1)}, u32[]{:S(2)}, u32[]{:S(2)}) collective-permute-start(bf16[256,2048]{1,0:T(8,128)(2,1)S(1)} %collective-permute-done), channel_id=1, source_target_pairs={{0,194},{64,0},{128,64},{192,128},{2,192},{66,2},{130,66},{194,130... | collective-permute-start | bytes 3145736 | tf_op jit(solution)/shard_map/direction/ppermute | solution.py:40
  55.7 25.4 %collective-permute-start.3 = (bf16[256,2048]{1,0:T(8,128)(2,1)}, bf16[256,2048]{1,0:T(8,128)(2,1)}, u32[]{:S(2)}, u32[]{:S(2)}) collective-permute-start(bf16[256,2048]{1,0:T(8,128)(2,1)} %collective-permute-done.2), channel_id=1, source_target_pairs={{0,64},{64,128},{128,192},{192,2},{2,66},{66,130},{130,194},{194,0... | collective-permute-start | bytes 3145736 | tf_op jit(solution)/shard_map/direction/ppermute | solution.py:40
  81.1 33.3 %collective-permute-start.8 = (bf16[256,2048]{1,0:T(8,128)(2,1)}, bf16[256,2048]{1,0:T(8,128)(2,1)S(1)}, u32[]{:S(2)}, u32[]{:S(2)}) collective-permute-start(bf16[256,2048]{1,0:T(8,128)(2,1)} %collective-permute-done.1), channel_id=1, source_target_pairs={{0,194},{64,0},{128,64},{192,128},{2,192},{66,2},{130,66},{194,130... | collective-permute-start | bytes 3145736 | tf_op jit(solution)/shard_map/direction/ppermute | solution.py:40
  81.5 32.9 %collective-permute-start.9 = (bf16[256,2048]{1,0:T(8,128)(2,1)}, bf16[256,2048]{1,0:T(8,128)(2,1)S(1)}, u32[]{:S(2)}, u32[]{:S(2)}) collective-permute-start(bf16[256,2048]{1,0:T(8,128)(2,1)} %collective-permute-done.3), channel_id=1, source_target_pairs={{0,64},{64,128},{128,192},{192,2},{2,66},{66,130},{130,194},{194,0... | collective-permute-start | bytes 3145736 | tf_op jit(solution)/shard_map/direction/ppermute | solution.py:40
  83.4 25.9 %collective-permute-start.7 = (f32[2,16,128]{2,1,0:T(8,128)S(1)}, f32[2,16,128]{2,1,0:T(8,128)S(1)}, u32[]{:S(2)}, u32[]{:S(2)}) collective-permute-start(f32[2,16,128]{2,1,0:T(8,128)S(1)} %pad_maximum_fusion.13), channel_id=1, source_target_pairs={{0,3},{1,67},{2,131},{3,195},{64,0},{65,64},{66,128},{67,192},{128... | collective-permute-start | bytes 49160 | tf_op jit(solution)/shard_map/direction/ppermute | solution.py:47
  85.8 28.2 %collective-permute-start.6 = (f32[2,16,128]{2,1,0:T(8,128)S(1)}, f32[2,16,128]{2,1,0:T(8,128)S(1)}, u32[]{:S(2)}, u32[]{:S(2)}) collective-permute-start(f32[2,16,128]{2,1,0:T(8,128)S(1)} %pad_maximum_fusion.13), channel_id=1, source_target_pairs={{0,2},{1,66},{2,130},{3,194},{64,3},{65,67},{66,131},{67,195},{128... | collective-permute-start | bytes 49160 | tf_op jit(solution)/shard_map/direction/ppermute | solution.py:47
  89.3 24.8 %collective-permute-start.5 = (f32[2,16,128]{2,1,0:T(8,128)S(1)}, f32[2,16,128]{2,1,0:T(8,128)S(1)}, u32[]{:S(2)}, u32[]{:S(2)}) collective-permute-start(f32[2,16,128]{2,1,0:T(8,128)S(1)} %pad_maximum_fusion.13), channel_id=1, source_target_pairs={{0,1},{1,65},{2,129},{3,193},{64,2},{65,66},{66,130},{67,194},{128... | collective-permute-start | bytes 49160 | tf_op jit(solution)/shard_map/direction/ppermute | solution.py:47
  109.4 5.0 %collective-permute-start.4 = (f32[2,16,128]{2,1,0:T(8,128)S(1)}, f32[2,16,128]{2,1,0:T(8,128)S(1)}, u32[]{:S(2)}, u32[]{:S(2)}) collective-permute-start(f32[2,16,128]{2,1,0:T(8,128)S(1)} %pad_maximum_fusion.13), channel_id=1, source_target_pairs={{0,0},{1,64},{2,128},{3,192},{64,1},{65,65},{66,129},{67,193},{128... | collective-permute-start | bytes 49160 | tf_op jit(solution)/shard_map/direction/ppermute | solution.py:47
  115.6 18.9 %collective-permute-start.10 = (bf16[256,2048]{1,0:T(8,128)(2,1)}, bf16[256,2048]{1,0:T(8,128)(2,1)}, u32[]{:S(2)}, u32[]{:S(2)}) collective-permute-start(bf16[256,2048]{1,0:T(8,128)(2,1)} %broadcast_select_fusion), channel_id=1, source_target_pairs={{0,64},{1,195},{64,128},{65,1},{128,192},{129,65},{192,2},{193,129... | collective-permute-start | bytes 3145736 | tf_op jit(solution)/shard_map/direction/ppermute | solution.py:123
  117.8 2.9 %collective-permute-start.14 = (f32[256,1]{1,0:T(8,128)S(1)}, f32[256,1]{1,0:T(8,128)S(1)}, u32[]{:S(2)}, u32[]{:S(2)}) collective-permute-start(f32[256,1]{1,0:T(8,128)S(1)} %broadcast_select_fusion.11), channel_id=1, source_target_pairs={{0,1},{1,0},{2,3},{3,2},{4,5},{5,4},{6,7},{7,6},{8,9},{9,8},{10,11... | collective-permute-start | bytes 3080 | tf_op jit(solution)/shard_map/project/ppermute | solution.py:60
  120.8 6.3 %copy-start.2 = (bf16[2048,1536]{1,0:T(8,128)(2,1)S(1)}, bf16[2048,1536]{1,0:T(8,128)(2,1)}, u32[]{:S(2)}) copy-start(bf16[2048,1536]{1,0:T(8,128)(2,1)} %all-gather.2.cloned.1.call-done) | copy-start | bytes 18874372
  129.5 3.7 %collective-permute-start.13 = (f32[256,768]{1,0:T(8,128)S(1)}, f32[256,768]{1,0:T(8,128)S(1)}, u32[]{:S(2)}, u32[]{:S(2)}) collective-permute-start(f32[256,768]{1,0:T(8,128)S(1)} %get-tuple-element.76), channel_id=1, source_target_pairs={{0,1},{1,0},{2,3},{3,2},{4,5},{5,4},{6,7},{7,6},{8,9},{9,8},{10,11... | collective-permute-start | bytes 2359304 | tf_op jit(solution)/shard_map/project/ppermute | solution.py:60
  138.1 5.5 %collective-permute-start.15 = (f32[256,768]{1,0:T(8,128)}, f32[256,768]{1,0:T(8,128)S(1)}, u32[]{:S(2)}, u32[]{:S(2)}) collective-permute-start(f32[256,768]{1,0:T(8,128)} %get-tuple-element.74), channel_id=1, source_target_pairs={{0,1},{1,0},{2,3},{3,2},{4,5},{5,4},{6,7},{7,6},{8,9},{9,8},{10,11... | collective-permute-start | bytes 2359304 | tf_op jit(solution)/shard_map/project/ppermute | solution.py:60
  138.6 5.0 %collective-permute-start.16 = (f32[256,1]{1,0:T(8,128)S(1)}, f32[256,1]{1,0:T(8,128)S(1)}, u32[]{:S(2)}, u32[]{:S(2)}) collective-permute-start(f32[256,1]{1,0:T(8,128)S(1)} %broadcast_select_fusion.10), channel_id=1, source_target_pairs={{0,1},{1,0},{2,3},{3,2},{4,5},{5,4},{6,7},{7,6},{8,9},{9,8},{10,11... | collective-permute-start | bytes 3080 | tf_op jit(solution)/shard_map/project/ppermute | solution.py:60
  139.1 25.1 %collective-permute-start.18 = (bf16[256,512]{1,0:T(8,128)(2,1)S(1)}, bf16[256,512]{1,0:T(8,128)(2,1)S(1)}, u32[]{:S(2)}, u32[]{:S(2)}) collective-permute-start(bf16[256,512]{1,0:T(8,128)(2,1)S(1)} %get-tuple-element.64), channel_id=1, source_target_pairs={{0,64},{1,192},{64,128},{65,0},{128,193},{129,65},{192,1},{193,129... | collective-permute-start | bytes 786440 | tf_op jit(solution)/shard_map/tail/ppermute | solution.py:34
  145.0 19.2 %collective-permute-start.17 = (bf16[256,512]{1,0:T(8,128)(2,1)S(1)}, bf16[256,512]{1,0:T(8,128)(2,1)S(1)}, u32[]{:S(2)}, u32[]{:S(2)}) collective-permute-start(bf16[256,512]{1,0:T(8,128)(2,1)S(1)} %get-tuple-element.63), channel_id=1, source_target_pairs={{0,0},{1,128},{64,64},{65,192},{128,129},{129,1},{192,193},{193,65... | collective-permute-start | bytes 786440 | tf_op jit(solution)/shard_map/tail/ppermute | solution.py:34
  148.0 8.6 %all-to-all-start.1 = ((bf16[8,4,512]{2,1,0:T(4,128)(2,1)}), bf16[8,4,512]{2,1,0:T(4,128)(2,1)S(1)}, u32[]{:S(2)}, u32[]{:S(2)}) async-start(bf16[8,4,512]{2,1,0:T(4,128)(2,1)} %broadcast_in_dim.113), calls=%async_computation.1 | async-start | bytes 65536 | tf_op jit(solution)/shard_map/tail/all_to_all | solution.py:23
  157.4 14.3 %all-to-all-start.2 = ((bf16[16,4,4,512]{3,2,1,0:T(4,128)(2,1)}), bf16[16,4,4,512]{3,2,1,0:T(4,128)(2,1)S(1)}, u32[]{:S(2)}, u32[]{:S(2)}) async-start(bf16[16,4,4,512]{3,2,1,0:T(4,128)(2,1)} %broadcast_in_dim.114), calls=%async_computation.2 | async-start | bytes 524288 | tf_op jit(solution)/shard_map/tail/all_to_all | solution.py:23
  172.2 8.0 %collective-permute-start.21 = (bf16[64,128]{1,0:T(8,128)(2,1)S(1)}, bf16[64,128]{1,0:T(8,128)(2,1)S(1)}, u32[]{:S(2)}, u32[]{:S(2)}) collective-permute-start(bf16[64,128]{1,0:T(8,128)(2,1)S(1)} %convolution_convert_fusion.1), channel_id=1, source_target_pairs={{0,3},{1,2},{2,1},{3,0},{4,7},{5,6},{6,5},{7,4},{8,11},{9,10},{10,... | collective-permute-start | bytes 49160 | tf_op jit(solution)/shard_map/tail/ppermute | solution.py:54
  176.2 6.5 %collective-permute-start.20 = (bf16[64,128]{1,0:T(8,128)(2,1)S(1)}, bf16[64,128]{1,0:T(8,128)(2,1)S(1)}, u32[]{:S(2)}, u32[]{:S(2)}) collective-permute-start(bf16[64,128]{1,0:T(8,128)(2,1)S(1)} %convolution_convert_fusion.1), channel_id=1, source_target_pairs={{0,2},{1,3},{2,0},{3,1},{4,6},{5,7},{6,4},{7,5},{8,10},{9,11},{10,... | collective-permute-start | bytes 49160 | tf_op jit(solution)/shard_map/tail/ppermute | solution.py:54
  179.7 3.0 %collective-permute-start.19 = (bf16[64,128]{1,0:T(8,128)(2,1)S(1)}, bf16[64,128]{1,0:T(8,128)(2,1)S(1)}, u32[]{:S(2)}, u32[]{:S(2)}) collective-permute-start(bf16[64,128]{1,0:T(8,128)(2,1)S(1)} %convolution_convert_fusion.1), channel_id=1, source_target_pairs={{0,1},{1,0},{2,3},{3,2},{4,5},{5,4},{6,7},{7,6},{8,9},{9,8},{10,11... | collective-permute-start | bytes 49160 | tf_op jit(solution)/shard_map/tail/ppermute | solution.py:54
  (6 other events, 12.6 us)
Sparse Core Ops, SparseCore 0:
  25.4 70.3 all-gather.1

commit v5 on v4

--- a/solution.py
+++ b/solution.py
@@ -227,28 +227,18 @@
             )
 
     with jax.named_scope("tail"):
-        total = total_0 + total_1
-        high = lax.reduce_precision(total, 8, 7)
-        line = jnp.concatenate(
-            [mixed_0[-1:], mixed_1[-1:], high.astype(BF16), (total - high).astype(BF16)], axis=0
-        )
-        line = lax.dynamic_slice_in_dim(from_everyone(line, ("zl", "c")), 4 * core, 4, 0)
-        every = from_everyone(line, ("y", "x"))
+        own = owned(
+            jnp.concatenate([mixed_0[-1:], total_0.astype(BF16)], axis=0),
+            jnp.concatenate([mixed_1[-1:], total_1.astype(BF16)], axis=0),
+        )
+        own, mixed_0 = lax.optimization_barrier((own, mixed_0))
+        every = from_everyone(own, DP)
         head_out = owned(mixed_0, mixed_1)
         every, head_out = lax.optimization_barrier((every, head_out))
-        every = every.reshape(16, 2, 2, 4, width)
-        last = every[:, :, :, :2].reshape(16, 2, 4, width)
-        last = jnp.concatenate(
-            [
-                jnp.where(first, jnp.roll(last[:, h], h, axis=1), jnp.roll(last[:, h], h + 2, axis=1))
-                for h in (0, 1)
-            ],
-            axis=2,
-        )
-        last = last.swapaxes(0, 1).reshape(64, 2 * width)
+        last = every[:, 0]
         part = jnp.dot(last, w_out, preferred_element_type=F32).astype(BF16)
         attn_last = sum_over_mp(part).astype(BF16)
-        head_mean = jnp.sum(every[:, :, :, 2:].astype(F32), axis=(0, 2, 3)).reshape(-1) / TOKENS
+        head_mean = jnp.sum(every[:, 1].astype(F32), axis=0) / TOKENS
         gap = head_mean[None] - last.astype(F32)
 
         def per_head(grads):

time: 209 us -> 212 us (1.014)
    ppermute x4 -> x6, starting transfers between devices: 14.6 us -> 18.8 us  [send(): return lax.ppermute(value, ('zl', 'c'), pairs)]
    ppermute x4 -> x6, waiting for transfers between devices: 7.52 us -> 9.22 us  [send(): return lax.ppermute(value, ('zl', 'c'), pairs)]
    all_to_all x2 -> x1, starting transfers between devices: 10.4 us -> 8.86 us  [from_everyone(): lax.all_to_all(jnp.broadcast_to(value[None], (count, *value.shape)), axis...]
    all_to_all x2 -> x1, waiting for transfers between devices: 11.6 us -> 11.3 us  [from_everyone(): lax.all_to_all(jnp.broadcast_to(value[None], (count, *value.shape)), axis...]
  transfers between devices with their start and end apart: 26 -> 27, of which waited for: 12 -> 12; matrix products, arithmetic and copies ran while one was open for 17% -> 16% of each run, Pallas kernels for 1% -> 1%
where the time goes in v5:
time: 212 us; the launch traced here: 211 us
  waiting for transfers between devices  69.7 us (33%)
  starting transfers between devices  63.6 us (30%)
  other arithmetic  22.7 us (11%)
  between operations  17.7 us (8%)
  matrix products  16 us (8%)
  blocking collectives  13.8 us (7%)
  local copies, waits for them, and re-layouts  4.69 us (2%)
  Pallas kernels  2.63 us (1%)
    ppermute x6, waiting for transfers between devices, along(): return lax.ppermute(value, ('zl', 'zh'), pairs)  26.7 us
    ppermute x6, starting transfers between devices, send(): return lax.ppermute(value, ('zl', 'c'), pairs)  18.8 us
    ppermute x4, waiting for transfers between devices, to_column_owners(): got.append(lax.ppermute(value, ('zl', *MP), pairs))  17.9 us
    all_to_all x1, blocking collectives, per_device(): lax.all_to_all(packed[:, None], DP, 0, 0, tiled=True)  13.8 us
    reduce_sum x7, other arithmetic, scaled(): done = ((t * g).astype(BF16), jnp.sum(t * t, axis=1, keepdims=True))  13.7 us
    dot_general x8, matrix products, project(): return (jnp.dot(block, weight, preferred_element_type=F32), square)  12.3 us
    all_to_all x1, waiting for transfers between devices, from_everyone(): lax.all_to_all(jnp.broadcast_to(value[None], (count, *value.shape)), axis...  11.3 us
    ppermute x6, starting transfers between devices, along(): return lax.ppermute(value, ('zl', 'zh'), pairs)  10.1 us
  transfers between devices with their start and end apart: 27, of which 12 were waited for; matrix products, arithmetic and copies ran while one was open for 16% of the time, Pallas kernels for 1%

profile of v5, /device:TPU:1, one launch (start us, length us, event | category | flops | bytes accessed | tf_op | source)
XLA Modules:
  0.0 210.7 jit_solution(12435065761021551136)
XLA Ops:
  9.2 6.3 %collective-permute-start.11 = (bf16[128,768]{1,0:T(8,128)(2,1)S(1)}, bf16[128,768]{1,0:T(8,128)(2,1)S(1)}, u32[]{:S(2)}, u32[]{:S(2)}) collective-permute-start(bf16[128,768]{1,0:T(8,128)(2,1)S(1)} %get-tuple-element.106), channel_id=1, source_target_pairs={{0,0},{1,128},{64,1},{65,129},{128,64},{129,192},{192,65},{193,193... | collective-permute-start | bytes 589832 | tf_op jit(solution)/shard_map/weights/ppermute | solution.py:34
  16.9 2.6 %collective-permute-done.11 = bf16[128,768]{1,0:T(8,128)(2,1)S(1)} collective-permute-done((bf16[128,768]{1,0:T(8,128)(2,1)S(1)}, bf16[128,768]{1,0:T(8,128)(2,1)S(1)}, u32[]{:S(2)}, u32[]{:S(2)}) %collective-permute-start.11) | collective-permute-done | bytes 196640 | tf_op jit(solution)/shard_map/weights/ppermute | solution.py:34
  19.5 4.9 %collective-permute-done.12 = bf16[128,768]{1,0:T(8,128)(2,1)S(1)} collective-permute-done((bf16[128,768]{1,0:T(8,128)(2,1)S(1)}, bf16[128,768]{1,0:T(8,128)(2,1)S(1)}, u32[]{:S(2)}, u32[]{:S(2)}) %collective-permute-start.12) | collective-permute-done | bytes 196640 | tf_op jit(solution)/shard_map/weights/ppermute | solution.py:34
  25.3 4.4 %collective-permute-start = (bf16[256,2048]{1,0:T(8,128)(2,1)S(1)}, bf16[256,2048]{1,0:T(8,128)(2,1)S(1)}, u32[]{:S(2)}, u32[]{:S(2)}) collective-permute-start(bf16[256,2048]{1,0:T(8,128)(2,1)S(1)} %copy-done.3), channel_id=1, source_target_pairs={{0,194},{64,0},{128,64},{192,128},{2,192},{66,2},{130,66},{194,130... | collective-permute-start | bytes 3145736 | tf_op jit(solution)/shard_map/direction/ppermute | solution.py:40
  29.9 3.1 %fusion.41 = bf16[8,8,16,128]{3,1,2,0:T(8,128)(2,1)S(1)} fusion(bf16[1002,2048]{1,0:T(8,128)(2,1)} %param.17, s32[1002]{0:T(1024)S(1)} %iota_add_fusion, s32[64]{0:T(128)S(1)} %copy-done.10, s32[64]{0:T(128)S(1)} %copy-done.11), kind=kOutput, calls=%fused_computation.52 | convolution fusion | flops 263184128 | bytes 4370856 | tf_op jit(solution)/shard_map/direction/dot_general | solution.py:159
  34.1 8.5 %all-to-all-start = ((bf16[64,17,128]{2,1,0:T(8,128)(2,1)}), bf16[64,17,128]{2,1,0:T(8,128)(2,1)S(1)}, u32[]{:S(2)}, u32[]{:S(2)}) async-start(bf16[64,17,128]{2,1,0:T(8,128)(2,1)} %pad_maximum_fusion.1), calls=%async_computation | async-start | bytes 786432 | tf_op jit(solution)/shard_map/direction/all_to_all | solution.py:164
  44.2 8.0 %collective-permute-done = bf16[256,2048]{1,0:T(8,128)(2,1)S(1)} collective-permute-done((bf16[256,2048]{1,0:T(8,128)(2,1)S(1)}, bf16[256,2048]{1,0:T(8,128)(2,1)S(1)}, u32[]{:S(2)}, u32[]{:S(2)}) %collective-permute-start) | collective-permute-done | bytes 1048608 | tf_op jit(solution)/shard_map/direction/ppermute | solution.py:40
  52.2 3.5 %collective-permute-start.1 = (bf16[256,2048]{1,0:T(8,128)(2,1)S(1)}, bf16[256,2048]{1,0:T(8,128)(2,1)}, u32[]{:S(2)}, u32[]{:S(2)}) collective-permute-start(bf16[256,2048]{1,0:T(8,128)(2,1)S(1)} %collective-permute-done), channel_id=1, source_target_pairs={{0,194},{64,0},{128,64},{192,128},{2,192},{66,2},{130,66},{194,130... | collective-permute-start | bytes 3145736 | tf_op jit(solution)/shard_map/direction/ppermute | solution.py:40
  58.6 2.6 %fusion.27 = (f32[256]{0:T(256)S(1)}, bf16[256,2048]{1,0:T(8,128)(2,1)}) fusion(bf16[256,2048]{1,0:T(8,128)(2,1)} %collective-permute-done.2, f32[2048]{0:T(1024)S(1)} %get-tuple-element.113), kind=kLoop, calls=%fused_computation.44 | loop fusion | flops 2621184 | bytes 2106368 | tf_op jit(solution)/shard_map/project/reduce_sum | solution.py:192
  62.5 16.2 %collective-permute-done.1 = bf16[256,2048]{1,0:T(8,128)(2,1)} collective-permute-done((bf16[256,2048]{1,0:T(8,128)(2,1)S(1)}, bf16[256,2048]{1,0:T(8,128)(2,1)}, u32[]{:S(2)}, u32[]{:S(2)}) %collective-permute-start.1) | collective-permute-done | bytes 1048608 | tf_op jit(solution)/shard_map/direction/ppermute | solution.py:40
  78.7 2.5 %collective-permute-done.3 = bf16[256,2048]{1,0:T(8,128)(2,1)} collective-permute-done((bf16[256,2048]{1,0:T(8,128)(2,1)}, bf16[256,2048]{1,0:T(8,128)(2,1)}, u32[]{:S(2)}, u32[]{:S(2)}) %collective-permute-start.3) | collective-permute-done | bytes 1048608 | tf_op jit(solution)/shard_map/direction/ppermute | solution.py:40
  81.5 1.8 collective-permute-start.9
  83.4 2.4 %collective-permute-start.7 = (f32[2,16,128]{2,1,0:T(8,128)S(1)}, f32[2,16,128]{2,1,0:T(8,128)S(1)}, u32[]{:S(2)}, u32[]{:S(2)}) collective-permute-start(f32[2,16,128]{2,1,0:T(8,128)S(1)} %pad_maximum_fusion.12), channel_id=1, source_target_pairs={{0,3},{1,67},{2,131},{3,195},{64,0},{65,64},{66,128},{67,192},{128... | collective-permute-start | bytes 49160 | tf_op jit(solution)/shard_map/direction/ppermute | solution.py:47
  85.8 3.4 %collective-permute-start.6 = (f32[2,16,128]{2,1,0:T(8,128)S(1)}, f32[2,16,128]{2,1,0:T(8,128)S(1)}, u32[]{:S(2)}, u32[]{:S(2)}) collective-permute-start(f32[2,16,128]{2,1,0:T(8,128)S(1)} %pad_maximum_fusion.12), channel_id=1, source_target_pairs={{0,2},{1,66},{2,130},{3,194},{64,3},{65,67},{66,131},{67,195},{128... | collective-permute-start | bytes 49160 | tf_op jit(solution)/shard_map/direction/ppermute | solution.py:47
  89.3 2.5 %fusion.21 = (f32[256]{0:T(256)S(1)}, bf16[256,2048]{1,0:T(8,128)(2,1)}) fusion(bf16[256,2048]{1,0:T(8,128)(2,1)} %collective-permute-done.3, f32[2048]{0:T(1024)S(1)} %get-tuple-element.116), kind=kLoop, calls=%fused_computation.38 | loop fusion | flops 2621184 | bytes 2106368 | tf_op jit(solution)/shard_map/project/reduce_sum | solution.py:192
  91.8 17.6 %collective-permute-done.7 = f32[2,16,128]{2,1,0:T(8,128)S(1)} collective-permute-done((f32[2,16,128]{2,1,0:T(8,128)S(1)}, f32[2,16,128]{2,1,0:T(8,128)S(1)}, u32[]{:S(2)}, u32[]{:S(2)}) %collective-permute-start.7) | collective-permute-done | bytes 16416 | tf_op jit(solution)/shard_map/direction/ppermute | solution.py:47
  109.4 1.9 collective-permute-start.4
  111.3 2.5 %fusion.19 = (f32[256]{0:T(256)S(1)}, bf16[256,2048]{1,0:T(8,128)(2,1)}) fusion(bf16[256,2048]{1,0:T(8,128)(2,1)} %collective-permute-done.1, f32[2048]{0:T(1024)S(1)} %get-tuple-element.117), kind=kLoop, calls=%fused_computation.36 | loop fusion | flops 2621184 | bytes 2106368 | tf_op jit(solution)/shard_map/project/reduce_sum | solution.py:192
  115.6 1.9 fusion.25
  117.8 2.0 collective-permute-start.14
  120.8 3.3 %fusion.6 = f32[256,768]{1,0:T(8,128)S(1)} fusion(bf16[256,2048]{1,0:T(8,128)(2,1)} %get-tuple-element.49, bf16[2048,1536]{1,0:T(8,128)(2,1)} %all-gather.2.cloned.1.call-done, s32[]{:T(128)S(6)} %select_n.290), kind=kOutput, calls=%fused_computation.6 | convolution fusion | flops 805306368 | bytes 4980740 | tf_op jit(solution)/shard_map/project/dot_general | solution.py:197
  124.2 3.0 %fusion.2 = f32[256,768]{1,0:T(8,128)S(1)} fusion(bf16[256,2048]{1,0:T(8,128)(2,1)S(1)} %copy-done.8, bf16[2048,1536]{1,0:T(8,128)(2,1)} %all-gather.2.cloned.1.call-done, s32[]{:T(128)S(6)} %select_n.298), kind=kOutput, calls=%fused_computation.2 | convolution fusion | flops 805306368 | bytes 4980740 | tf_op jit(solution)/shard_map/project/dot_general | solution.py:197
  139.1 4.6 %collective-permute-start.18 = (bf16[2,512]{1,0:T(2,128)(2,1)S(1)}, bf16[2,512]{1,0:T(2,128)(2,1)S(1)}, u32[]{:S(2)}, u32[]{:S(2)}) collective-permute-start(bf16[2,512]{1,0:T(2,128)(2,1)S(1)} %pad_maximum_fusion.15), channel_id=1, source_target_pairs={{0,64},{1,192},{64,128},{65,0},{128,193},{129,65},{192,1},{193,129... | collective-permute-start | bytes 6152 | tf_op jit(solution)/shard_map/tail/ppermute | solution.py:34
  145.1 2.3 %collective-permute-start.17 = (bf16[2,512]{1,0:T(2,128)(2,1)S(1)}, bf16[2,512]{1,0:T(2,128)(2,1)S(1)}, u32[]{:S(2)}, u32[]{:S(2)}) collective-permute-start(bf16[2,512]{1,0:T(2,128)(2,1)S(1)} %pad_maximum_fusion.14), channel_id=1, source_target_pairs={{0,0},{1,128},{64,64},{65,192},{128,129},{129,1},{192,193},{193,65... | collective-permute-start | bytes 6152 | tf_op jit(solution)/shard_map/tail/ppermute | solution.py:34
  148.8 1.7 collective-permute-done.17
  150.5 2.8 %collective-permute-start.19 = (bf16[256,512]{1,0:T(8,128)(2,1)S(1)}, bf16[256,512]{1,0:T(8,128)(2,1)S(1)}, u32[]{:S(2)}, u32[]{:S(2)}) collective-permute-start(bf16[256,512]{1,0:T(8,128)(2,1)S(1)} %get-tuple-element.70), channel_id=1, source_target_pairs={{0,0},{1,128},{64,64},{65,192},{128,129},{129,1},{192,193},{193,65... | collective-permute-start | bytes 786440 | tf_op jit(solution)/shard_map/tail/ppermute | solution.py:34
  154.1 8.9 %all-to-all-start.1 = ((bf16[64,2,1024]{2,1,0:T(2,128)(2,1)}), bf16[64,2,1024]{2,1,0:T(2,128)(2,1)S(1)}, u32[]{:S(2)}, u32[]{:S(2)}) async-start(bf16[64,2,1024]{2,1,0:T(2,128)(2,1)} %broadcast_in_dim.107), calls=%async_computation.1 | async-start | bytes 524288 | tf_op jit(solution)/shard_map/tail/all_to_all | solution.py:23
  163.9 11.3 %all-to-all-done.1 = bf16[64,2,1024]{2,1,0:T(2,128)(2,1)S(1)} async-done(((bf16[64,2,1024]{2,1,0:T(2,128)(2,1)}), bf16[64,2,1024]{2,1,0:T(2,128)(2,1)S(1)}, u32[]{:S(2)}, u32[]{:S(2)}) %all-to-all-start.1) | async-done | bytes 262176 | tf_op jit(solution)/shard_map/tail/all_to_all | solution.py:23
  175.5 3.6 %collective-permute-start.23 = (bf16[64,128]{1,0:T(8,128)(2,1)S(1)}, bf16[64,128]{1,0:T(8,128)(2,1)S(1)}, u32[]{:S(2)}, u32[]{:S(2)}) collective-permute-start(bf16[64,128]{1,0:T(8,128)(2,1)S(1)} %convolution_convert_fusion.1), channel_id=1, source_target_pairs={{0,3},{1,2},{2,1},{3,0},{4,7},{5,6},{6,5},{7,4},{8,11},{9,10},{10,... | collective-permute-start | bytes 49160 | tf_op jit(solution)/shard_map/tail/ppermute | solution.py:54
  179.1 3.0 %collective-permute-start.22 = (bf16[64,128]{1,0:T(8,128)(2,1)S(1)}, bf16[64,128]{1,0:T(8,128)(2,1)S(1)}, u32[]{:S(2)}, u32[]{:S(2)}) collective-permute-start(bf16[64,128]{1,0:T(8,128)(2,1)S(1)} %convolution_convert_fusion.1), channel_id=1, source_target_pairs={{0,2},{1,3},{2,0},{3,1},{4,6},{5,7},{6,4},{7,5},{8,10},{9,11},{10,... | collective-permute-start | bytes 49160 | tf_op jit(solution)/shard_map/tail/ppermute | solution.py:54
  182.8 2.8 %collective-permute-done.22 = bf16[64,128]{1,0:T(8,128)(2,1)S(1)} collective-permute-done((bf16[64,128]{1,0:T(8,128)(2,1)S(1)}, bf16[64,128]{1,0:T(8,128)(2,1)S(1)}, u32[]{:S(2)}, u32[]{:S(2)}) %collective-permute-start.22) | collective-permute-done | bytes 16416 | tf_op jit(solution)/shard_map/tail/ppermute | solution.py:54
  186.4 13.8 %all_to_all.15 = f32[64,1,128]{2,1,0:T(1,128)S(1)} all-to-all(f32[64,1,128]{2,1,0:T(1,128)S(1)} %bitcast.70), channel_id=1, replica_groups=mesh['zl'=4,'y'=4,'x'=4,'zh'=2,'c'=2] {'zl','y','x'}, dimensions={0} | all-to-all | bytes 65536 | tf_op jit(solution)/shard_map/tail/all_to_all | solution.py:259
  (139 shorter events, 33.5 us)
Async XLA Ops:
  7.2 112.6 %copy-start = (bf16[1024,128]{1,0:T(8,128)(2,1)S(1)}, bf16[1024,128]{1,0:T(8,128)(2,1)}, u32[]{:S(2)}) copy-start(bf16[1024,128]{1,0:T(8,128)(2,1)} %param.15) | copy-start | bytes 786436
  7.2 18.1 %copy-start.3 = (bf16[256,2048]{1,0:T(8,128)(2,1)S(1)}, bf16[256,2048]{1,0:T(8,128)(2,1)}, u32[]{:S(2)}) copy-start(bf16[256,2048]{1,0:T(8,128)(2,1)} %param.10) | copy-start | bytes 3145732
  7.2 22.7 %copy-start.10 = (s32[64]{0:T(128)S(1)}, s32[64]{0:T(128)}, u32[]{:S(2)}) copy-start(s32[64]{0:T(128)} %param.19) | copy-start | bytes 772
  7.2 22.7 %copy-start.11 = (s32[64]{0:T(128)S(1)}, s32[64]{0:T(128)}, u32[]{:S(2)}) copy-start(s32[64]{0:T(128)} %param.18) | copy-start | bytes 772
  7.2 113.6 %all-gather.2.cloned.1.call-start = ((), (), s32[]{:S(2)}) async-start(), calls=%async_computation.3 | async-start | bytes 6684672 | tf_op jit(solution)/shard_map/weights/all_gather | solution.py:151
  9.2 10.3 %collective-permute-start.11 = (bf16[128,768]{1,0:T(8,128)(2,1)S(1)}, bf16[128,768]{1,0:T(8,128)(2,1)S(1)}, u32[]{:S(2)}, u32[]{:S(2)}) collective-permute-start(bf16[128,768]{1,0:T(8,128)(2,1)S(1)} %get-tuple-element.106), channel_id=1, source_target_pairs={{0,0},{1,128},{64,1},{65,129},{128,64},{129,192},{192,65},{193,193... | collective-permute-start | bytes 589832 | tf_op jit(solution)/shard_map/weights/ppermute | solution.py:34
  15.5 9.0 %collective-permute-start.12 = (bf16[128,768]{1,0:T(8,128)(2,1)S(1)}, bf16[128,768]{1,0:T(8,128)(2,1)S(1)}, u32[]{:S(2)}, u32[]{:S(2)}) collective-permute-start(bf16[128,768]{1,0:T(8,128)(2,1)S(1)} %get-tuple-element.107), channel_id=1, source_target_pairs={{0,64},{1,192},{64,65},{65,193},{128,0},{129,128},{192,1},{193,129... | collective-permute-start | bytes 589832 | tf_op jit(solution)/shard_map/weights/ppermute | solution.py:34
  25.3 26.9 %collective-permute-start = (bf16[256,2048]{1,0:T(8,128)(2,1)S(1)}, bf16[256,2048]{1,0:T(8,128)(2,1)S(1)}, u32[]{:S(2)}, u32[]{:S(2)}) collective-permute-start(bf16[256,2048]{1,0:T(8,128)(2,1)S(1)} %copy-done.3), channel_id=1, source_target_pairs={{0,194},{64,0},{128,64},{192,128},{2,192},{66,2},{130,66},{194,130... | collective-permute-start | bytes 3145736 | tf_op jit(solution)/shard_map/direction/ppermute | solution.py:40
  29.7 26.1 %collective-permute-start.2 = (bf16[256,2048]{1,0:T(8,128)(2,1)S(1)}, bf16[256,2048]{1,0:T(8,128)(2,1)}, u32[]{:S(2)}, u32[]{:S(2)}) collective-permute-start(bf16[256,2048]{1,0:T(8,128)(2,1)S(1)} %copy-done.3), channel_id=1, source_target_pairs={{0,64},{64,128},{128,192},{192,2},{2,66},{66,130},{130,194},{194,0... | collective-permute-start | bytes 3145736 | tf_op jit(solution)/shard_map/direction/ppermute | solution.py:40
  29.9 13.0 %copy-start.9 = (bf16[8192]{0:T(1024)(128)(2,1)S(1)}, bf16[8192]{0:T(1024)(128)(2,1)}, u32[]{:S(2)}) copy-start(bf16[8192]{0:T(1024)(128)(2,1)} %param.11) | copy-start | bytes 49156
  34.1 28.4 %all-to-all-start = ((bf16[64,17,128]{2,1,0:T(8,128)(2,1)}), bf16[64,17,128]{2,1,0:T(8,128)(2,1)S(1)}, u32[]{:S(2)}, u32[]{:S(2)}) async-start(bf16[64,17,128]{2,1,0:T(8,128)(2,1)} %pad_maximum_fusion.1), calls=%async_computation | async-start | bytes 786432 | tf_op jit(solution)/shard_map/direction/all_to_all | solution.py:164
  52.2 26.4 %collective-permute-start.1 = (bf16[256,2048]{1,0:T(8,128)(2,1)S(1)}, bf16[256,2048]{1,0:T(8,128)(2,1)}, u32[]{:S(2)}, u32[]{:S(2)}) collective-permute-start(bf16[256,2048]{1,0:T(8,128)(2,1)S(1)} %collective-permute-done), channel_id=1, source_target_pairs={{0,194},{64,0},{128,64},{192,128},{2,192},{66,2},{130,66},{194,130... | collective-permute-start | bytes 3145736 | tf_op jit(solution)/shard_map/direction/ppermute | solution.py:40
  55.7 25.4 %collective-permute-start.3 = (bf16[256,2048]{1,0:T(8,128)(2,1)}, bf16[256,2048]{1,0:T(8,128)(2,1)}, u32[]{:S(2)}, u32[]{:S(2)}) collective-permute-start(bf16[256,2048]{1,0:T(8,128)(2,1)} %collective-permute-done.2), channel_id=1, source_target_pairs={{0,64},{64,128},{128,192},{192,2},{2,66},{66,130},{130,194},{194,0... | collective-permute-start | bytes 3145736 | tf_op jit(solution)/shard_map/direction/ppermute | solution.py:40
  81.1 33.3 %collective-permute-start.8 = (bf16[256,2048]{1,0:T(8,128)(2,1)}, bf16[256,2048]{1,0:T(8,128)(2,1)S(1)}, u32[]{:S(2)}, u32[]{:S(2)}) collective-permute-start(bf16[256,2048]{1,0:T(8,128)(2,1)} %collective-permute-done.1), channel_id=1, source_target_pairs={{0,194},{64,0},{128,64},{192,128},{2,192},{66,2},{130,66},{194,130... | collective-permute-start | bytes 3145736 | tf_op jit(solution)/shard_map/direction/ppermute | solution.py:40
  81.5 32.9 %collective-permute-start.9 = (bf16[256,2048]{1,0:T(8,128)(2,1)}, bf16[256,2048]{1,0:T(8,128)(2,1)S(1)}, u32[]{:S(2)}, u32[]{:S(2)}) collective-permute-start(bf16[256,2048]{1,0:T(8,128)(2,1)} %collective-permute-done.3), channel_id=1, source_target_pairs={{0,64},{64,128},{128,192},{192,2},{2,66},{66,130},{130,194},{194,0... | collective-permute-start | bytes 3145736 | tf_op jit(solution)/shard_map/direction/ppermute | solution.py:40
  83.4 25.9 %collective-permute-start.7 = (f32[2,16,128]{2,1,0:T(8,128)S(1)}, f32[2,16,128]{2,1,0:T(8,128)S(1)}, u32[]{:S(2)}, u32[]{:S(2)}) collective-permute-start(f32[2,16,128]{2,1,0:T(8,128)S(1)} %pad_maximum_fusion.12), channel_id=1, source_target_pairs={{0,3},{1,67},{2,131},{3,195},{64,0},{65,64},{66,128},{67,192},{128... | collective-permute-start | bytes 49160 | tf_op jit(solution)/shard_map/direction/ppermute | solution.py:47
  85.8 28.3 %collective-permute-start.6 = (f32[2,16,128]{2,1,0:T(8,128)S(1)}, f32[2,16,128]{2,1,0:T(8,128)S(1)}, u32[]{:S(2)}, u32[]{:S(2)}) collective-permute-start(f32[2,16,128]{2,1,0:T(8,128)S(1)} %pad_maximum_fusion.12), channel_id=1, source_target_pairs={{0,2},{1,66},{2,130},{3,194},{64,3},{65,67},{66,131},{67,195},{128... | collective-permute-start | bytes 49160 | tf_op jit(solution)/shard_map/direction/ppermute | solution.py:47
  89.3 24.8 %collective-permute-start.5 = (f32[2,16,128]{2,1,0:T(8,128)S(1)}, f32[2,16,128]{2,1,0:T(8,128)S(1)}, u32[]{:S(2)}, u32[]{:S(2)}) collective-permute-start(f32[2,16,128]{2,1,0:T(8,128)S(1)} %pad_maximum_fusion.12), channel_id=1, source_target_pairs={{0,1},{1,65},{2,129},{3,193},{64,2},{65,66},{66,130},{67,194},{128... | collective-permute-start | bytes 49160 | tf_op jit(solution)/shard_map/direction/ppermute | solution.py:47
  109.4 5.0 %collective-permute-start.4 = (f32[2,16,128]{2,1,0:T(8,128)S(1)}, f32[2,16,128]{2,1,0:T(8,128)S(1)}, u32[]{:S(2)}, u32[]{:S(2)}) collective-permute-start(f32[2,16,128]{2,1,0:T(8,128)S(1)} %pad_maximum_fusion.12), channel_id=1, source_target_pairs={{0,0},{1,64},{2,128},{3,192},{64,1},{65,65},{66,129},{67,193},{128... | collective-permute-start | bytes 49160 | tf_op jit(solution)/shard_map/direction/ppermute | solution.py:47
  115.6 18.9 %collective-permute-start.10 = (bf16[256,2048]{1,0:T(8,128)(2,1)}, bf16[256,2048]{1,0:T(8,128)(2,1)}, u32[]{:S(2)}, u32[]{:S(2)}) collective-permute-start(bf16[256,2048]{1,0:T(8,128)(2,1)} %broadcast_select_fusion), channel_id=1, source_target_pairs={{0,64},{1,195},{64,128},{65,1},{128,192},{129,65},{192,2},{193,129... | collective-permute-start | bytes 3145736 | tf_op jit(solution)/shard_map/direction/ppermute | solution.py:123
  117.8 2.9 %collective-permute-start.14 = (f32[256,1]{1,0:T(8,128)S(1)}, f32[256,1]{1,0:T(8,128)S(1)}, u32[]{:S(2)}, u32[]{:S(2)}) collective-permute-start(f32[256,1]{1,0:T(8,128)S(1)} %broadcast_select_fusion.11), channel_id=1, source_target_pairs={{0,1},{1,0},{2,3},{3,2},{4,5},{5,4},{6,7},{7,6},{8,9},{9,8},{10,11... | collective-permute-start | bytes 3080 | tf_op jit(solution)/shard_map/project/ppermute | solution.py:60
  129.5 3.7 %collective-permute-start.13 = (f32[256,768]{1,0:T(8,128)S(1)}, f32[256,768]{1,0:T(8,128)S(1)}, u32[]{:S(2)}, u32[]{:S(2)}) collective-permute-start(f32[256,768]{1,0:T(8,128)S(1)} %get-tuple-element.80), channel_id=1, source_target_pairs={{0,1},{1,0},{2,3},{3,2},{4,5},{5,4},{6,7},{7,6},{8,9},{9,8},{10,11... | collective-permute-start | bytes 2359304 | tf_op jit(solution)/shard_map/project/ppermute | solution.py:60
  138.2 5.6 %collective-permute-start.15 = (f32[256,768]{1,0:T(8,128)}, f32[256,768]{1,0:T(8,128)S(1)}, u32[]{:S(2)}, u32[]{:S(2)}) collective-permute-start(f32[256,768]{1,0:T(8,128)} %get-tuple-element.78), channel_id=1, source_target_pairs={{0,1},{1,0},{2,3},{3,2},{4,5},{5,4},{6,7},{7,6},{8,9},{9,8},{10,11... | collective-permute-start | bytes 2359304 | tf_op jit(solution)/shard_map/project/ppermute | solution.py:60
  138.6 5.1 %collective-permute-start.16 = (f32[256,1]{1,0:T(8,128)S(1)}, f32[256,1]{1,0:T(8,128)S(1)}, u32[]{:S(2)}, u32[]{:S(2)}) collective-permute-start(f32[256,1]{1,0:T(8,128)S(1)} %broadcast_select_fusion.10), channel_id=1, source_target_pairs={{0,1},{1,0},{2,3},{3,2},{4,5},{5,4},{6,7},{7,6},{8,9},{9,8},{10,11... | collective-permute-start | bytes 3080 | tf_op jit(solution)/shard_map/project/ppermute | solution.py:60
  139.1 9.7 %collective-permute-start.18 = (bf16[2,512]{1,0:T(2,128)(2,1)S(1)}, bf16[2,512]{1,0:T(2,128)(2,1)S(1)}, u32[]{:S(2)}, u32[]{:S(2)}) collective-permute-start(bf16[2,512]{1,0:T(2,128)(2,1)S(1)} %pad_maximum_fusion.15), channel_id=1, source_target_pairs={{0,64},{1,192},{64,128},{65,0},{128,193},{129,65},{192,1},{193,129... | collective-permute-start | bytes 6152 | tf_op jit(solution)/shard_map/tail/ppermute | solution.py:34
  145.1 5.3 %collective-permute-start.17 = (bf16[2,512]{1,0:T(2,128)(2,1)S(1)}, bf16[2,512]{1,0:T(2,128)(2,1)S(1)}, u32[]{:S(2)}, u32[]{:S(2)}) collective-permute-start(bf16[2,512]{1,0:T(2,128)(2,1)S(1)} %pad_maximum_fusion.14), channel_id=1, source_target_pairs={{0,0},{1,128},{64,64},{65,192},{128,129},{129,1},{192,193},{193,65... | collective-permute-start | bytes 6152 | tf_op jit(solution)/shard_map/tail/ppermute | solution.py:34
  147.4 15.6 %collective-permute-start.20 = (bf16[256,512]{1,0:T(8,128)(2,1)S(1)}, bf16[256,512]{1,0:T(8,128)(2,1)S(1)}, u32[]{:S(2)}, u32[]{:S(2)}) collective-permute-start(bf16[256,512]{1,0:T(8,128)(2,1)S(1)} %get-tuple-element.67), channel_id=1, source_target_pairs={{0,64},{1,192},{64,128},{65,0},{128,193},{129,65},{192,1},{193,129... | collective-permute-start | bytes 786440 | tf_op jit(solution)/shard_map/tail/ppermute | solution.py:34
  150.5 12.5 %collective-permute-start.19 = (bf16[256,512]{1,0:T(8,128)(2,1)S(1)}, bf16[256,512]{1,0:T(8,128)(2,1)S(1)}, u32[]{:S(2)}, u32[]{:S(2)}) collective-permute-start(bf16[256,512]{1,0:T(8,128)(2,1)S(1)} %get-tuple-element.70), channel_id=1, source_target_pairs={{0,0},{1,128},{64,64},{65,192},{128,129},{129,1},{192,193},{193,65... | collective-permute-start | bytes 786440 | tf_op jit(solution)/shard_map/tail/ppermute | solution.py:34
  154.1 21.1 %all-to-all-start.1 = ((bf16[64,2,1024]{2,1,0:T(2,128)(2,1)}), bf16[64,2,1024]{2,1,0:T(2,128)(2,1)S(1)}, u32[]{:S(2)}, u32[]{:S(2)}) async-start(bf16[64,2,1024]{2,1,0:T(2,128)(2,1)} %broadcast_in_dim.107), calls=%async_computation.1 | async-start | bytes 524288 | tf_op jit(solution)/shard_map/tail/all_to_all | solution.py:23
  175.5 7.2 %collective-permute-start.23 = (bf16[64,128]{1,0:T(8,128)(2,1)S(1)}, bf16[64,128]{1,0:T(8,128)(2,1)S(1)}, u32[]{:S(2)}, u32[]{:S(2)}) collective-permute-start(bf16[64,128]{1,0:T(8,128)(2,1)S(1)} %convolution_convert_fusion.1), channel_id=1, source_target_pairs={{0,3},{1,2},{2,1},{3,0},{4,7},{5,6},{6,5},{7,4},{8,11},{9,10},{10,... | collective-permute-start | bytes 49160 | tf_op jit(solution)/shard_map/tail/ppermute | solution.py:54
  179.1 6.5 %collective-permute-start.22 = (bf16[64,128]{1,0:T(8,128)(2,1)S(1)}, bf16[64,128]{1,0:T(8,128)(2,1)S(1)}, u32[]{:S(2)}, u32[]{:S(2)}) collective-permute-start(bf16[64,128]{1,0:T(8,128)(2,1)S(1)} %convolution_convert_fusion.1), channel_id=1, source_target_pairs={{0,2},{1,3},{2,0},{3,1},{4,6},{5,7},{6,4},{7,5},{8,10},{9,11},{10,... | collective-permute-start | bytes 49160 | tf_op jit(solution)/shard_map/tail/ppermute | solution.py:54
  182.1 3.5 %collective-permute-start.21 = (bf16[64,128]{1,0:T(8,128)(2,1)S(1)}, bf16[64,128]{1,0:T(8,128)(2,1)S(1)}, u32[]{:S(2)}, u32[]{:S(2)}) collective-permute-start(bf16[64,128]{1,0:T(8,128)(2,1)S(1)} %convolution_convert_fusion.1), channel_id=1, source_target_pairs={{0,1},{1,0},{2,3},{3,2},{4,5},{5,4},{6,7},{7,6},{8,9},{9,8},{10,11... | collective-permute-start | bytes 49160 | tf_op jit(solution)/shard_map/tail/ppermute | solution.py:54
  (7 other events, 18.9 us)
Sparse Core Ops, SparseCore 0:
  25.4 70.4 all-gather.1

commit v6 on v4

--- a/solution.py
+++ b/solution.py
@@ -121,6 +121,16 @@
         (place(z, c), place((z + 1 - 2 * c) % 8, c)) for z in range(8) for c in range(2)
     ]
     return lax.ppermute(value, ("zl", *MP), pairs)
+
+
+def to_line(value, zl):
+    got = []
+    for i in range(4):
+        got.append(send(value, lambda z, c: (2 * (z % 2) + c + i, z // 2)))
+    got = jnp.stack(got)
+    return jnp.stack(
+        [lax.dynamic_index_in_dim(got, (zl - q) % 4, 0, keepdims=False) for q in range(4)]
+    )
 
 
 def per_device(tokens, gain, w_query, w_key, w_value, w_out, final_gain, unembed, clean, corrupt):
@@ -232,7 +242,7 @@
         line = jnp.concatenate(
             [mixed_0[-1:], mixed_1[-1:], high.astype(BF16), (total - high).astype(BF16)], axis=0
         )
-        line = lax.dynamic_slice_in_dim(from_everyone(line, ("zl", "c")), 4 * core, 4, 0)
+        line, mixed_0 = lax.optimization_barrier((to_line(line, zl), mixed_0))
         every = from_everyone(line, ("y", "x"))
         head_out = owned(mixed_0, mixed_1)
         every, head_out = lax.optimization_barrier((every, head_out))

time: 209 us -> 211 us (level)
  waiting for transfers between devices: 67.9 us -> 64.8 us
  starting transfers between devices: 61.9 us -> 64.9 us
  blocking collectives: 13.9 us -> 16.3 us
    ppermute x4 -> x8, starting transfers between devices: 14.6 us -> 22.7 us  [send(): return lax.ppermute(value, ('zl', 'c'), pairs)]
    all_to_all x2 -> x1, waiting for transfers between devices: 11.6 us -> 4.15 us  [from_everyone(): lax.all_to_all(jnp.broadcast_to(value[None], (count, *value.shape)), axis...]
    ppermute x4 -> x8, waiting for transfers between devices: 7.52 us -> 12.3 us  [send(): return lax.ppermute(value, ('zl', 'c'), pairs)]
    all_to_all x2 -> x1, starting transfers between devices: 10.4 us -> 6.76 us  [from_everyone(): lax.all_to_all(jnp.broadcast_to(value[None], (count, *value.shape)), axis...]
    all_to_all x1, blocking collectives: 13.9 us -> 16.3 us  [per_device(): lax.all_to_all(packed[:, None], DP, 0, 0, tiled=True)]
  transfers between devices with their start and end apart: 26 -> 29, of which waited for: 12 -> 15; matrix products, arithmetic and copies ran while one was open for 17% -> 16% of each run, Pallas kernels for 1% -> 1%
where the time goes in v6:
time: 211 us; the launch traced here: 210 us
  starting transfers between devices  64.9 us (31%)
  waiting for transfers between devices  64.8 us (31%)
  other arithmetic  22.6 us (11%)
  between operations  17.8 us (8%)
  blocking collectives  16.3 us (8%)
  matrix products  16 us (8%)
  local copies, waits for them, and re-layouts  4.8 us (2%)
  Pallas kernels  2.63 us (1%)
    ppermute x6, waiting for transfers between devices, along(): return lax.ppermute(value, ('zl', 'zh'), pairs)  26.7 us
    ppermute x8, starting transfers between devices, send(): return lax.ppermute(value, ('zl', 'c'), pairs)  22.7 us
    ppermute x4, waiting for transfers between devices, to_column_owners(): got.append(lax.ppermute(value, ('zl', *MP), pairs))  17.8 us
    all_to_all x1, blocking collectives, per_device(): lax.all_to_all(packed[:, None], DP, 0, 0, tiled=True)  16.3 us
    reduce_sum x7, other arithmetic, scaled(): done = ((t * g).astype(BF16), jnp.sum(t * t, axis=1, keepdims=True))  13.8 us
    dot_general x8, matrix products, project(): return (jnp.dot(block, weight, preferred_element_type=F32), square)  12.3 us
    ppermute x8, waiting for transfers between devices, send(): return lax.ppermute(value, ('zl', 'c'), pairs)  12.3 us
    ppermute x6, starting transfers between devices, along(): return lax.ppermute(value, ('zl', 'zh'), pairs)  10.1 us
  transfers between devices with their start and end apart: 29, of which 15 were waited for; matrix products, arithmetic and copies ran while one was open for 16% of the time, Pallas kernels for 1%

profile of v6, /device:TPU:1, one launch (start us, length us, event | category | flops | bytes accessed | tf_op | source)
XLA Modules:
  0.0 209.9 jit_solution(583690858849347993)
XLA Ops:
  9.2 6.3 %collective-permute-start.11 = (bf16[128,768]{1,0:T(8,128)(2,1)S(1)}, bf16[128,768]{1,0:T(8,128)(2,1)S(1)}, u32[]{:S(2)}, u32[]{:S(2)}) collective-permute-start(bf16[128,768]{1,0:T(8,128)(2,1)S(1)} %get-tuple-element.114), channel_id=1, source_target_pairs={{0,0},{1,128},{64,1},{65,129},{128,64},{129,192},{192,65},{193,193... | collective-permute-start | bytes 589832 | tf_op jit(solution)/shard_map/weights/ppermute | solution.py:34
  16.9 2.6 %collective-permute-done.11 = bf16[128,768]{1,0:T(8,128)(2,1)S(1)} collective-permute-done((bf16[128,768]{1,0:T(8,128)(2,1)S(1)}, bf16[128,768]{1,0:T(8,128)(2,1)S(1)}, u32[]{:S(2)}, u32[]{:S(2)}) %collective-permute-start.11) | collective-permute-done | bytes 196640 | tf_op jit(solution)/shard_map/weights/ppermute | solution.py:34
  19.5 4.9 %collective-permute-done.12 = bf16[128,768]{1,0:T(8,128)(2,1)S(1)} collective-permute-done((bf16[128,768]{1,0:T(8,128)(2,1)S(1)}, bf16[128,768]{1,0:T(8,128)(2,1)S(1)}, u32[]{:S(2)}, u32[]{:S(2)}) %collective-permute-start.12) | collective-permute-done | bytes 196640 | tf_op jit(solution)/shard_map/weights/ppermute | solution.py:34
  25.3 4.4 %collective-permute-start = (bf16[256,2048]{1,0:T(8,128)(2,1)S(1)}, bf16[256,2048]{1,0:T(8,128)(2,1)S(1)}, u32[]{:S(2)}, u32[]{:S(2)}) collective-permute-start(bf16[256,2048]{1,0:T(8,128)(2,1)S(1)} %copy-done.3), channel_id=1, source_target_pairs={{0,194},{64,0},{128,64},{192,128},{2,192},{66,2},{130,66},{194,130... | collective-permute-start | bytes 3145736 | tf_op jit(solution)/shard_map/direction/ppermute | solution.py:40
  29.9 3.1 %fusion.41 = bf16[8,8,16,128]{3,1,2,0:T(8,128)(2,1)S(1)} fusion(bf16[1002,2048]{1,0:T(8,128)(2,1)} %param.17, s32[1002]{0:T(1024)S(1)} %iota_add_fusion, s32[64]{0:T(128)S(1)} %copy-done.10, s32[64]{0:T(128)S(1)} %copy-done.11), kind=kOutput, calls=%fused_computation.52 | convolution fusion | flops 263184128 | bytes 4370856 | tf_op jit(solution)/shard_map/direction/dot_general | solution.py:169
  34.1 8.5 %all-to-all-start = ((bf16[64,17,128]{2,1,0:T(8,128)(2,1)}), bf16[64,17,128]{2,1,0:T(8,128)(2,1)S(1)}, u32[]{:S(2)}, u32[]{:S(2)}) async-start(bf16[64,17,128]{2,1,0:T(8,128)(2,1)} %pad_maximum_fusion.1), calls=%async_computation | async-start | bytes 786432 | tf_op jit(solution)/shard_map/direction/all_to_all | solution.py:174
  44.2 8.0 %collective-permute-done = bf16[256,2048]{1,0:T(8,128)(2,1)S(1)} collective-permute-done((bf16[256,2048]{1,0:T(8,128)(2,1)S(1)}, bf16[256,2048]{1,0:T(8,128)(2,1)S(1)}, u32[]{:S(2)}, u32[]{:S(2)}) %collective-permute-start) | collective-permute-done | bytes 1048608 | tf_op jit(solution)/shard_map/direction/ppermute | solution.py:40
  52.2 3.5 %collective-permute-start.1 = (bf16[256,2048]{1,0:T(8,128)(2,1)S(1)}, bf16[256,2048]{1,0:T(8,128)(2,1)}, u32[]{:S(2)}, u32[]{:S(2)}) collective-permute-start(bf16[256,2048]{1,0:T(8,128)(2,1)S(1)} %collective-permute-done), channel_id=1, source_target_pairs={{0,194},{64,0},{128,64},{192,128},{2,192},{66,2},{130,66},{194,130... | collective-permute-start | bytes 3145736 | tf_op jit(solution)/shard_map/direction/ppermute | solution.py:40
  58.7 2.6 %fusion.27 = (f32[256]{0:T(256)S(1)}, bf16[256,2048]{1,0:T(8,128)(2,1)}) fusion(bf16[256,2048]{1,0:T(8,128)(2,1)} %collective-permute-done.2, f32[2048]{0:T(1024)S(1)} %get-tuple-element.125), kind=kLoop, calls=%fused_computation.44 | loop fusion | flops 2621184 | bytes 2106368 | tf_op jit(solution)/shard_map/project/reduce_sum | solution.py:202
  62.5 16.2 %collective-permute-done.1 = bf16[256,2048]{1,0:T(8,128)(2,1)} collective-permute-done((bf16[256,2048]{1,0:T(8,128)(2,1)S(1)}, bf16[256,2048]{1,0:T(8,128)(2,1)}, u32[]{:S(2)}, u32[]{:S(2)}) %collective-permute-start.1) | collective-permute-done | bytes 1048608 | tf_op jit(solution)/shard_map/direction/ppermute | solution.py:40
  78.7 2.5 %collective-permute-done.3 = bf16[256,2048]{1,0:T(8,128)(2,1)} collective-permute-done((bf16[256,2048]{1,0:T(8,128)(2,1)}, bf16[256,2048]{1,0:T(8,128)(2,1)}, u32[]{:S(2)}, u32[]{:S(2)}) %collective-permute-start.3) | collective-permute-done | bytes 1048608 | tf_op jit(solution)/shard_map/direction/ppermute | solution.py:40
  83.4 2.4 %collective-permute-start.7 = (f32[2,16,128]{2,1,0:T(8,128)S(1)}, f32[2,16,128]{2,1,0:T(8,128)S(1)}, u32[]{:S(2)}, u32[]{:S(2)}) collective-permute-start(f32[2,16,128]{2,1,0:T(8,128)S(1)} %pad_maximum_fusion.13), channel_id=1, source_target_pairs={{0,3},{1,67},{2,131},{3,195},{64,0},{65,64},{66,128},{67,192},{128... | collective-permute-start | bytes 49160 | tf_op jit(solution)/shard_map/direction/ppermute | solution.py:47
  85.8 3.4 %collective-permute-start.6 = (f32[2,16,128]{2,1,0:T(8,128)S(1)}, f32[2,16,128]{2,1,0:T(8,128)S(1)}, u32[]{:S(2)}, u32[]{:S(2)}) collective-permute-start(f32[2,16,128]{2,1,0:T(8,128)S(1)} %pad_maximum_fusion.13), channel_id=1, source_target_pairs={{0,2},{1,66},{2,130},{3,194},{64,3},{65,67},{66,131},{67,195},{128... | collective-permute-start | bytes 49160 | tf_op jit(solution)/shard_map/direction/ppermute | solution.py:47
  89.3 2.5 %fusion.21 = (f32[256]{0:T(256)S(1)}, bf16[256,2048]{1,0:T(8,128)(2,1)}) fusion(bf16[256,2048]{1,0:T(8,128)(2,1)} %collective-permute-done.3, f32[2048]{0:T(1024)S(1)} %get-tuple-element.128), kind=kLoop, calls=%fused_computation.38 | loop fusion | flops 2621184 | bytes 2106368 | tf_op jit(solution)/shard_map/project/reduce_sum | solution.py:202
  91.8 17.6 %collective-permute-done.7 = f32[2,16,128]{2,1,0:T(8,128)S(1)} collective-permute-done((f32[2,16,128]{2,1,0:T(8,128)S(1)}, f32[2,16,128]{2,1,0:T(8,128)S(1)}, u32[]{:S(2)}, u32[]{:S(2)}) %collective-permute-start.7) | collective-permute-done | bytes 16416 | tf_op jit(solution)/shard_map/direction/ppermute | solution.py:47
  109.4 1.9 collective-permute-start.4
  111.3 2.5 %fusion.19 = (f32[256]{0:T(256)S(1)}, bf16[256,2048]{1,0:T(8,128)(2,1)}) fusion(bf16[256,2048]{1,0:T(8,128)(2,1)} %collective-permute-done.1, f32[2048]{0:T(1024)S(1)} %get-tuple-element.129), kind=kLoop, calls=%fused_computation.36 | loop fusion | flops 2621184 | bytes 2106368 | tf_op jit(solution)/shard_map/project/reduce_sum | solution.py:202
  115.6 1.9 fusion.25
  117.8 2.0 collective-permute-start.14
  120.8 3.3 %fusion.6 = f32[256,768]{1,0:T(8,128)S(1)} fusion(bf16[256,2048]{1,0:T(8,128)(2,1)} %get-tuple-element.49, bf16[2048,1536]{1,0:T(8,128)(2,1)} %all-gather.2.cloned.1.call-done, s32[]{:T(128)S(6)} %select_n.318), kind=kOutput, calls=%fused_computation.6 | convolution fusion | flops 805306368 | bytes 4980740 | tf_op jit(solution)/shard_map/project/dot_general | solution.py:207
  124.2 3.0 %fusion.2 = f32[256,768]{1,0:T(8,128)S(1)} fusion(bf16[256,2048]{1,0:T(8,128)(2,1)S(1)} %copy-done.8, bf16[2048,1536]{1,0:T(8,128)(2,1)} %all-gather.2.cloned.1.call-done, s32[]{:T(128)S(6)} %select_n.326), kind=kOutput, calls=%fused_computation.2 | convolution fusion | flops 805306368 | bytes 4980740 | tf_op jit(solution)/shard_map/project/dot_general | solution.py:207
  142.0 2.1 collective-permute-start.20
  144.1 5.0 %collective-permute-start.19 = (bf16[4,512]{1,0:T(4,128)(2,1)S(1)}, bf16[4,512]{1,0:T(4,128)(2,1)S(1)}, u32[]{:S(2)}, u32[]{:S(2)}) collective-permute-start(bf16[4,512]{1,0:T(4,128)(2,1)S(1)} %pad_maximum_fusion.16), channel_id=1, source_target_pairs={{0,128},{1,192},{64,0},{65,64},{128,129},{129,193},{192,1},{193,65... | collective-permute-start | bytes 12296 | tf_op jit(solution)/shard_map/tail/ppermute | solution.py:34
  149.1 1.9 collective-permute-start.18
  151.0 3.4 %collective-permute-start.17 = (bf16[4,512]{1,0:T(4,128)(2,1)S(1)}, bf16[4,512]{1,0:T(4,128)(2,1)S(1)}, u32[]{:S(2)}, u32[]{:S(2)}) collective-permute-start(bf16[4,512]{1,0:T(4,128)(2,1)S(1)} %pad_maximum_fusion.16), channel_id=1, source_target_pairs={{0,0},{1,64},{64,128},{65,192},{128,1},{129,65},{192,129},{193,193... | collective-permute-start | bytes 12296 | tf_op jit(solution)/shard_map/tail/ppermute | solution.py:34
  157.0 2.5 %collective-permute-start.21 = (bf16[256,512]{1,0:T(8,128)(2,1)S(1)}, bf16[256,512]{1,0:T(8,128)(2,1)S(1)}, u32[]{:S(2)}, u32[]{:S(2)}) collective-permute-start(bf16[256,512]{1,0:T(8,128)(2,1)S(1)} %get-tuple-element.70), channel_id=1, source_target_pairs={{0,0},{1,128},{64,64},{65,192},{128,129},{129,1},{192,193},{193,65... | collective-permute-start | bytes 786440 | tf_op jit(solution)/shard_map/tail/ppermute | solution.py:34
  160.3 6.8 %all-to-all-start.1 = ((bf16[16,4,4,512]{3,2,1,0:T(4,128)(2,1)}), bf16[16,4,4,512]{3,2,1,0:T(4,128)(2,1)S(1)}, u32[]{:S(2)}, u32[]{:S(2)}) async-start(bf16[16,4,4,512]{3,2,1,0:T(4,128)(2,1)} %broadcast_in_dim.107), calls=%async_computation.1 | async-start | bytes 524288 | tf_op jit(solution)/shard_map/tail/all_to_all | solution.py:23
  167.0 2.5 %collective-permute-done.21 = bf16[256,512]{1,0:T(8,128)(2,1)S(1)} collective-permute-done((bf16[256,512]{1,0:T(8,128)(2,1)S(1)}, bf16[256,512]{1,0:T(8,128)(2,1)S(1)}, u32[]{:S(2)}, u32[]{:S(2)}) %collective-permute-start.21) | collective-permute-done | bytes 262176 | tf_op jit(solution)/shard_map/tail/ppermute | solution.py:34
  170.4 4.2 %all-to-all-done.1 = bf16[16,4,4,512]{3,2,1,0:T(4,128)(2,1)S(1)} async-done(((bf16[16,4,4,512]{3,2,1,0:T(4,128)(2,1)}), bf16[16,4,4,512]{3,2,1,0:T(4,128)(2,1)S(1)}, u32[]{:S(2)}, u32[]{:S(2)}) %all-to-all-start.1) | async-done | bytes 262176 | tf_op jit(solution)/shard_map/tail/all_to_all | solution.py:23
  175.3 2.9 %collective-permute-start.24 = (bf16[64,128]{1,0:T(8,128)(2,1)S(1)}, bf16[64,128]{1,0:T(8,128)(2,1)S(1)}, u32[]{:S(2)}, u32[]{:S(2)}) collective-permute-start(bf16[64,128]{1,0:T(8,128)(2,1)S(1)} %convolution_convert_fusion.1), channel_id=1, source_target_pairs={{0,2},{1,3},{2,0},{3,1},{4,6},{5,7},{6,4},{7,5},{8,10},{9,11},{10,... | collective-permute-start | bytes 49160 | tf_op jit(solution)/shard_map/tail/ppermute | solution.py:54
  178.1 3.0 %collective-permute-start.23 = (bf16[64,128]{1,0:T(8,128)(2,1)S(1)}, bf16[64,128]{1,0:T(8,128)(2,1)S(1)}, u32[]{:S(2)}, u32[]{:S(2)}) collective-permute-start(bf16[64,128]{1,0:T(8,128)(2,1)S(1)} %convolution_convert_fusion.1), channel_id=1, source_target_pairs={{0,1},{1,0},{2,3},{3,2},{4,5},{5,4},{6,7},{7,6},{8,9},{9,8},{10,11... | collective-permute-start | bytes 49160 | tf_op jit(solution)/shard_map/tail/ppermute | solution.py:54
  183.0 16.3 %all_to_all.15 = f32[64,1,128]{2,1,0:T(1,128)S(1)} all-to-all(f32[64,1,128]{2,1,0:T(1,128)S(1)} %bitcast.89), channel_id=1, replica_groups=mesh['zl'=4,'y'=4,'x'=4,'zh'=2,'c'=2] {'zl','y','x'}, dimensions={0} | all-to-all | bytes 65536 | tf_op jit(solution)/shard_map/tail/all_to_all | solution.py:279
  (151 shorter events, 38.6 us)
Async XLA Ops:
  7.2 112.6 %copy-start = (bf16[1024,128]{1,0:T(8,128)(2,1)S(1)}, bf16[1024,128]{1,0:T(8,128)(2,1)}, u32[]{:S(2)}) copy-start(bf16[1024,128]{1,0:T(8,128)(2,1)} %param.15) | copy-start | bytes 786436
  7.2 22.7 %copy-start.10 = (s32[64]{0:T(128)S(1)}, s32[64]{0:T(128)}, u32[]{:S(2)}) copy-start(s32[64]{0:T(128)} %param.19) | copy-start | bytes 772
  7.2 22.7 %copy-start.11 = (s32[64]{0:T(128)S(1)}, s32[64]{0:T(128)}, u32[]{:S(2)}) copy-start(s32[64]{0:T(128)} %param.18) | copy-start | bytes 772
  7.2 113.6 %all-gather.2.cloned.1.call-start = ((), (), s32[]{:S(2)}) async-start(), calls=%async_computation.3 | async-start | bytes 6684672 | tf_op jit(solution)/shard_map/weights/all_gather | solution.py:161
  9.2 10.3 %collective-permute-start.11 = (bf16[128,768]{1,0:T(8,128)(2,1)S(1)}, bf16[128,768]{1,0:T(8,128)(2,1)S(1)}, u32[]{:S(2)}, u32[]{:S(2)}) collective-permute-start(bf16[128,768]{1,0:T(8,128)(2,1)S(1)} %get-tuple-element.114), channel_id=1, source_target_pairs={{0,0},{1,128},{64,1},{65,129},{128,64},{129,192},{192,65},{193,193... | collective-permute-start | bytes 589832 | tf_op jit(solution)/shard_map/weights/ppermute | solution.py:34
  15.5 9.0 %collective-permute-start.12 = (bf16[128,768]{1,0:T(8,128)(2,1)S(1)}, bf16[128,768]{1,0:T(8,128)(2,1)S(1)}, u32[]{:S(2)}, u32[]{:S(2)}) collective-permute-start(bf16[128,768]{1,0:T(8,128)(2,1)S(1)} %get-tuple-element.115), channel_id=1, source_target_pairs={{0,64},{1,192},{64,65},{65,193},{128,0},{129,128},{192,1},{193,129... | collective-permute-start | bytes 589832 | tf_op jit(solution)/shard_map/weights/ppermute | solution.py:34
  25.3 26.9 %collective-permute-start = (bf16[256,2048]{1,0:T(8,128)(2,1)S(1)}, bf16[256,2048]{1,0:T(8,128)(2,1)S(1)}, u32[]{:S(2)}, u32[]{:S(2)}) collective-permute-start(bf16[256,2048]{1,0:T(8,128)(2,1)S(1)} %copy-done.3), channel_id=1, source_target_pairs={{0,194},{64,0},{128,64},{192,128},{2,192},{66,2},{130,66},{194,130... | collective-permute-start | bytes 3145736 | tf_op jit(solution)/shard_map/direction/ppermute | solution.py:40
  29.7 26.1 %collective-permute-start.2 = (bf16[256,2048]{1,0:T(8,128)(2,1)S(1)}, bf16[256,2048]{1,0:T(8,128)(2,1)}, u32[]{:S(2)}, u32[]{:S(2)}) collective-permute-start(bf16[256,2048]{1,0:T(8,128)(2,1)S(1)} %copy-done.3), channel_id=1, source_target_pairs={{0,64},{64,128},{128,192},{192,2},{2,66},{66,130},{130,194},{194,0... | collective-permute-start | bytes 3145736 | tf_op jit(solution)/shard_map/direction/ppermute | solution.py:40
  34.1 28.4 %all-to-all-start = ((bf16[64,17,128]{2,1,0:T(8,128)(2,1)}), bf16[64,17,128]{2,1,0:T(8,128)(2,1)S(1)}, u32[]{:S(2)}, u32[]{:S(2)}) async-start(bf16[64,17,128]{2,1,0:T(8,128)(2,1)} %pad_maximum_fusion.1), calls=%async_computation | async-start | bytes 786432 | tf_op jit(solution)/shard_map/direction/all_to_all | solution.py:174
  52.2 26.4 %collective-permute-start.1 = (bf16[256,2048]{1,0:T(8,128)(2,1)S(1)}, bf16[256,2048]{1,0:T(8,128)(2,1)}, u32[]{:S(2)}, u32[]{:S(2)}) collective-permute-start(bf16[256,2048]{1,0:T(8,128)(2,1)S(1)} %collective-permute-done), channel_id=1, source_target_pairs={{0,194},{64,0},{128,64},{192,128},{2,192},{66,2},{130,66},{194,130... | collective-permute-start | bytes 3145736 | tf_op jit(solution)/shard_map/direction/ppermute | solution.py:40
  55.7 25.4 %collective-permute-start.3 = (bf16[256,2048]{1,0:T(8,128)(2,1)}, bf16[256,2048]{1,0:T(8,128)(2,1)}, u32[]{:S(2)}, u32[]{:S(2)}) collective-permute-start(bf16[256,2048]{1,0:T(8,128)(2,1)} %collective-permute-done.2), channel_id=1, source_target_pairs={{0,64},{64,128},{128,192},{192,2},{2,66},{66,130},{130,194},{194,0... | collective-permute-start | bytes 3145736 | tf_op jit(solution)/shard_map/direction/ppermute | solution.py:40
  81.1 33.3 %collective-permute-start.8 = (bf16[256,2048]{1,0:T(8,128)(2,1)}, bf16[256,2048]{1,0:T(8,128)(2,1)S(1)}, u32[]{:S(2)}, u32[]{:S(2)}) collective-permute-start(bf16[256,2048]{1,0:T(8,128)(2,1)} %collective-permute-done.1), channel_id=1, source_target_pairs={{0,194},{64,0},{128,64},{192,128},{2,192},{66,2},{130,66},{194,130... | collective-permute-start | bytes 3145736 | tf_op jit(solution)/shard_map/direction/ppermute | solution.py:40
  81.5 32.9 %collective-permute-start.9 = (bf16[256,2048]{1,0:T(8,128)(2,1)}, bf16[256,2048]{1,0:T(8,128)(2,1)S(1)}, u32[]{:S(2)}, u32[]{:S(2)}) collective-permute-start(bf16[256,2048]{1,0:T(8,128)(2,1)} %collective-permute-done.3), channel_id=1, source_target_pairs={{0,64},{64,128},{128,192},{192,2},{2,66},{66,130},{130,194},{194,0... | collective-permute-start | bytes 3145736 | tf_op jit(solution)/shard_map/direction/ppermute | solution.py:40
  83.4 25.9 %collective-permute-start.7 = (f32[2,16,128]{2,1,0:T(8,128)S(1)}, f32[2,16,128]{2,1,0:T(8,128)S(1)}, u32[]{:S(2)}, u32[]{:S(2)}) collective-permute-start(f32[2,16,128]{2,1,0:T(8,128)S(1)} %pad_maximum_fusion.13), channel_id=1, source_target_pairs={{0,3},{1,67},{2,131},{3,195},{64,0},{65,64},{66,128},{67,192},{128... | collective-permute-start | bytes 49160 | tf_op jit(solution)/shard_map/direction/ppermute | solution.py:47
  85.8 28.3 %collective-permute-start.6 = (f32[2,16,128]{2,1,0:T(8,128)S(1)}, f32[2,16,128]{2,1,0:T(8,128)S(1)}, u32[]{:S(2)}, u32[]{:S(2)}) collective-permute-start(f32[2,16,128]{2,1,0:T(8,128)S(1)} %pad_maximum_fusion.13), channel_id=1, source_target_pairs={{0,2},{1,66},{2,130},{3,194},{64,3},{65,67},{66,131},{67,195},{128... | collective-permute-start | bytes 49160 | tf_op jit(solution)/shard_map/direction/ppermute | solution.py:47
  89.3 24.8 %collective-permute-start.5 = (f32[2,16,128]{2,1,0:T(8,128)S(1)}, f32[2,16,128]{2,1,0:T(8,128)S(1)}, u32[]{:S(2)}, u32[]{:S(2)}) collective-permute-start(f32[2,16,128]{2,1,0:T(8,128)S(1)} %pad_maximum_fusion.13), channel_id=1, source_target_pairs={{0,1},{1,65},{2,129},{3,193},{64,2},{65,66},{66,130},{67,194},{128... | collective-permute-start | bytes 49160 | tf_op jit(solution)/shard_map/direction/ppermute | solution.py:47
  109.4 5.0 %collective-permute-start.4 = (f32[2,16,128]{2,1,0:T(8,128)S(1)}, f32[2,16,128]{2,1,0:T(8,128)S(1)}, u32[]{:S(2)}, u32[]{:S(2)}) collective-permute-start(f32[2,16,128]{2,1,0:T(8,128)S(1)} %pad_maximum_fusion.13), channel_id=1, source_target_pairs={{0,0},{1,64},{2,128},{3,192},{64,1},{65,65},{66,129},{67,193},{128... | collective-permute-start | bytes 49160 | tf_op jit(solution)/shard_map/direction/ppermute | solution.py:47
  115.6 18.9 %collective-permute-start.10 = (bf16[256,2048]{1,0:T(8,128)(2,1)}, bf16[256,2048]{1,0:T(8,128)(2,1)}, u32[]{:S(2)}, u32[]{:S(2)}) collective-permute-start(bf16[256,2048]{1,0:T(8,128)(2,1)} %broadcast_select_fusion), channel_id=1, source_target_pairs={{0,64},{1,195},{64,128},{65,1},{128,192},{129,65},{192,2},{193,129... | collective-permute-start | bytes 3145736 | tf_op jit(solution)/shard_map/direction/ppermute | solution.py:123
  117.8 2.9 %collective-permute-start.14 = (f32[256,1]{1,0:T(8,128)S(1)}, f32[256,1]{1,0:T(8,128)S(1)}, u32[]{:S(2)}, u32[]{:S(2)}) collective-permute-start(f32[256,1]{1,0:T(8,128)S(1)} %broadcast_select_fusion.11), channel_id=1, source_target_pairs={{0,1},{1,0},{2,3},{3,2},{4,5},{5,4},{6,7},{7,6},{8,9},{9,8},{10,11... | collective-permute-start | bytes 3080 | tf_op jit(solution)/shard_map/project/ppermute | solution.py:60
  129.5 3.7 %collective-permute-start.13 = (f32[256,768]{1,0:T(8,128)S(1)}, f32[256,768]{1,0:T(8,128)S(1)}, u32[]{:S(2)}, u32[]{:S(2)}) collective-permute-start(f32[256,768]{1,0:T(8,128)S(1)} %get-tuple-element.80), channel_id=1, source_target_pairs={{0,1},{1,0},{2,3},{3,2},{4,5},{5,4},{6,7},{7,6},{8,9},{9,8},{10,11... | collective-permute-start | bytes 2359304 | tf_op jit(solution)/shard_map/project/ppermute | solution.py:60
  138.1 2.5 %collective-permute-start.15 = (f32[256,768]{1,0:T(8,128)}, f32[256,768]{1,0:T(8,128)S(1)}, u32[]{:S(2)}, u32[]{:S(2)}) collective-permute-start(f32[256,768]{1,0:T(8,128)} %get-tuple-element.78), channel_id=1, source_target_pairs={{0,1},{1,0},{2,3},{3,2},{4,5},{5,4},{6,7},{7,6},{8,9},{9,8},{10,11... | collective-permute-start | bytes 2359304 | tf_op jit(solution)/shard_map/project/ppermute | solution.py:60
  138.6 2.0 collective-permute-start.16
  142.0 12.6 %collective-permute-start.20 = (bf16[4,512]{1,0:T(4,128)(2,1)S(1)}, bf16[4,512]{1,0:T(4,128)(2,1)S(1)}, u32[]{:S(2)}, u32[]{:S(2)}) collective-permute-start(bf16[4,512]{1,0:T(4,128)(2,1)S(1)} %pad_maximum_fusion.16), channel_id=1, source_target_pairs={{0,192},{1,0},{64,64},{65,128},{128,193},{129,1},{192,65},{193,129... | collective-permute-start | bytes 12296 | tf_op jit(solution)/shard_map/tail/ppermute | solution.py:34
  144.1 10.5 %collective-permute-start.19 = (bf16[4,512]{1,0:T(4,128)(2,1)S(1)}, bf16[4,512]{1,0:T(4,128)(2,1)S(1)}, u32[]{:S(2)}, u32[]{:S(2)}) collective-permute-start(bf16[4,512]{1,0:T(4,128)(2,1)S(1)} %pad_maximum_fusion.16), channel_id=1, source_target_pairs={{0,128},{1,192},{64,0},{65,64},{128,129},{129,193},{192,1},{193,65... | collective-permute-start | bytes 12296 | tf_op jit(solution)/shard_map/tail/ppermute | solution.py:34
  149.1 6.1 %collective-permute-start.18 = (bf16[4,512]{1,0:T(4,128)(2,1)S(1)}, bf16[4,512]{1,0:T(4,128)(2,1)S(1)}, u32[]{:S(2)}, u32[]{:S(2)}) collective-permute-start(bf16[4,512]{1,0:T(4,128)(2,1)S(1)} %pad_maximum_fusion.16), channel_id=1, source_target_pairs={{0,64},{1,128},{64,192},{65,0},{128,65},{129,129},{192,193},{193,1... | collective-permute-start | bytes 12296 | tf_op jit(solution)/shard_map/tail/ppermute | solution.py:34
  151.0 5.9 %collective-permute-start.17 = (bf16[4,512]{1,0:T(4,128)(2,1)S(1)}, bf16[4,512]{1,0:T(4,128)(2,1)S(1)}, u32[]{:S(2)}, u32[]{:S(2)}) collective-permute-start(bf16[4,512]{1,0:T(4,128)(2,1)S(1)} %pad_maximum_fusion.16), channel_id=1, source_target_pairs={{0,0},{1,64},{64,128},{65,192},{128,1},{129,65},{192,129},{193,193... | collective-permute-start | bytes 12296 | tf_op jit(solution)/shard_map/tail/ppermute | solution.py:34
  154.5 12.5 %collective-permute-start.22 = (bf16[256,512]{1,0:T(8,128)(2,1)S(1)}, bf16[256,512]{1,0:T(8,128)(2,1)S(1)}, u32[]{:S(2)}, u32[]{:S(2)}) collective-permute-start(bf16[256,512]{1,0:T(8,128)(2,1)S(1)} %get-tuple-element.66), channel_id=1, source_target_pairs={{0,64},{1,192},{64,128},{65,0},{128,193},{129,65},{192,1},{193,129... | collective-permute-start | bytes 786440 | tf_op jit(solution)/shard_map/tail/ppermute | solution.py:34
  157.0 12.5 %collective-permute-start.21 = (bf16[256,512]{1,0:T(8,128)(2,1)S(1)}, bf16[256,512]{1,0:T(8,128)(2,1)S(1)}, u32[]{:S(2)}, u32[]{:S(2)}) collective-permute-start(bf16[256,512]{1,0:T(8,128)(2,1)S(1)} %get-tuple-element.70), channel_id=1, source_target_pairs={{0,0},{1,128},{64,64},{65,192},{128,129},{129,1},{192,193},{193,65... | collective-permute-start | bytes 786440 | tf_op jit(solution)/shard_map/tail/ppermute | solution.py:34
  160.3 14.3 %all-to-all-start.1 = ((bf16[16,4,4,512]{3,2,1,0:T(4,128)(2,1)}), bf16[16,4,4,512]{3,2,1,0:T(4,128)(2,1)S(1)}, u32[]{:S(2)}, u32[]{:S(2)}) async-start(bf16[16,4,4,512]{3,2,1,0:T(4,128)(2,1)} %broadcast_in_dim.107), calls=%async_computation.1 | async-start | bytes 524288 | tf_op jit(solution)/shard_map/tail/all_to_all | solution.py:23
  175.0 7.2 %collective-permute-start.25 = (bf16[64,128]{1,0:T(8,128)(2,1)S(1)}, bf16[64,128]{1,0:T(8,128)(2,1)S(1)}, u32[]{:S(2)}, u32[]{:S(2)}) collective-permute-start(bf16[64,128]{1,0:T(8,128)(2,1)S(1)} %convolution_convert_fusion.1), channel_id=1, source_target_pairs={{0,3},{1,2},{2,1},{3,0},{4,7},{5,6},{6,5},{7,4},{8,11},{9,10},{10,... | collective-permute-start | bytes 49160 | tf_op jit(solution)/shard_map/tail/ppermute | solution.py:54
  175.3 6.9 %collective-permute-start.24 = (bf16[64,128]{1,0:T(8,128)(2,1)S(1)}, bf16[64,128]{1,0:T(8,128)(2,1)S(1)}, u32[]{:S(2)}, u32[]{:S(2)}) collective-permute-start(bf16[64,128]{1,0:T(8,128)(2,1)S(1)} %convolution_convert_fusion.1), channel_id=1, source_target_pairs={{0,2},{1,3},{2,0},{3,1},{4,6},{5,7},{6,4},{7,5},{8,10},{9,11},{10,... | collective-permute-start | bytes 49160 | tf_op jit(solution)/shard_map/tail/ppermute | solution.py:54
  178.1 4.1 %collective-permute-start.23 = (bf16[64,128]{1,0:T(8,128)(2,1)S(1)}, bf16[64,128]{1,0:T(8,128)(2,1)S(1)}, u32[]{:S(2)}, u32[]{:S(2)}) collective-permute-start(bf16[64,128]{1,0:T(8,128)(2,1)S(1)} %convolution_convert_fusion.1), channel_id=1, source_target_pairs={{0,1},{1,0},{2,3},{3,2},{4,5},{5,4},{6,7},{7,6},{8,9},{9,8},{10,11... | collective-permute-start | bytes 49160 | tf_op jit(solution)/shard_map/tail/ppermute | solution.py:54
  (9 other events, 50.0 us)
Sparse Core Ops, SparseCore 0:
  25.4 70.3 all-gather.1
